TPU v7x, 128 devices: a whole 4x4x4 slice. The times are simulated.
128 devices in a mesh: seq: 32 (over y, z_lo, x), batch: 4 (over z_hi, core).
Axes of the slice: x: 4, y: 4, z: 4 (z_hi: 2, z_lo: 2; z = z_hi * 2 + z_lo), core: 2. Of those that a mesh axis runs over, the one named last changes fastest.
Arguments:
- tokens: bfloat16 [4, 8192, 768], P('batch', 'seq'), may hold values from -6 to 6
- token_pos: int32 [4, 8192], P('batch', 'seq'), may hold values from 0 to 4095, as said below
- token_pass: int32 [4, 8192], P('batch', 'seq'), may hold values from 0 to 4, as said below
- token_count: int32 [4, 8192], P('batch', 'seq'), may hold values from 2 to 5, as said below
- w_qkv: bfloat16 [768, 2304], replicated, may hold values from -0.21875 to 0.21875
- w_out: bfloat16 [768, 768], replicated, may hold values from -0.875 to 0.875
- w_up: bfloat16 [768, 3072], replicated, may hold values from -0.21875 to 0.21875
- w_down: bfloat16 [3072, 768], replicated, may hold values from -0.109375 to 0.109375
- gain_attn: float32 [768], replicated, may hold values from 0.5 to 1.5
- gain_mlp: float32 [768], replicated, may hold values from 0.5 to 1.5
- pass_table: float32 [5, 768], replicated, may hold values from -3 to 3
- cotangent: bfloat16 [4, 8192, 768], P('batch', 'seq'), may hold values from -6 to 6
Outputs:
- mixed: bfloat16 [4, 8192, 768], P('batch', 'seq')
- grad_tokens: float32 [4, 8192, 768], P('batch', 'seq')
- grad_qkv: float32 [768, 2304], replicated
- grad_out: float32 [768, 768], replicated
- grad_up: float32 [768, 3072], replicated
- grad_down: float32 [3072, 768], replicated
- grad_gain_attn: float32 [768], replicated
- grad_gain_mlp: float32 [768], replicated
- grad_pass_table: float32 [5, 768], replicated
Inputs may be any that keep to these rules, and one draw needn't show every extreme that they name: `token_pos`: A stream holds three documents end to end; the middle one begins on the first 256 tokens and ends in the last 256. Inside a document of c passes, the token at position p and pass r stands p * c + r places after its first token; only a document's last position may hold fewer than c passes. `token_pass`: the pass number of a token in its document. `token_count`: equal for all tokens of one document; every stream has a document of 2 and one of 5 passes.
All inputs are finite; a program needn't handle non-finite values.
Results may differ from a plain program's by a relative error of at most 0.018.
Values may be sent and summed in bfloat16 or wider, within the bound.
No kernel may reach another device: no remote copies, remote signals or barrier semaphores. Data moves between devices by JAX's collectives and lax.ppermute only.
A program may use at most 320 MiB of HBM per device.

v0:
```python
import math

import jax
import jax.numpy as jnp
from jax import lax
from jax.sharding import PartitionSpec as P

HEADS = 12
HEAD_DIM = 64
PASSES = 5


def sent_together(arrays, axis, dim, along):
    ends, at = ([], 0)
    for a in arrays[:-1]:
        at += a.shape[along]
        ends.append(at)
    both = jnp.concatenate(arrays, axis=along)
    return tuple(jnp.split(lax.all_gather(both, axis, axis=dim, tiled=True), ends, axis=along))


def norm_rows(values, gain):
    row_mean = jnp.mean(values, axis=-1, keepdims=True)
    centered = values - row_mean
    variance = jnp.mean(centered * centered, axis=-1, keepdims=True)
    return centered * lax.rsqrt(variance + 1e-05) * gain


def heads_of(values):
    return values.reshape(values.shape[0], HEADS, HEAD_DIM)


def contract_rows(left, right):
    return lax.dot_general(
        left, right, (((0,), (0,)), ((), ())), preferred_element_type=jnp.float32
    )


def times_transposed(left, right):
    return lax.dot_general(
        left, right, (((1,), (1,)), ((), ())), preferred_element_type=jnp.float32
    )


def attend_keys(carried, pieces, start, queries, first_key, rows_at, lowest, highest):
    keys_all, values_all = pieces
    key_count = keys_all.shape[0]
    block_rows = math.gcd(key_count, 512)
    scale = HEAD_DIM ** (-0.5)

    def compute(state, key_rows, value_rows, block_start):
        row_top, row_total, summed = state
        keys_at = block_start + jnp.arange(block_rows, dtype=jnp.int32)
        scores = (
            jnp.einsum(
                "qhe,khe->hqk", queries, heads_of(key_rows), preferred_element_type=jnp.float32
            )
            * scale
        )
        allowed = (keys_at[None, :] >= first_key[:, None]) & (keys_at[None, :] <= rows_at[:, None])
        masked = jnp.where(allowed[None], scores, -1e30)
        new_top = jnp.maximum(row_top, jnp.max(masked, axis=-1))
        weights = jnp.where(allowed[None], jnp.exp(masked - new_top[..., None]), 0.0)
        shrink = jnp.exp(row_top - new_top)
        row_total = row_total * shrink + jnp.sum(weights, axis=-1)
        summed = summed * shrink[..., None] + jnp.einsum(
            "hqk,khe->hqe",
            weights.astype(jnp.bfloat16),
            heads_of(value_rows),
            preferred_element_type=jnp.float32,
        )
        return (new_top, row_total, summed)

    def one_step(block_index, state):
        block_start = start + block_index * block_rows
        key_rows = lax.dynamic_slice_in_dim(keys_all, block_index * block_rows, block_rows, 0)
        value_rows = lax.dynamic_slice_in_dim(values_all, block_index * block_rows, block_rows, 0)
        visible = (block_start <= highest) & (block_start + block_rows - 1 >= lowest)
        return lax.cond(
            visible,
            lambda inner: compute(inner, key_rows, value_rows, block_start),
            lambda inner: inner,
            state,
        )

    return lax.fori_loop(0, key_count // block_rows, one_step, carried)


def attend_back(
    keys_all, values_all, queries, grad_att, delta, lse, first_key, rows_at, lowest, highest
):
    key_count = keys_all.shape[0]
    row_count = queries.shape[0]
    width = keys_all.shape[1]
    block_rows = math.gcd(key_count, 512)
    scale = HEAD_DIM ** (-0.5)
    grad_heads = heads_of(grad_att)

    def compute(state, block_start):
        grad_query, key_grads = state
        key_rows = heads_of(lax.dynamic_slice_in_dim(keys_all, block_start, block_rows, 0))
        value_rows = heads_of(lax.dynamic_slice_in_dim(values_all, block_start, block_rows, 0))
        keys_at = block_start + jnp.arange(block_rows, dtype=jnp.int32)
        scores = (
            jnp.einsum("qhe,khe->hqk", queries, key_rows, preferred_element_type=jnp.float32)
            * scale
        )
        allowed = (keys_at[None, :] >= first_key[:, None]) & (keys_at[None, :] <= rows_at[:, None])
        masked = jnp.where(allowed[None], scores, -1e30)
        probs = jnp.where(allowed[None], jnp.exp(masked - lse[..., None]), 0.0)
        grad_probs = jnp.einsum(
            "qhe,khe->hqk", grad_heads, value_rows, preferred_element_type=jnp.float32
        )
        grad_scores = (scale * probs * (grad_probs - delta[..., None])).astype(jnp.bfloat16)
        grad_query = grad_query + jnp.einsum(
            "hqk,khe->qhe", grad_scores, key_rows, preferred_element_type=jnp.float32
        )
        grad_keys = jnp.einsum(
            "hqk,qhe->khe", grad_scores, queries, preferred_element_type=jnp.float32
        )
        grad_values = jnp.einsum(
            "hqk,qhe->khe",
            probs.astype(jnp.bfloat16),
            grad_heads,
            preferred_element_type=jnp.float32,
        )
        joined = jnp.concatenate(
            [grad_keys.reshape(block_rows, width), grad_values.reshape(block_rows, width)], axis=1
        )
        key_grads = lax.dynamic_update_slice_in_dim(key_grads, joined, block_start, 0)
        return (grad_query, key_grads)

    def one_step(block_index, state):
        block_start = block_index * block_rows
        visible = (block_start <= highest) & (block_start + block_rows - 1 >= lowest)
        return lax.cond(
            visible, lambda inner: compute(inner, block_start), lambda inner: inner, state
        )

    holder = jnp.zeros((key_count, 2 * width), jnp.float32)
    start_state = (jnp.zeros((row_count, HEADS, HEAD_DIM), jnp.float32), holder)
    return lax.fori_loop(0, key_count // block_rows, one_step, start_state)


def on_device(
    tokens,
    token_pos,
    token_pass,
    token_count,
    w_qkv,
    w_out,
    w_up,
    w_down,
    gain_attn,
    gain_mlp,
    pass_table,
    cotangent,
):
    row_count = tokens.shape[1]
    width = tokens.shape[2]
    first_row = lax.axis_index("seq") * row_count
    rows_at = first_row + jnp.arange(row_count, dtype=jnp.int32)
    first_key = rows_at - (token_pos[0] * token_count[0] + token_pass[0])
    lowest = jnp.min(first_key)
    highest = first_row + row_count - 1

    def block_forward(stream_in):
        normed = norm_rows(stream_in, gain_attn).astype(jnp.bfloat16)
        projected = jnp.dot(normed, w_qkv, preferred_element_type=jnp.float32)
        queries = projected[:, :width].astype(jnp.bfloat16)
        keys_local = projected[:, width : 2 * width].astype(jnp.bfloat16)
        values_local = projected[:, 2 * width :].astype(jnp.bfloat16)
        query_heads = heads_of(queries)
        start_state = (
            jnp.full((HEADS, row_count), -1e30, jnp.float32),
            jnp.zeros((HEADS, row_count), jnp.float32),
            jnp.zeros((HEADS, row_count, HEAD_DIM), jnp.float32),
        )
        collected = sent_together((keys_local, values_local), "seq", 0, 1)
        state = attend_keys(
            start_state, collected, 0, query_heads, first_key, rows_at, lowest, highest
        )
        row_top, row_total, summed = state
        att_f = jnp.transpose(summed / row_total[..., None], (1, 0, 2)).reshape(row_count, width)
        lse = row_top + jnp.log(row_total)
        attended = att_f.astype(jnp.bfloat16)
        resid_mid = stream_in + jnp.dot(attended, w_out, preferred_element_type=jnp.float32)
        mid_normed = norm_rows(resid_mid, gain_mlp).astype(jnp.bfloat16)
        hidden = jnp.dot(mid_normed, w_up, preferred_element_type=jnp.float32)
        activated = jax.nn.gelu(hidden, approximate=True).astype(jnp.bfloat16)
        result = resid_mid + jnp.dot(activated, w_down, preferred_element_type=jnp.float32)
        saved = (
            stream_in,
            normed,
            queries,
            keys_local,
            values_local,
            collected,
            att_f,
            attended,
            lse,
            resid_mid,
            mid_normed,
            hidden,
            activated,
        )
        return (result, saved)

    def block_backward(grad_result, saved):
        (
            stream_in,
            normed,
            queries,
            keys_local,
            values_local,
            collected,
            att_f,
            attended,
            lse,
            resid_mid,
            mid_normed,
            hidden,
            activated,
        ) = saved
        query_heads = heads_of(queries)
        grad_z = grad_result.astype(jnp.bfloat16)
        grad_down_part = contract_rows(activated, grad_z)
        grad_act = times_transposed(grad_z, w_down)
        gelu_value, gelu_back = jax.vjp(
            lambda hidden_in: jax.nn.gelu(hidden_in, approximate=True), hidden
        )
        grad_hidden = gelu_back(grad_act)[0].astype(jnp.bfloat16)
        grad_up_part = contract_rows(mid_normed, grad_hidden)
        grad_mid = times_transposed(grad_hidden, w_up)
        norm_value, norm_back = jax.vjp(norm_rows, resid_mid, gain_mlp)
        grad_resid, grad_gain_two = norm_back(grad_mid)
        grad_resid = grad_resid + grad_result
        grad_y = grad_resid.astype(jnp.bfloat16)
        grad_out_part = contract_rows(attended, grad_y)
        grad_att = times_transposed(grad_y, w_out).astype(jnp.bfloat16)
        delta = jnp.einsum("qhe,qhe->hq", heads_of(grad_att).astype(jnp.float32), heads_of(att_f))
        keys_all, values_all = collected
        grad_query, key_grads = attend_back(
            keys_all,
            values_all,
            query_heads,
            grad_att,
            delta,
            lse,
            first_key,
            rows_at,
            lowest,
            highest,
        )
        own_grads = lax.psum_scatter(
            key_grads.astype(jnp.bfloat16), "seq", scatter_dimension=0, tiled=True
        )
        grad_projected = jnp.concatenate(
            [grad_query.reshape(row_count, width).astype(jnp.bfloat16), own_grads], axis=1
        )
        grad_qkv_part = contract_rows(normed, grad_projected)
        grad_normed = times_transposed(grad_projected, w_qkv)
        first_value, first_back = jax.vjp(norm_rows, stream_in, gain_attn)
        grad_in, grad_gain_one = first_back(grad_normed)
        grad_in = grad_in + grad_resid
        return (
            grad_in,
            (
                grad_qkv_part,
                grad_out_part,
                grad_up_part,
                grad_down_part,
                grad_gain_one,
                grad_gain_two,
            ),
        )

    first_out, saved_first = block_forward(tokens[0].astype(jnp.float32))
    pass_onehot = (token_pass[0][:, None] == jnp.arange(PASSES, dtype=jnp.int32)[None, :]).astype(
        jnp.float32
    )
    second_in = first_out + jnp.dot(pass_onehot, pass_table)
    second_out, saved_second = block_forward(second_in)
    grad_second, parts_second = block_backward(cotangent[0].astype(jnp.float32), saved_second)
    table_part = lax.dot_general(pass_onehot, grad_second, (((0,), (0,)), ((), ())))
    grad_first, parts_first = block_backward(grad_second, saved_first)
    summed_parts = tuple((parts_first[place] + parts_second[place] for place in range(6)))
    totals = lax.psum(
        (
            summed_parts[0],
            summed_parts[1],
            summed_parts[2],
            summed_parts[3],
            summed_parts[4],
            summed_parts[5],
            table_part,
        ),
        ("seq", "batch"),
    )
    return (
        second_out.astype(jnp.bfloat16)[None],
        grad_first[None],
        totals[0],
        totals[1],
        totals[2],
        totals[3],
        totals[4],
        totals[5],
        totals[6],
    )


def solution(mesh):
    return jax.shard_map(
        on_device,
        mesh=mesh,
        in_specs=(
            P("batch", "seq", None),
            P("batch", "seq"),
            P("batch", "seq"),
            P("batch", "seq"),
            P(),
            P(),
            P(),
            P(),
            P(),
            P(),
            P(),
            P("batch", "seq", None),
        ),
        out_specs=(
            P("batch", "seq", None),
            P("batch", "seq", None),
            P(),
            P(),
            P(),
            P(),
            P(),
            P(),
            P(),
        ),
        check_vma=False,
    )
```

profile of v0, /device:TPU:1, one launch (start us, length us, event | category | flops | bytes accessed | tf_op | source)
XLA Modules:
  0.0 2278.5 jit_solution(10359963262208317924)
XLA Ops:
  20.1 276.0 %all-gather.3.cloned.1.call-done = bf16[8192,1536]{1,0:T(8,128)(2,1)} async-done(((bf16[256,1536]{1,0:T(8,128)(2,1)}), bf16[8192,1536]{1,0:T(8,128)(2,1)}) %all-gather.3.cloned.1.call-update) | async-done | bytes 25165840 | tf_op jit(solution)/shard_map/all_gather | solution.py:19
  296.1 17.1 fusion.125
  313.2 16.8 copy.52
  330.0 16.7 copy.53
  348.3 28.1 %while.84 = (s32[]{:T(128)}, f32[12,256]{1,0:T(8,128)S(1)}, f32[12,256]{1,0:T(8,128)}, f32[12,256,64]{1,2,0:T(8,128)}, s32[]{:T(128)}, /*index=5*/s32[]{:T(128)}...) while((s32[]{:T(128)}, f32[12,256]{1,0:T(8,128)S(1)}, ...), condition=%wide.region_8.9_spmd.clone, body=%wide.region_3.8_spmd.clone.sunk | while | flops 423893760 | bytes 34776608 | solution.py:86
  349.5 9.2 conditional.12
  393.6 408.1 %all-gather.5.cloned.1.call-done = bf16[8192,1536]{1,0:T(8,128)(2,1)} async-done(((bf16[256,1536]{1,0:T(8,128)(2,1)}), bf16[8192,1536]{1,0:T(8,128)(2,1)}) %all-gather.5.cloned.1.call-update) | async-done | bytes 25165840 | tf_op jit(solution)/shard_map/all_gather | solution.py:19
  801.7 17.2 fusion.124
  818.8 16.0 copy.55
  834.9 15.7 copy.56
  852.2 28.4 %while.85 = (s32[]{:T(128)}, f32[12,256]{1,0:T(8,128)S(1)}, f32[12,256]{1,0:T(8,128)}, f32[12,256,64]{1,2,0:T(8,128)}, s32[]{:T(128)}, /*index=5*/s32[]{:T(128)}...) while((s32[]{:T(128)}, f32[12,256]{1,0:T(8,128)S(1)}, ...), condition=%wide.region_18.19_spmd.clone, body=%wide.region_13.18_spmd.clone.sunk | while | flops 423893760 | bytes 34776608 | solution.py:86
  853.3 9.2 conditional.13
  884.3 4.0 fusion.119
  889.0 5.5 fusion.69
  905.1 8.6 broadcast.409.clone
  913.7 22.3 while.86
  914.8 11.3 conditional.14
  940.0 576.8 %reduce-scatter.3.cloned.1.call-done = bf16[256,1536]{0,1:T(8,128)(2,1)} async-done(((bf16[8192,1536]{0,1:T(8,128)(2,1)}), bf16[256,1536]{0,1:T(8,128)(2,1)}) %reduce-scatter.3.cloned.1.call-update) | async-done | bytes 786448 | tf_op jit(solution)/shard_map/reduce_scatter | solution.py:255
  1516.9 3.5 multiply_reduce_fusion.2
  1535.4 8.6 broadcast.409
  1544.0 21.9 while.87
  1544.6 11.3 conditional.15
  1576.5 5.3 convolution_add_fusion.2
  1581.8 6.1 convolution_add_fusion.1
  1587.9 420.4 %reduce-scatter.5.cloned.1.call-done = bf16[256,1536]{0,1:T(8,128)(2,1)} async-done(((bf16[8192,1536]{0,1:T(8,128)(2,1)}), bf16[256,1536]{0,1:T(8,128)(2,1)}) %reduce-scatter.5.cloned.1.call-update) | async-done | bytes 786448 | tf_op jit(solution)/shard_map/reduce_scatter | solution.py:255
  2011.1 4.3 convolution_add_fusion
  2015.5 6.5 fusion.71
  2026.0 64.2 %all-reduce = (f32[768]{0:T(1024)}, f32[768]{0:T(1024)}, f32[5,768]{1,0:T(8,128)}) all-reduce(f32[768]{0:T(1024)} %add.458, f32[768]{0:T(1024)S(1)} %add.459, f32[5,768]{1,0:T(8,128)} %fusion.103), channel_id=1, replica_groups=mesh['seq'=32,'batch'=4] {'seq','batch'}, use_global_device_ids=true, to_apply=%region_45.46 | all-reduce | flops 5376 | bytes 43008 | tf_op jit(solution)/shard_map/psum | solution.py:288
  2093.5 157.1 %all-reduce.4.cloned.1.call-done = (f32[768,2304]{1,0:T(8,128)}, f32[768,768]{1,0:T(8,128)}, f32[768,3072]{1,0:T(8,128)}, f32[3072,768]{1,0:T(8,128)}) async-done(((f32[768,2304]{1,0:T(8,128)}, f32[768,768]{1,0:T(8,128)}, f32[768,3072]{1,0:T(8,128)}, f32[3072,768]{1,0:T(8,128)}), (f32[768,2304]{1,0:T(8,128)}, f32[768,768]{1,0:T(8,128)}, f32[768,3072]{1,0:T(8,128)}, ...) | async-done | bytes 28311568 | tf_op jit(solution)/shard_map/psum | solution.py:288
  2250.5 6.6 copy.159
  2258.5 9.3 copy.161
  2267.8 3.7 copy.162
  (515 shorter events, 147.3 us)
Async XLA Ops:
  7.2 288.9 %all-gather.3.cloned.1.call-start = ((), (), s32[]{:S(2)}) async-start(), calls=%async_computation.2 | async-start | bytes 25952256 | tf_op jit(solution)/shard_map/all_gather | solution.py:19
  15.1 786.6 %all-gather.5.cloned.1.call-start = ((), (), s32[]{:S(2)}) async-start(), calls=%async_computation.3 | async-start | bytes 25952256 | tf_op jit(solution)/shard_map/all_gather | solution.py:19
  376.4 6.7 copy-start.46
  389.6 1127.2 %reduce-scatter.3.cloned.1.call-start = ((), (), s32[]{:S(2)}) async-start(), calls=%async_computation.4 | async-start | bytes 25952256 | tf_op jit(solution)/shard_map/reduce_scatter | solution.py:255
  884.0 12.7 copy-start.16
  884.0 12.7 copy-start.79
  884.3 12.5 copy-start.92
  884.3 10.2 slice-start.3
  888.3 6.2 copy-start.26
  889.0 5.5 slice-start.4
  896.8 5.4 copy-start.63
  905.1 8.6 copy-start.68
  936.1 1072.2 %reduce-scatter.5.cloned.1.call-start = ((), (), s32[]{:S(2)}) async-start(), calls=%async_computation.5 | async-start | bytes 25952256 | tf_op jit(solution)/shard_map/reduce_scatter | solution.py:255
  1522.3 5.9 copy-start.19
  1535.4 8.6 copy-start.69
  1565.9 684.6 %all-reduce.4.cloned.1.call-start = ((), (), s32[]{:S(2)}) async-start(), calls=%async_computation.6 | async-start | bytes 56623104 | tf_op jit(solution)/shard_map/psum | solution.py:288
  1576.5 5.4 copy-start.27
  1576.5 5.3 copy-start.44
  1581.8 426.4 %copy-start.76 = (f32[768]{0:T(1024)S(1)}, f32[768]{0:T(1024)}, u32[]{:S(2)}) copy-start(f32[768]{0:T(1024)} %param.36) | copy-start | bytes 9220
  1581.8 426.4 %copy-start.78 = (f32[256]{0:T(256)S(1)}, f32[256]{0:T(256)}, u32[]{:S(2)}) copy-start(f32[256]{0:T(256)} %copy-done.77) | copy-start | bytes 3076
  1581.8 426.4 %copy-start.82 = (f32[256]{0:T(256)S(1)}, f32[256]{0:T(256)}, u32[]{:S(2)}) copy-start(f32[256]{0:T(256)} %copy-done.81) | copy-start | bytes 3076
  2015.4 6.6 copy-start.114
  2015.5 6.6 copy-start.116
  2015.5 6.6 copy-start.21
  2015.5 6.6 copy-start.105
  2015.5 7.5 copy-start.18
  2015.5 7.5 copy-start.56
  2015.5 7.5 copy-start.67
  2250.5 6.6 copy-start.48
  2257.1 10.7 slice-start
  2258.5 9.3 slice-start.1
  2258.5 9.3 slice-start.2
  (103 other events, 242.4 us)
Sparse Core Ops, SparseCore 0:
  15.2 280.8 all-gather.2
  389.8 411.8 all-gather.4
  936.2 580.5 reduce-scatter.2
  1566.1 442.1 reduce-scatter.4
  2015.6 234.9 all-reduce.3
where the time goes:
time: 2290 us; the launch traced here: 2280 us
  waiting for transfers between devices  1840 us (80%)
  local copies, waits for them, and re-layouts  194 us (8%)
  matrix products  89.7 us (4%)
  blocking collectives  64.2 us (3%)
  loops' own time  42.2 us (2%)
  other arithmetic  33.8 us (1%)
    reduce_scatter x2, waiting for transfers between devices, block_backward(): lax.psum_scatter(key_grads.astype(jnp.bfloat16), 'seq', scatter_dimension...  997 us
    all_gather x2, waiting for transfers between devices, sent_together(): lax.all_gather(both, axis, axis=dim, tiled=True)  684 us
    psum x1, waiting for transfers between devices, on_device(): lax.psum((summed_parts[0], summed_parts[1], summed_parts[2], summed_parts...  157 us
    unnamed x220, local copies, waits for them, and re-layouts  96.6 us
    psum x1, blocking collectives, on_device(): lax.psum((summed_parts[0], summed_parts[1], summed_parts[2], summed_parts...  64.2 us
  transfers between devices with their start and end apart: 5, of which 5 were waited for; matrix products, arithmetic and copies ran while one was open for 2% of the time, Pallas kernels for 0%

commit v1 on v0

v1 whole, which is shorter than its diff:
```python
import functools

import jax
import jax.numpy as jnp
from jax import lax
from jax.experimental import pallas as pl
from jax.experimental.pallas import tpu as pltpu
from jax.sharding import PartitionSpec as P

HEADS = 12
HEAD_DIM = 64
PASSES = 5
SEQ = 32
ROWS = 256
HALF = 128
SLOT = ROWS + 64 + 16
WIDTH = 768
FF = 3072
FF_BLOCK = 512
EPS = 1e-5
LOG2E = 1.4426950408889634
LOW = -1e30
F32 = jnp.float32
BF16 = jnp.bfloat16

WORK = [3 * (e // 4) + e % 4 if e % 4 < 3 else None for e in range(SEQ)]
SLOT_OF = {w: e for e, w in enumerate(WORK) if w is not None}


def dot(left, right):
    return jnp.dot(left, right, preferred_element_type=F32)


def contract_rows(left, right):
    return lax.dot_general(left, right, (((0,), (0,)), ((), ())), preferred_element_type=F32)


def times_transposed(left, right):
    return lax.dot_general(left, right, (((1,), (1,)), ((), ())), preferred_element_type=F32)


def standardise(values):
    centered = values - jnp.mean(values, axis=-1, keepdims=True)
    inverse = lax.rsqrt(jnp.mean(centered * centered, axis=-1, keepdims=True) + EPS)
    return centered * inverse, inverse


def standardise_back(grad, gain, values):
    normal, inverse = standardise(values)
    scaled = grad * gain
    along = jnp.mean(scaled * normal, axis=-1, keepdims=True)
    grad_values = inverse * (scaled - jnp.mean(scaled, axis=-1, keepdims=True) - normal * along)
    return grad_values, jnp.sum(grad * normal, axis=0, keepdims=True)


GELU_A = 0.7978845608028654
GELU_B = 0.044715


def gelu(value):
    return 0.5 * value * (1.0 + jnp.tanh(GELU_A * (value + GELU_B * value * value * value)))


def gelu_slope(value):
    square = value * value
    bent = jnp.tanh(GELU_A * value * (1.0 + GELU_B * square))
    inner = GELU_A * (1.0 + 3.0 * GELU_B * square)
    return 0.5 * (1.0 + bent) + 0.5 * value * (1.0 - bent * bent) * inner


def slot_of(head, block, odd):
    this, other = SLOT_OF[2 * head + block], SLOT_OF[2 * head + 1 - block]
    return jnp.where(odd == 1, other, this)


class Held:
    def __init__(self, source, target, sem):
        self.target = target
        self.copy = pltpu.make_async_copy(source, target, sem)
        self.copy.start()
        self.waited = False

    def ready(self):
        if not self.waited:
            self.copy.wait()
            self.waited = True
        return self.target

    def __getitem__(self, at):
        return self.ready()[at]


class Kept:
    def __init__(self, source, target, sem):
        self.source = source
        self.copy = pltpu.make_async_copy(source, target, sem)
        self.started = False

    def __getitem__(self, at):
        return self.source[at]

    def __setitem__(self, at, value):
        self.source[at] = value

    def flush(self):
        self.copy.start()
        self.started = True

    def finish(self):
        if not self.started:
            self.flush()
        self.copy.wait()


def project(stream, gain, w_qkv, odd, third, slots, normed_out):
    normed = (standardise(stream)[0] * gain).astype(BF16)
    normed_out[...] = normed
    low_lanes = lax.broadcasted_iota(jnp.int32, (ROWS, 128), 1) < 64
    for pair in range(HEADS // 2):
        at = 128 * pair
        queries = dot(normed, w_qkv[:, at : at + 128]) * HEAD_DIM**-0.5
        keys = dot(normed, w_qkv[:, WIDTH + at : WIDTH + at + 128])
        values = dot(normed, w_qkv[:, 2 * WIDTH + at : 2 * WIDTH + at + 128])
        queries_t = queries.T.astype(BF16)
        first = jnp.where(low_lanes, keys, pltpu.roll(values, 64, 1)).astype(BF16)
        second = jnp.where(low_lanes, pltpu.roll(keys, 64, 1), values).astype(BF16)
        for j, both in enumerate((first, second)):
            head = 2 * pair + j
            for block in range(2):
                to = slot_of(head, block, odd)
                slots[to, 0:ROWS, :] = both
                slots[to, ROWS : ROWS + 64, :] = queries_t[
                    64 * j : 64 * j + 64, block * HALF : (block + 1) * HALF
                ]
                slots[to, ROWS + 64 : SLOT, :] = jnp.broadcast_to(third, (16, 128)).astype(BF16)


def gather_heads(recv, odd, row, target):
    for head in range(HEADS):
        for block in range(2):
            target[64 * head : 64 * head + 64, block * HALF : (block + 1) * HALF] = recv[
                slot_of(head, block, odd), row : row + 64, :
            ]


def scatter_heads(features, odd, slots):
    for head in range(HEADS):
        for block in range(2):
            slots[slot_of(head, block, odd)] = features[
                64 * head : 64 * head + 64, block * HALF : (block + 1) * HALF
            ]


def mix(recv, stream, odd, gain, weights, features, acc, att_out, mid_out, normed_out, hidden_out, act_out):
    gather_heads(recv, odd, 0, features)
    attended = features[...].T
    att_out[...] = attended
    mid = stream + dot(attended, weights[0][...])
    mid_out[...] = mid
    normed_out[...] = (standardise(mid)[0] * gain).astype(BF16)
    acc[...] = mid
    up, down = weights[1].ready(), weights[2].ready()

    def step(c, _):
        here = pl.ds(pl.multiple_of(c * FF_BLOCK, FF_BLOCK), FF_BLOCK)
        hidden = dot(normed_out[...], up[:, here])
        hidden_out[:, here] = hidden
        active = gelu(hidden).astype(BF16)
        act_out[:, here] = active
        acc[...] += dot(active, down[here, :])
        return 0

    lax.fori_loop(0, FF // FF_BLOCK, step, 0)


def mix_back(grad, odd, gain, mid, hidden, weights, acc, dz_out, dh_out, dy_out, dmid_out, gain_out, slots):
    out, up, down = weights
    up, down = up.ready(), down.ready()
    dz_out[...] = grad.astype(BF16)
    acc[...] = jnp.zeros(acc.shape, F32)

    def step(c, _):
        here = pl.ds(pl.multiple_of(c * FF_BLOCK, FF_BLOCK), FF_BLOCK)
        grad_act = times_transposed(dz_out[...], down[here, :])
        low = (gelu_slope(hidden[:, here]) * grad_act).astype(BF16)
        dh_out[:, here] = low
        acc[...] += times_transposed(low, up[:, here])
        return 0

    lax.fori_loop(0, FF // FF_BLOCK, step, 0)
    grad_mid, grad_gain = standardise_back(acc[...], gain, mid[...])
    gain_out[...] = grad_gain
    grad_mid = grad_mid + grad
    dmid_out[...] = grad_mid
    for done in (dh_out, dmid_out, dz_out):
        if isinstance(done, Kept):
            done.flush()
    low = grad_mid.astype(BF16)
    dy_out[...] = low
    scatter_heads(times_transposed(low, out[...]).T.astype(BF16), odd, slots)


def project_back(recv, odd, gain, stream, grad_mid, w_qkv, features, dproj_out, gain_out):
    gather_heads(recv, odd, ROWS, features)
    dproj_out[:, 0:WIDTH] = features[...].T
    low_lanes = lax.broadcasted_iota(jnp.int32, (ROWS, 128), 1) < 64
    for pair in range(HEADS // 2):
        at = 128 * pair
        both = []
        for head in (2 * pair, 2 * pair + 1):
            one, two = recv[SLOT_OF[2 * head], 0:ROWS, :], recv[SLOT_OF[2 * head + 1], 0:ROWS, :]
            both.append(one.astype(F32) + two.astype(F32))
        keys = jnp.where(low_lanes, both[0], pltpu.roll(both[1], 64, 1)).astype(BF16)
        values = jnp.where(low_lanes, pltpu.roll(both[0], 64, 1), both[1]).astype(BF16)
        dproj_out[:, WIDTH + at : WIDTH + at + 128] = keys
        dproj_out[:, 2 * WIDTH + at : 2 * WIDTH + at + 128] = values
    grad_normed = times_transposed(dproj_out[...], w_qkv[...])
    grad_stream, grad_gain = standardise_back(grad_normed, gain, stream[...].astype(F32))
    gain_out[...] = grad_gain
    return grad_stream + grad_mid[...]


def enter_kernel(info, gain_attn, ins, outs):
    tokens, w_qkv = ins
    slots, normed = outs
    project(tokens[...].astype(F32), gain_attn[...], w_qkv, info[3], info[4].astype(F32), slots, normed)


def turn_kernel(info, passes, table, gain_attn, gain_mlp, ins, outs, features, acc):
    recv, tokens, w_out, w_up, w_down, w_qkv = ins
    slots, normed, second, att, mid, mid_normed, hidden, act = outs
    odd = info[3]
    mix(recv, tokens[...].astype(F32), odd, gain_mlp[...], (w_out, w_up, w_down), features, acc, att, mid, mid_normed, hidden, act)
    for out in (att, mid, mid_normed, hidden, act):
        out.flush()
    stream = acc[...]
    for row in range(PASSES):
        stream = stream + jnp.where(passes[...] == row, table[row : row + 1, :], 0.0)
    second[...] = stream
    second.flush()
    project(stream, gain_attn[...], w_qkv, odd, info[4].astype(F32), slots, normed)


def crest_kernel(info, gain_mlp, ins, outs, features, acc, mid, hidden, dz):
    recv, stream, w_out, w_up, w_down, cotangent = ins
    slots, mixed, att, mid_normed, act, dh, dy, dmid, gain_out = outs
    odd = info[3]
    gain = gain_mlp[...]
    mix(recv, stream[...], odd, gain, (w_out, w_up, w_down), features, acc, att, mid, mid_normed, hidden, act)
    mixed[...] = acc[...].astype(BF16)
    for out in (att, mid_normed, act, mixed):
        out.flush()
    mix_back(cotangent[...].astype(F32), odd, gain, mid, hidden, (w_out, w_up, w_down), acc, dz, dh, dy, dmid, gain_out, slots)


def return_kernel(info, passes, gain_attn, gain_mlp, ins, outs, features, acc):
    recv, w_qkv, stream, grad_mid, w_down, hidden, w_up, mid, w_out = ins
    slots, dproj, gain_attn_out, table_out, dz, dh, dy, dmid, gain_mlp_out = outs
    odd = info[3]
    grad = project_back(recv, odd, gain_attn[...], stream, grad_mid, w_qkv, features, dproj, gain_attn_out)
    dproj.flush()
    for row in range(PASSES):
        table_out[row : row + 1, :] = jnp.sum(jnp.where(passes[...] == row, grad, 0.0), axis=0, keepdims=True)
    table_out[PASSES:8, :] = jnp.zeros((8 - PASSES, WIDTH), F32)
    mix_back(grad, odd, gain_mlp[...], mid, hidden.ready(), (w_out, w_up, w_down), acc, dz, dh, dy, dmid, gain_mlp_out, slots)


def leave_kernel(info, gain_attn, ins, outs, features):
    recv, w_qkv, tokens, grad_mid = ins
    grad_tokens, dproj, gain_out = outs
    grad_tokens[...] = project_back(recv, info[3], gain_attn[...], tokens, grad_mid, w_qkv, features, dproj, gain_out)


def shape(*dims, dtype=BF16):
    return jax.ShapeDtypeStruct(dims, dtype)


def in_vmem(kernel, name, info, small, arrays, outs, scratch, flops):
    vmem = pl.BlockSpec(memory_space=pltpu.VMEM)
    hbm = pl.BlockSpec(memory_space=pl.ANY)
    ins, count = len(arrays), len(arrays) + len(outs)

    def body(info, *refs):
        few, refs = refs[: len(small)], refs[len(small) :]
        far, near, sems, rest = refs[:count], refs[count : 2 * count], refs[2 * count], refs[2 * count + 1 :]
        held = [Held(far[i], near[i], sems.at[i]) for i in range(ins)]
        kept = [Kept(near[i], far[i], sems.at[i]) for i in range(ins, count)]
        kernel(info, *few, held, kept, *rest)
        for one in kept:
            if not one.started:
                one.flush()
        for one in held:
            one.ready()
        for one in kept:
            one.finish()

    return pl.pallas_call(
        body,
        out_shape=tuple(outs),
        in_specs=[pl.BlockSpec(memory_space=pltpu.SMEM)] + [vmem] * len(small) + [hbm] * ins,
        out_specs=(hbm,) * len(outs),
        scratch_shapes=[pltpu.VMEM(x.shape, x.dtype) for x in (*arrays, *outs)]
        + [pltpu.SemaphoreType.DMA((count,))]
        + scratch,
        compiler_params=pltpu.CompilerParams(vmem_limit_bytes=56 << 20),
        cost_estimate=pl.CostEstimate(flops=int(flops), bytes_accessed=16 << 20, transcendentals=1 << 20),
        name=name,
    )(info, *small, *arrays)


EARLY = 21504
LATE = 7680
CORE = 5


def grads_kernel(info, small, ins, outs):
    mid_one, dh_one, mid_two, dh_two, act_one, dz_one, act_two, dz_two, att_one, dy_one, att_two, dy_two = ins
    core = info[CORE]

    def left(one, two):
        return jnp.concatenate([one, two], axis=0).T

    def put(half, row, rows, value):
        for to, out in enumerate(outs):

            @pl.when((half ^ core) == to)
            def _():
                for i in range(value.shape[1] // 128):
                    out[pl.ds(row + i * rows, value.shape[0]), :] = value[:, 128 * i : 128 * i + 128]

    mid = left(mid_one[...], mid_two[...])
    dh_one.ready(), dh_two.ready()

    def up(c, _):
        here = pl.ds(pl.multiple_of(c * 512, 512), 512)
        right = jnp.concatenate([dh_one[:, here], dh_two[:, here]], axis=0)
        result = dot(mid, right).astype(BF16)
        row = pl.multiple_of(c * 1536, 512)
        put(0, row, 384, result[:384])
        put(1, row, 384, result[384:])
        return 0

    lax.fori_loop(0, 6, up, 0)
    dz = jnp.concatenate([dz_one[...], dz_two[...]], axis=0)
    act_one.ready(), act_two.ready()

    def down(c, _):
        here = pl.ds(pl.multiple_of(c * 512, 512), 512)
        result = dot(left(act_one[:, here], act_two[:, here]), dz).astype(BF16)
        put(c // 3, pl.multiple_of(9216 + (c % 3) * 512, 512), 1536, result)
        return 0

    lax.fori_loop(0, 6, down, 0)
    dy = jnp.concatenate([dy_one[...], dy_two[...]], axis=0)
    result = dot(left(att_one[...], att_two[...]), dy).astype(BF16)
    put(0, 18432, 384, result[:384])
    put(1, 18432, 384, result[384:])
    for out in outs:
        out[20736:20784, :] = small[...].astype(BF16)


def grad_qkv_kernel(info, ins, outs):
    normed, dproj = ins
    left = normed[...].T
    dproj.ready()

    def step(c, _):
        result = dot(left, dproj[:, pl.ds(pl.multiple_of(c * 384, 384), 384)])
        for i in range(3):
            outs[0][3 * c + i] = result[:, 128 * i : 128 * i + 128]
        return 0

    lax.fori_loop(0, 6, step, 0)


def grad_qkv_both_kernel(info, gains, ins, outs):
    normed, dproj, before = ins
    left = normed[...].T
    dproj.ready(), before.ready()
    core = info[CORE]

    def step(c, _):
        result = dot(left, dproj[:, pl.ds(pl.multiple_of(c * 384, 384), 384)])
        for to, out in enumerate(outs):

            @pl.when(core == to)
            def _():
                for i in range(3):
                    part = (result[:384, 128 * i : 128 * i + 128] + before[3 * c + i, :384, :]).astype(BF16)
                    out[pl.ds(pl.multiple_of((3 * c + i) * 384, 384), 384), :] = part

            @pl.when(core != to)
            def _():
                for i in range(3):
                    part = (result[384:, 128 * i : 128 * i + 128] + before[3 * c + i, 384:, :]).astype(BF16)
                    out[pl.ds(pl.multiple_of((3 * c + i) * 384, 384), 384), :] = part

        return 0

    lax.fori_loop(0, 6, step, 0)
    for out in outs:
        out[6912:6928, :] = gains[...].astype(BF16)


def widen_kernel(core, mine, other, out):
    half = pl.program_id(0) // 3

    def put(ref):
        for i in range(ref.shape[0]):
            out[:, 128 * i : 128 * i + 128] = ref[i].astype(F32)

    @pl.when(half == core[0])
    def _():
        put(mine)

    @pl.when(half != core[0])
    def _():
        put(other)


def widen(core, mine, other, columns, height, first):
    def place(own):
        def index(i, core):
            low = core[0] == (0 if own else 1)
            part = jnp.where(low, jnp.minimum(i, 2), jnp.maximum(i - 3, 0))
            return (first // columns, part, 0)

        return pl.BlockSpec((columns, height // 3, 128), index)

    return pl.pallas_call(
        widen_kernel,
        out_shape=shape(2 * height, columns * 128, dtype=F32),
        grid_spec=pltpu.PrefetchScalarGridSpec(
            num_scalar_prefetch=1,
            grid=(6,),
            in_specs=[place(True), place(False)],
            out_specs=pl.BlockSpec((height // 3, columns * 128), lambda i, core: (i, 0)),
        ),
        compiler_params=pltpu.CompilerParams(vmem_limit_bytes=20 << 20),
        name="widen",
    )(core, mine.reshape(-1, height, 128), other.reshape(-1, height, 128))


def swap(value, bit):
    return lax.ppermute(value, "batch", [(i, i ^ bit) for i in range(4)])


def exchange(slots):
    return lax.all_to_all(slots, "seq", 0, 0)


def sum_cores(partial):
    mine, other = partial
    return (mine.astype(F32) + swap(other, 1).astype(F32)).astype(BF16)


def deal(half):
    return exchange(half.reshape(SEQ, half.shape[0] // SEQ, 128))


def sum_chips(blocks):
    block = jnp.sum(blocks.astype(F32), axis=0).astype(BF16)
    return (block.astype(F32) + swap(block, 2).astype(F32)).astype(BF16)


def spread(block):
    whole = exchange(jnp.broadcast_to(block[None], (SEQ, *block.shape))).reshape(-1, 128)
    return whole, swap(whole, 1)


def positions(half, first_row, count):
    at = lax.broadcasted_iota(jnp.int32, (1, count), 1)
    block = at // HALF
    return first_row + block * ROWS + ((half + block) % 2) * HALF + at % HALF


def third_keys(recv, count):
    last = recv[SEQ - 1, ROWS + 64 : SLOT, :].astype(F32)[0:1].astype(jnp.int32)
    row = last + (SEQ - 1) * ROWS
    return jnp.concatenate([row] * (count // 128), axis=1)


def first_keys(at, second, third):
    return jnp.where(at < second, 0, jnp.where(at < third, second, third))


def attend_kernel(info, recv_far, out_low_far, out_f_far, lse_far, kv_t_far, q_t_far, recv, out_low, out_f, lse, kv_t, q_t, sems, top, acc, *, devs):
    tile_rows = devs * HALF
    span = devs * ROWS
    active, half, second = info[0], info[1], info[2]

    @pl.when(active == 1)
    def _():
        parts = [
            Held(recv_far.at[8 * i : 8 * i + 8], recv.at[8 * i : 8 * i + 8], sems.at[i]) for i in range(4)
        ]
        fars = (kv_t_far, q_t_far, out_low_far, out_f_far, lse_far)
        kept = [
            Kept(near, far, sems.at[4 + i])
            for i, (near, far) in enumerate(zip((kv_t, q_t, out_low, out_f, lse), fars))
        ]
        ones = (lax.broadcasted_iota(jnp.int32, (16, ROWS), 0) == 0).astype(BF16)
        for d in range(SEQ):
            parts[d // 8].ready()
            keys = slice(d * ROWS, (d + 1) * ROWS)
            kv_t[0:128, keys] = recv[d, 0:ROWS, :].T
            kv_t[128:144, keys] = ones
            q_t[0:64, d * HALF : (d + 1) * HALF] = recv[d, ROWS : ROWS + 64, :]
        q_t[64:128, :] = jnp.zeros((64, SEQ * HALF), BF16)
        kept[0].flush()
        kept[1].flush()

        third = third_keys(recv, tile_rows)

        def one_tile(t, _):
            start = t * span
            columns = pl.ds(pl.multiple_of(t * tile_rows, tile_rows), tile_rows)
            at = positions(half, start, tile_rows)
            first = first_keys(at, second, third)
            top[...] = jnp.full((1, tile_rows), LOW, F32)
            acc[...] = jnp.zeros((80, tile_rows), F32)
            queries = q_t[:, columns]

            def update(scores, key_rows, left):
                here = slice(left, tile_rows)
                old_top = top[:, here]
                new_top = jnp.maximum(old_top, jnp.max(scores, axis=0, keepdims=True))
                weights = jnp.exp2(scores - new_top).astype(BF16)
                shrink = jnp.exp2(old_top - new_top)
                acc[:, here] = acc[:, here] * shrink + dot(kv_t[64:144, key_rows], weights)
                top[:, here] = new_top

            def whole(j, masked):
                key_start = pl.multiple_of(j * 1024, 1024)
                kv = recv[pl.ds(j * 4, 4), 0:ROWS, :].reshape(1024, 128)
                scores = dot(kv, queries) * LOG2E
                if masked:
                    key_at = lax.broadcasted_iota(jnp.int32, (1024, 1), 0)
                    scores = jnp.where(key_at >= second, scores, LOW)
                update(scores, pl.ds(key_start, 1024), 0)

            @pl.when(t > 0)
            def _():
                whole(0, True)

            def step(j, _):
                whole(j, False)
                return 0

            lax.fori_loop(1, t * (span // 1024), step, 0)
            fresh = first >= start
            top[...] = jnp.where(fresh, LOW, top[...])
            acc[...] = jnp.where(fresh, 0.0, acc[...])
            for i in range(devs // 2):
                left = 256 * i
                key_start = pl.multiple_of(start + 512 * i, 512)
                kv = recv[pl.ds(t * devs + 2 * i, 2), 0:ROWS, :].reshape(512, 128)
                scores = dot(kv, queries[:, left:]) * LOG2E
                key_at = key_start + lax.broadcasted_iota(jnp.int32, (512, 1), 0)
                allowed = (key_at >= first[:, left:]) & (key_at <= at[:, left:])
                update(jnp.where(allowed, scores, LOW), pl.ds(key_start, 512), left)
            total = acc[64:65, :]
            result = acc[0:64, :] / total
            out_f[:, columns] = result
            lse[:, columns] = top[...] + jnp.log2(total)
            low = result.astype(BF16)
            for i in range(devs):
                out_low[t * devs + i] = low[:, i * HALF : (i + 1) * HALF]
            return 0

        lax.fori_loop(0, SEQ // devs, one_tile, 0)
        for one in kept[2:]:
            one.flush()
        for one in kept:
            one.finish()


def attend(info, recv):
    devs = 8
    pairs = 17.8e6
    out_low, *rest = pl.pallas_call(
        functools.partial(attend_kernel, devs=devs),
        out_shape=(
            jax.ShapeDtypeStruct((SEQ, 64, HALF), BF16),
            jax.ShapeDtypeStruct((64, SEQ * HALF), F32),
            jax.ShapeDtypeStruct((1, SEQ * HALF), F32),
            jax.ShapeDtypeStruct((144, SEQ * ROWS), BF16),
            jax.ShapeDtypeStruct((128, SEQ * HALF), BF16),
        ),
        in_specs=[
            pl.BlockSpec(memory_space=pltpu.SMEM),
            pl.BlockSpec(memory_space=pl.ANY),
        ],
        out_specs=tuple(pl.BlockSpec(memory_space=pl.ANY) for _ in range(5)),
        scratch_shapes=[
            pltpu.VMEM((SEQ, SLOT, 128), BF16),
            pltpu.VMEM((SEQ, 64, HALF), BF16),
            pltpu.VMEM((64, SEQ * HALF), F32),
            pltpu.VMEM((1, SEQ * HALF), F32),
            pltpu.VMEM((144, SEQ * ROWS), BF16),
            pltpu.VMEM((128, SEQ * HALF), BF16),
            pltpu.SemaphoreType.DMA((9,)),
            pltpu.VMEM((1, devs * HALF), F32),
            pltpu.VMEM((80, devs * HALF), F32),
        ],
        compiler_params=pltpu.CompilerParams(vmem_limit_bytes=56 << 20),
        cost_estimate=pl.CostEstimate(
            flops=int(pairs * 1024), bytes_accessed=8 << 20, transcendentals=int(pairs)
        ),
        name="attend",
    )(info, recv)
    out_f, lse, kv_t, q_t = rest
    return out_low, recv, kv_t, q_t, out_f, lse


def attend_back_kernel(info, recv_far, kv_t_far, q_t_far, out_f_far, lse_far, grad_out_far, send_far, recv, kv_t, q_t, out_f, lse, grad_out, send, sems, grad_kv, do_t, grad_q, *, devs):
    tile_rows = devs * HALF
    span = devs * ROWS
    active, half, second = info[0], info[1], info[2]

    @pl.when(active == 1)
    def _():
        fars = (grad_out_far, recv_far, q_t_far, out_f_far, lse_far, kv_t_far)
        nears = (grad_out, recv, q_t, out_f, lse, kv_t)
        held = [Held(far, near, sems.at[i]) for i, (far, near) in enumerate(zip(fars, nears))]
        grad_kv[...] = jnp.zeros(grad_kv.shape, F32)
        held[0].ready()
        for d in range(SEQ):
            do_t[64:128, d * HALF : (d + 1) * HALF] = grad_out[d]
        do_t[0:64, :] = jnp.zeros((64, SEQ * HALF), BF16)
        for one in held:
            one.ready()

        third = third_keys(recv, tile_rows)

        def one_tile(t, _):
            start = t * span
            columns = pl.ds(pl.multiple_of(t * tile_rows, tile_rows), tile_rows)
            at = positions(half, start, tile_rows)
            first = first_keys(at, second, third)
            queries = q_t[:, columns]
            grads = do_t[:, columns]
            query_rows = queries.T
            grad_rows = grads.T
            delta = jnp.sum(
                grads[64:128, :].astype(F32) * out_f[:, columns], axis=0, keepdims=True
            )
            own_lse = lse[:, columns]
            far_lse = jnp.where(first >= start, -LOW, own_lse)
            grad_q[...] = jnp.zeros((64, tile_rows), F32)

            def update(kv, key_rows, left, row_lse, mask):
                here = slice(left, tile_rows)
                scores = dot(kv, queries[:, here]) * LOG2E
                probs = jnp.exp2(scores - row_lse[:, here])
                if mask is not None:
                    probs = jnp.where(mask, probs, 0.0)
                grad_probs = dot(kv, grads[:, here])
                grad_scores = (probs * (grad_probs - delta[:, here])).astype(BF16)
                grad_kv[key_rows, :] += dot(grad_scores, query_rows[here, :]) + dot(
                    probs.astype(BF16), grad_rows[here, :]
                )
                grad_q[:, here] += dot(kv_t[0:64, key_rows], grad_scores)

            def whole(j, masked):
                key_start = pl.multiple_of(j * 1024, 1024)
                kv = recv[pl.ds(j * 4, 4), 0:ROWS, :].reshape(1024, 128)
                mask = None
                if masked:
                    mask = lax.broadcasted_iota(jnp.int32, (1024, 1), 0) >= second
                update(kv, pl.ds(key_start, 1024), 0, far_lse, mask)

            @pl.when(t > 0)
            def _():
                whole(0, True)

            def step(j, _):
                whole(j, False)
                return 0

            lax.fori_loop(1, t * (span // 1024), step, 0)
            for i in range(devs // 2):
                left = 256 * i
                key_start = pl.multiple_of(start + 512 * i, 512)
                kv = recv[pl.ds(t * devs + 2 * i, 2), 0:ROWS, :].reshape(512, 128)
                key_at = key_start + lax.broadcasted_iota(jnp.int32, (512, 1), 0)
                allowed = (key_at >= first[:, left:]) & (key_at <= at[:, left:])
                update(kv, pl.ds(key_start, 512), left, own_lse, allowed)
            low = (grad_q[...] * HEAD_DIM**-0.5).astype(BF16)
            for i in range(devs):
                send[t * devs + i, ROWS:, :] = low[:, i * HALF : (i + 1) * HALF]
            return 0

        lax.fori_loop(0, SEQ // devs, one_tile, 0)
        for d in range(SEQ):
            send[d, 0:ROWS, :] = grad_kv[d * ROWS : (d + 1) * ROWS, :].astype(BF16)
        out = Kept(send, send_far, sems.at[6])
        out.finish()


def attend_back(info, recv, kv_t, q_t, out_f, lse, grad_out):
    devs = 4
    pairs = 17.8e6
    return pl.pallas_call(
        functools.partial(attend_back_kernel, devs=devs),
        out_shape=jax.ShapeDtypeStruct((SEQ, ROWS + 64, HALF), BF16),
        in_specs=[pl.BlockSpec(memory_space=pltpu.SMEM)]
        + [pl.BlockSpec(memory_space=pl.ANY)] * 6,
        out_specs=pl.BlockSpec(memory_space=pl.ANY),
        scratch_shapes=[
            pltpu.VMEM((SEQ, SLOT, 128), BF16),
            pltpu.VMEM((144, SEQ * ROWS), BF16),
            pltpu.VMEM((128, SEQ * HALF), BF16),
            pltpu.VMEM((64, SEQ * HALF), F32),
            pltpu.VMEM((1, SEQ * HALF), F32),
            pltpu.VMEM((SEQ, 64, HALF), BF16),
            pltpu.VMEM((SEQ, ROWS + 64, HALF), BF16),
            pltpu.SemaphoreType.DMA((7,)),
            pltpu.VMEM((SEQ * ROWS, 128), F32),
            pltpu.VMEM((128, SEQ * HALF), BF16),
            pltpu.VMEM((64, devs * HALF), F32),
        ],
        compiler_params=pltpu.CompilerParams(vmem_limit_bytes=56 << 20),
        cost_estimate=pl.CostEstimate(
            flops=int(pairs * 1024), bytes_accessed=8 << 20, transcendentals=int(pairs)
        ),
        name="attend_back",
    )(info, recv, kv_t, q_t, out_f, lse, grad_out)


def on_device(
    tokens,
    token_pos,
    token_pass,
    token_count,
    w_qkv,
    w_out,
    w_up,
    w_down,
    gain_attn,
    gain_mlp,
    pass_table,
    cotangent,
):
    here = lax.axis_index("seq")
    offset = token_pos[0] * token_count[0] + token_pass[0]
    first_token = here * ROWS - offset[0]
    last_token = here * ROWS + ROWS - 1 - offset[ROWS - 1]
    second = jnp.where(here == 0, last_token, first_token)
    third = last_token - (SEQ - 1) * ROWS
    third = jnp.where((third < 0) | (third > ROWS), ROWS, third)
    group, place = here // 4, here % 4
    active = (place < 3).astype(jnp.int32)
    core = lax.axis_index("batch") % 2
    info = jnp.stack([active, (3 * group + place) % 2, second, here % 2, third, core])
    passes = token_pass[0][:, None]
    table = jnp.pad(pass_table, ((0, 8 - PASSES), (0, 0)))
    gain_a, gain_m = gain_attn[None], gain_mlp[None]
    stream_one = tokens[0]
    features = pltpu.VMEM((WIDTH, ROWS), BF16)
    acc = pltpu.VMEM((ROWS, WIDTH), F32)
    square = shape(ROWS, WIDTH)
    wide = shape(ROWS, WIDTH, dtype=F32)
    row = shape(1, WIDTH, dtype=F32)
    sent = shape(SEQ, SLOT, 128)
    sent_back = shape(SEQ, 64, 128)

    slots, normed_one = in_vmem(
        enter_kernel, "enter", info, (gain_a,), (stream_one, w_qkv), (sent, square), [], 1e9
    )
    saved_one = attend(info, exchange(slots))
    slots, normed_two, stream_two, att_one, mid_one, midn_one, hidden_one, act_one = in_vmem(
        turn_kernel,
        "turn",
        info,
        (passes, table, gain_a, gain_m),
        (exchange(saved_one[0]), stream_one, w_out, w_up, w_down, w_qkv),
        (sent, square, wide, square, wide, square, shape(ROWS, FF, dtype=F32), shape(ROWS, FF)),
        [features, acc],
        3.6e9,
    )
    saved_two = attend(info, exchange(slots))
    slots, mixed, att_two, midn_two, act_two, dh_two, dy_two, dmid_two, gain_m_two = in_vmem(
        crest_kernel,
        "crest",
        info,
        (gain_m,),
        (exchange(saved_two[0]), stream_two, w_out, w_up, w_down, cotangent[0]),
        (sent_back, square, square, square, shape(ROWS, FF), shape(ROWS, FF), square, wide, row),
        [features, acc, acc, pltpu.VMEM((ROWS, FF), F32), pltpu.VMEM((ROWS, WIDTH), BF16)],
        5e9,
    )
    back = exchange(slots)
    recv = exchange(attend_back(info, *saved_two[1:], back))
    slots, dproj_two, gain_a_two, grad_table, dz_one, dh_one, dy_one, dmid_one, gain_m_one = in_vmem(
        return_kernel,
        "return",
        info,
        (passes, gain_a, gain_m),
        (recv, w_qkv, stream_two, dmid_two, w_down, hidden_one, w_up, mid_one, w_out),
        (
            sent_back,
            shape(ROWS, 3 * WIDTH),
            row,
            shape(8, WIDTH, dtype=F32),
            square,
            shape(ROWS, FF),
            square,
            wide,
            row,
        ),
        [features, acc],
        5e9,
    )
    back = exchange(slots)
    small = jnp.concatenate(
        [grad_table[:PASSES], gain_a_two, gain_m_one + gain_m_two, jnp.zeros((1, WIDTH), F32)]
    ).reshape(48, 128)
    early = in_vmem(
        grads_kernel,
        "grads",
        info,
        (small,),
        (midn_one, dh_one, midn_two, dh_two, act_one, dz_one, act_two, cotangent[0], att_one, dy_one, att_two, dy_two),
        (shape(EARLY, 128),) * 2,
        [],
        5.4e10,
    )
    early = sum_cores(early)
    back, early = lax.optimization_barrier((back, early))
    sent_one = attend_back(info, *saved_one[1:], back)
    sent_one, early = lax.optimization_barrier((sent_one, deal(early)))
    recv = exchange(sent_one)
    early = sum_chips(early)
    grad_tokens, dproj_one, gain_a_one = in_vmem(
        leave_kernel,
        "leave",
        info,
        (gain_a,),
        (recv, w_qkv, stream_one, dmid_one),
        (wide, shape(ROWS, 3 * WIDTH), row),
        [features],
        1e9,
    )
    (grad_two,) = in_vmem(
        grad_qkv_kernel,
        "grad_qkv_two",
        info,
        (),
        (normed_two, dproj_two),
        (shape(18, WIDTH, 128, dtype=F32),),
        [],
        9e8,
    )
    late = in_vmem(
        grad_qkv_both_kernel,
        "grad_qkv",
        info,
        (jnp.pad(gain_a_one.reshape(6, 128), ((0, 10), (0, 0))),),
        (normed_one, dproj_one, grad_two),
        (shape(LATE, 128),) * 2,
        [],
        9e8,
    )
    core = info[CORE : CORE + 1]
    early = spread(early)
    grad_down = widen(core, *early, 6, 1536, 6)
    grad_up = widen(core, *early, 24, 384, 0)
    grad_out = widen(core, *early, 6, 384, 48)
    late = sum_chips(deal(sum_cores(late)))
    late, grad_down, grad_up, grad_out = lax.optimization_barrier((late, grad_down, grad_up, grad_out))
    late = spread(late)
    tail = early[0][20736:20784].reshape(8, WIDTH).astype(F32)
    gain_a_sum = late[0][6912:6918].reshape(WIDTH).astype(F32)
    return (
        mixed[None],
        grad_tokens[None],
        widen(core, *late, 18, 384, 0),
        grad_out,
        grad_up,
        grad_down,
        tail[PASSES] + gain_a_sum,
        tail[PASSES + 1],
        tail[:PASSES],
    )


def solution(mesh):
    return jax.shard_map(
        on_device,
        mesh=mesh,
        in_specs=(
            P("batch", "seq", None),
            P("batch", "seq"),
            P("batch", "seq"),
            P("batch", "seq"),
            P(),
            P(),
            P(),
            P(),
            P(),
            P(),
            P(),
            P("batch", "seq", None),
        ),
        out_specs=(
            P("batch", "seq", None),
            P("batch", "seq", None),
            P(),
            P(),
            P(),
            P(),
            P(),
            P(),
            P(),
        ),
        check_vma=False,
    )
```

time: 2290 us -> 708 us (0.31)
  waiting for transfers between devices: 1840 us -> 131 us
  Pallas kernels: 0 us -> 298 us
  local copies, waits for them, and re-layouts: 194 us -> 13 us
  blocking collectives: 64.2 us -> 174 us
  matrix products: 89.7 us -> 0 us
  starting transfers between devices: 0.63 us -> 61.9 us
  loops' own time: 42.2 us -> 0 us
    reduce_scatter x2 -> x0, waiting for transfers between devices: 997 us -> none  [block_backward(): lax.psum_scatter(key_grads.astype(jnp.bfloat16), 'seq', scatter_dimension...]
    all_gather x2 -> x0, waiting for transfers between devices: 684 us -> none  [sent_together(): lax.all_gather(both, axis, axis=dim, tiled=True)]
    pallas_call x0 -> x16, Pallas kernels: none -> 298 us  [the longest x2 112 us: attend_back(): pl.pallas_call(functools.partial(attend_back_kernel, devs=devs), out_shap...]
    all_to_all x0 -> x6, blocking collectives: none -> 174 us  [exchange(): return lax.all_to_all(slots, 'seq', 0, 0)]
    psum x1 -> x0, waiting for transfers between devices: 157 us -> none  [on_device(): lax.psum((summed_parts[0], summed_parts[1], summed_parts[2], summed_parts...]
    unnamed x220 -> x16, local copies, waits for them, and re-layouts: 96.6 us -> 3.1 us
    all_to_all x0 -> x6, waiting for transfers between devices: none -> 91.8 us  [exchange(): return lax.all_to_all(slots, 'seq', 0, 0)]
    dot_general x40 -> x0, matrix products: 89.7 us -> none  [the longest x8 25.8 us: contract_rows(): lax.dot_general(left, right, (((0,), (0,)), ((), ())), preferred_element_...]
  transfers between devices with their start and end apart: 5 -> 12, of which waited for: 5 -> 8; matrix products, arithmetic and copies ran while one was open for 2% -> 3% of each run, Pallas kernels for 0% -> 11%
where the time goes in v1:
time: 708 us; the launch traced here: 699 us
  Pallas kernels  298 us (42%)
  blocking collectives  174 us (25%)
  waiting for transfers between devices  131 us (19%)
  starting transfers between devices  61.9 us (9%)
  other arithmetic  17.8 us (3%)
  local copies, waits for them, and re-layouts  13 us (2%)
    all_to_all x6, blocking collectives, exchange(): return lax.all_to_all(slots, 'seq', 0, 0)  174 us
    pallas_call x2, Pallas kernels, attend_back(): pl.pallas_call(functools.partial(attend_back_kernel, devs=devs), out_shap...  112 us
    pallas_call x8, Pallas kernels, in_vmem(): pl.pallas_call(body, out_shape=tuple(outs), in_specs=[pl.BlockSpec(memory...  93.2 us
    all_to_all x6, waiting for transfers between devices, exchange(): return lax.all_to_all(slots, 'seq', 0, 0)  91.8 us
    pallas_call x2, Pallas kernels, attend(): pl.pallas_call(functools.partial(attend_kernel, devs=devs), out_shape=(ja...  68.5 us
    all_to_all x6, starting transfers between devices, exchange(): return lax.all_to_all(slots, 'seq', 0, 0)  42.9 us
    ppermute x6, waiting for transfers between devices, swap(): return lax.ppermute(value, 'batch', [(i, i ^ bit) for i in range(4)])  38.8 us
    pallas_call x4, Pallas kernels, widen(): pl.pallas_call(widen_kernel, out_shape=shape(2 * height, columns * 128, d...  24.7 us
  transfers between devices with their start and end apart: 12, of which 8 were waited for; matrix products, arithmetic and copies ran while one was open for 3% of the time, Pallas kernels for 11%

profile of v1, /device:TPU:1, one launch (start us, length us, event | category | flops | bytes accessed | tf_op | source)
XLA Modules:
  0.0 698.7 jit_solution(13400425117372285509)
XLA Ops:
  5.2 6.6 enter.1
  11.8 43.0 %all_to_all.60.recv_far = bf16[32,336,128]{2,1,0:T(8,128)(2,1)} all-to-all(bf16[32,336,128]{2,1,0:T(8,128)(2,1)} %get-tuple-element.62), channel_id=1, replica_groups=mesh['seq'=32,'batch'=4] {'seq'}, dimensions={0} | all-to-all | bytes 5505024 | tf_op jit(solution)/shard_map/all_to_all | solution.py:449
  54.8 34.3 %attend.2 = (bf16[32,64,128]{2,1,0:T(8,128)(2,1)}, f32[64,4096]{1,0:T(8,128)}, f32[1,4096]{1,0:T(1,128)}, bf16[144,8192]{1,0:T(8,128)(2,1)}, bf16[128,4096]{1,0:T(8,128)(2,1)}) custom-call(s32[6]{0:T(128)} %stack.31.info, bf16[32,336,128]{2,1,0:T(8,128)(2,1)} %all_to_all.60.recv_far), custom_call_target="tpu_custom_call" | custom-call | flops 18227200000 | bytes 8388608 | tf_op jit(solution)/shard_map/attend/pallas_call | solution.py:581
  96.0 7.4 %all-to-all-done.1.refs_4_ = bf16[32,64,128]{2,1,0:T(8,128)(2,1)S(1)} async-done(((bf16[32,64,128]{2,1,0:T(8,128)(2,1)}), bf16[32,64,128]{2,1,0:T(8,128)(2,1)S(1)}, u32[]{:S(2)}, u32[]{:S(2)}) %all-to-all-start.1) | async-done | bytes 524320 | tf_op jit(solution)/shard_map/all_to_all | solution.py:449
  104.2 14.2 %turn.1 = (bf16[32,336,128]{2,1,0:T(8,128)(2,1)}, bf16[256,768]{1,0:T(8,128)(2,1)}, f32[256,768]{1,0:T(8,128)}, bf16[256,768]{1,0:T(8,128)(2,1)}, f32[256,768]{1...) custom-call(s32[6]{0:T(128)} %stack.31.info, s32[256,1]{1,0:T(8,128)} %copy.21.refs_0_, ...), custom_call_target="tpu_custom_call" | custom-call | flops 3600000000 | bytes 16777216 | tf_op jit(solution)/shard_map/turn/pallas_call | solution.py:297
  118.4 36.5 %all_to_all.61.recv_far = bf16[32,336,128]{2,1,0:T(8,128)(2,1)} all-to-all(bf16[32,336,128]{2,1,0:T(8,128)(2,1)} %get-tuple-element.64), channel_id=1, replica_groups=mesh['seq'=32,'batch'=4] {'seq'}, dimensions={0} | all-to-all | bytes 5505024 | tf_op jit(solution)/shard_map/all_to_all | solution.py:449
  155.0 34.2 %attend.3 = (bf16[32,64,128]{2,1,0:T(8,128)(2,1)}, f32[64,4096]{1,0:T(8,128)}, f32[1,4096]{1,0:T(1,128)}, bf16[144,8192]{1,0:T(8,128)(2,1)}, bf16[128,4096]{1,0:T(8,128)(2,1)}) custom-call(s32[6]{0:T(128)} %stack.31.info, bf16[32,336,128]{2,1,0:T(8,128)(2,1)} %all_to_all.61.recv_far), custom_call_target="tpu_custom_call" | custom-call | flops 18227200000 | bytes 8388608 | tf_op jit(solution)/shard_map/attend/pallas_call | solution.py:581
  189.2 14.2 %all_to_all.62.refs_1_ = bf16[32,64,128]{2,1,0:T(8,128)(2,1)} all-to-all(bf16[32,64,128]{2,1,0:T(8,128)(2,1)} %get-tuple-element.65), channel_id=1, replica_groups=mesh['seq'=32,'batch'=4] {'seq'}, dimensions={0} | all-to-all | bytes 1048576 | tf_op jit(solution)/shard_map/all_to_all | solution.py:449
  203.4 17.0 %crest.1 = (bf16[32,64,128]{2,1,0:T(8,128)(2,1)}, bf16[256,768]{1,0:T(8,128)(2,1)}, bf16[256,768]{1,0:T(8,128)(2,1)}, bf16[256,768]{1,0:T(8,128)(2,1)}, bf16[256...) custom-call(s32[6]{0:T(128)} %stack.31.info, ...), custom_call_target="tpu_custom_call" | custom-call | flops 5000000000 | bytes 16777216 | tf_op jit(solution)/shard_map/crest/pallas_call | solution.py:297
  220.4 13.6 %all_to_all.63.grad_out_far = bf16[32,64,128]{2,1,0:T(8,128)(2,1)} all-to-all(bf16[32,64,128]{2,1,0:T(8,128)(2,1)} %get-tuple-element.76), channel_id=1, replica_groups=mesh['seq'=32,'batch'=4] {'seq'}, dimensions={0} | all-to-all | bytes 1048576 | tf_op jit(solution)/shard_map/all_to_all | solution.py:449
  234.0 55.8 %attend_back.2 = bf16[32,320,128]{2,1,0:T(8,128)(2,1)} custom-call(s32[6]{0:T(128)} %stack.31.info, bf16[32,336,128]{2,1,0:T(8,128)(2,1)} %all_to_all.61.recv_far, bf16[144,8192]{1,0:T(8,128)(2,1)} %get-tuple-element.72.kv_t_far, bf16[128,4096]{1,0:T(8,128)(2,1)} %get-tuple-element.73.q_t_far, f32[64,4096]{1,0:T(8,128)} %get-tuple-element.74.out_f_far, ...), custom_call_target="tpu_custom_call" | custom-call | flops 18227200000 | bytes 8388608 | tf_op jit(solution)/shard_map/attend_back/pallas_call | solution.py:704
  294.2 27.8 %all-to-all-done.5.refs_3_ = bf16[32,320,128]{2,1,0:T(8,128)(2,1)S(1)} async-done(((bf16[32,320,128]{2,1,0:T(8,128)(2,1)}), bf16[32,320,128]{2,1,0:T(8,128)(2,1)S(1)}, u32[]{:S(2)}, u32[]{:S(2)}) %all-to-all-start.5) | async-done | bytes 2621472 | tf_op jit(solution)/shard_map/all_to_all | solution.py:449
  323.5 15.6 %return.1 = (bf16[32,64,128]{2,1,0:T(8,128)(2,1)}, bf16[256,2304]{1,0:T(8,128)(2,1)}, f32[1,768]{1,0:T(1,128)}, f32[8,768]{1,0:T(8,128)}, bf16[256,768]{1,0:T(8,...) custom-call(s32[6]{0:T(128)} %stack.31.info, ...), custom_call_target="tpu_custom_call" | custom-call | flops 5000000000 | bytes 16777216 | tf_op jit(solution)/shard_map/return/pallas_call | solution.py:297
  341.2 16.9 %grads.1 = (bf16[21504,128]{1,0:T(8,128)(2,1)}, bf16[21504,128]{1,0:T(8,128)(2,1)}) custom-call(s32[6]{0:T(128)} %stack.31.info, f32[48,128]{1,0:T(8,128)} %reshape.64.refs_0_, bf16[256,768]{1,0:T(8,128)(2,1)} %get-tuple-element.85.refs_1_, bf16[256,3072]{1,0:T(8,128)(2,1)} %get-tuple-element.86.refs_2_, bf16[256,768]{1,0:T(8,128)(2,1)} %get-tuple-element.87.refs_3_, ...), custom_call_target="tpu_custom_call" | custom-call | flops 54000001024 | bytes 16777216 | tf_op jit(solution)/shard_map/grads/pallas_call | solution.py:297
  358.1 6.9 collective-permute-start
  365.0 5.9 all-to-all-start.6
  374.1 7.7 %add_convert_fusion = bf16[21504,128]{1,0:T(8,128)(2,1)} fusion(bf16[21504,128]{1,0:T(8,128)(2,1)} %collective-permute-done, bf16[21504,128]{1,0:T(8,128)(2,1)} %get-tuple-element.96), kind=kLoop, calls=%fused_computation | loop fusion | flops 11010048 | bytes 16515072 | tf_op jit(solution)/shard_map/convert_element_type | solution.py:454
  382.6 6.0 all-to-all-start.7
  388.6 56.0 %attend_back.3 = bf16[32,320,128]{2,1,0:T(8,128)(2,1)} custom-call(s32[6]{0:T(128)} %stack.31.info, bf16[32,336,128]{2,1,0:T(8,128)(2,1)} %all_to_all.60.recv_far, bf16[144,8192]{1,0:T(8,128)(2,1)} %get-tuple-element.68.kv_t_far, bf16[128,4096]{1,0:T(8,128)(2,1)} %get-tuple-element.69.q_t_far, f32[64,4096]{1,0:T(8,128)} %get-tuple-element.70.out_f_far, ...), custom_call_target="tpu_custom_call" | custom-call | flops 18227200000 | bytes 8388608 | tf_op jit(solution)/shard_map/attend_back/pallas_call | solution.py:704
  444.7 13.3 %all-to-all-done.7 = bf16[32,672,128]{2,1,0:T(8,128)(2,1)} async-done(((bf16[32,672,128]{2,1,0:T(8,128)(2,1)}), bf16[32,672,128]{2,1,0:T(8,128)(2,1)}, u32[]{:S(2)}, u32[]{:S(2)}) %all-to-all-start.7) | async-done | bytes 5505056 | tf_op jit(solution)/shard_map/all_to_all | solution.py:449
  457.9 15.3 %all-to-all-start.8 = ((bf16[32,320,128]{2,1,0:T(8,128)(2,1)}), bf16[32,320,128]{2,1,0:T(8,128)(2,1)S(1)}, u32[]{:S(2)}, u32[]{:S(2)}) async-start(bf16[32,320,128]{2,1,0:T(8,128)(2,1)} %attend_back.3), calls=%async_computation.8 | async-start | bytes 5242880 | tf_op jit(solution)/shard_map/all_to_all | solution.py:449
  480.1 30.2 %collective-permute-done.3 = bf16[672,128]{1,0:T(8,128)(2,1)S(1)} collective-permute-done((bf16[672,128]{1,0:T(8,128)(2,1)S(1)}, bf16[672,128]{1,0:T(8,128)(2,1)S(1)}, u32[]{:S(2)}, u32[]{:S(2)}) %collective-permute-start.3) | collective-permute-done | bytes 172064 | tf_op jit(solution)/shard_map/ppermute | solution.py:445
  513.7 6.5 all-to-all-start.10
  520.2 7.2 %grad_qkv_two.1.refs_3_ = f32[18,768,128]{2,1,0:T(8,128)} custom-call(s32[6]{0:T(128)} %stack.31.info, bf16[256,768]{1,0:T(8,128)(2,1)} %get-tuple-element.106.refs_0_, bf16[256,2304]{1,0:T(8,128)(2,1)} %get-tuple-element.107.refs_1_), custom_call_target="tpu_custom_call" | custom-call | flops 900000000 | bytes 16777216 | tf_op jit(solution)/shard_map/grad_qkv_two/pallas_call | solution.py:297
  527.5 6.5 leave.1
  535.3 9.1 %grad_qkv.1 = (bf16[7680,128]{1,0:T(8,128)(2,1)}, bf16[7680,128]{1,0:T(8,128)(2,1)}) custom-call(s32[6]{0:T(128)} %stack.31.info, f32[16,128]{1,0:T(8,128)} %pad.9.refs_0_, bf16[256,768]{1,0:T(8,128)(2,1)} %get-tuple-element.104.refs_1_, bf16[256,2304]{1,0:T(8,128)(2,1)} %get-tuple-element.105.refs_2_, f32[18,768,128]{2,1,0:T(8,128)} %grad_qkv_two.1.refs_3_), custom_call_target="tpu_custom_call" | custom-call | flops 900000000 | bytes 16777216 | tf_op jit(solution)/shard_map/grad_qkv/pallas_call | solution.py:297
  545.2 43.3 %all-to-all-done.10 = bf16[32,672,128]{2,1,0:T(8,128)(2,1)} async-done(((bf16[32,672,128]{2,1,0:T(8,128)(2,1)}), bf16[32,672,128]{2,1,0:T(8,128)(2,1)}, u32[]{:S(2)}, u32[]{:S(2)}) %all-to-all-start.10) | async-done | bytes 5505056 | tf_op jit(solution)/shard_map/all_to_all | solution.py:449
  593.2 39.7 %all_to_all.64 = bf16[32,240,128]{2,1,0:T(8,128)(2,1)S(1)} all-to-all(bf16[32,240,128]{2,1,0:T(8,128)(2,1)S(1)} %bitcast.34), channel_id=1, replica_groups=mesh['seq'=32,'batch'=4] {'seq'}, dimensions={0} | all-to-all | bytes 3932160 | tf_op jit(solution)/shard_map/all_to_all | solution.py:449
  642.6 7.3 %widen.5 = f32[768,3072]{1,0:T(8,128)} custom-call(s32[1]{0:T(128)} %bitcast.7.core, bf16[56,384,128]{2,1,0:T(8,128)(2,1)} %bitcast.18.mine, bf16[56,384,128]{2,1,0:T(8,128)(2,1)} %bitcast.19.other), custom_call_target="tpu_custom_call" | custom-call | tf_op jit(solution)/shard_map/widen/pallas_call | solution.py:430
  649.9 7.2 %widen.4 = f32[3072,768]{1,0:T(8,128)} custom-call(s32[1]{0:T(128)} %bitcast.7.core, bf16[14,1536,128]{2,1,0:T(8,128)(2,1)} %bitcast.15.mine, bf16[14,1536,128]{2,1,0:T(8,128)(2,1)} %bitcast.17.other), custom_call_target="tpu_custom_call" | custom-call | tf_op jit(solution)/shard_map/widen/pallas_call | solution.py:430
  657.4 27.3 %all_to_all.65 = bf16[32,240,128]{2,1,0:T(8,128)(2,1)S(1)} all-to-all(bf16[32,240,128]{2,1,0:T(8,128)(2,1)S(1)} %broadcast_in_dim.33), channel_id=1, replica_groups=mesh['seq'=32,'batch'=4] {'seq'}, dimensions={0} | all-to-all | bytes 3932160 | tf_op jit(solution)/shard_map/all_to_all | solution.py:449
  692.8 5.4 widen.7
  (55 shorter events, 57.8 us)
Async XLA Ops:
  54.8 39.2 %copy-start.6 = (f32[768]{0:T(1024)S(1)}, f32[768]{0:T(1024)}, u32[]{:S(2)}) copy-start(f32[768]{0:T(1024)} %param.21) | copy-start | bytes 9220
  54.8 39.8 %copy-start.5 = (s32[1,256]{1,0:T(1,128)S(1)}, s32[1,256]{1,0:T(1,128)}, u32[]{:S(2)}) copy-start(s32[1,256]{1,0:T(1,128)} %param.14) | copy-start | bytes 3076
  54.8 40.6 %copy-start.4 = (f32[5,768]{1,0:T(8,128)S(1)}, f32[5,768]{1,0:T(8,128)}, u32[]{:S(2)}) copy-start(f32[5,768]{1,0:T(8,128)} %param.22) | copy-start | bytes 46084
  89.1 14.3 %all-to-all-start.1 = ((bf16[32,64,128]{2,1,0:T(8,128)(2,1)}), bf16[32,64,128]{2,1,0:T(8,128)(2,1)S(1)}, u32[]{:S(2)}, u32[]{:S(2)}) async-start(bf16[32,64,128]{2,1,0:T(8,128)(2,1)} %get-tuple-element.63), calls=%async_computation.1 | async-start | bytes 1048576 | tf_op jit(solution)/shard_map/all_to_all | solution.py:449
  103.5 0.8 copy-start.2
  289.8 32.2 %all-to-all-start.5 = ((bf16[32,320,128]{2,1,0:T(8,128)(2,1)}), bf16[32,320,128]{2,1,0:T(8,128)(2,1)S(1)}, u32[]{:S(2)}, u32[]{:S(2)}) async-start(bf16[32,320,128]{2,1,0:T(8,128)(2,1)} %attend_back.2), calls=%async_computation.5 | async-start | bytes 5242880 | tf_op jit(solution)/shard_map/all_to_all | solution.py:449
  322.0 1.5 copy-start.1
  323.5 15.6 %copy-start.7 = (f32[1,768]{1,0:T(1,128)S(1)}, f32[1,768]{1,0:T(1,128)}, u32[]{:S(2)}) copy-start(f32[1,768]{1,0:T(1,128)} %get-tuple-element.84) | copy-start | bytes 9220
  358.1 15.9 %collective-permute-start = (bf16[21504,128]{1,0:T(8,128)(2,1)}, bf16[21504,128]{1,0:T(8,128)(2,1)}, u32[]{:S(2)}, u32[]{:S(2)}) collective-permute-start(bf16[21504,128]{1,0:T(8,128)(2,1)} %get-tuple-element.97), channel_id=1, source_target_pairs={{0,1},{1,0},{2,3},{3,2},{4,5},{5,4},{6,7},{7,6},{8,9},{9,8},{10,11... | collective-permute-start | bytes 16515080 | tf_op jit(solution)/shard_map/ppermute | solution.py:445
  365.0 16.8 %all-to-all-start.6 = ((bf16[32,64,128]{2,1,0:T(8,128)(2,1)}), bf16[32,64,128]{2,1,0:T(8,128)(2,1)S(1)}, u32[]{:S(2)}, u32[]{:S(2)}) async-start(bf16[32,64,128]{2,1,0:T(8,128)(2,1)} %get-tuple-element.80), calls=%async_computation.6 | async-start | bytes 1048576 | tf_op jit(solution)/shard_map/all_to_all | solution.py:449
  381.8 0.8 copy-start.3
  382.6 75.3 %all-to-all-start.7 = ((bf16[32,672,128]{2,1,0:T(8,128)(2,1)}), bf16[32,672,128]{2,1,0:T(8,128)(2,1)}, u32[]{:S(2)}, u32[]{:S(2)}) async-start(bf16[32,672,128]{2,1,0:T(8,128)(2,1)} %bitcast.33), calls=%async_computation.7 | async-start | bytes 11010048 | tf_op jit(solution)/shard_map/all_to_all | solution.py:449
  457.9 52.4 %all-to-all-start.8 = ((bf16[32,320,128]{2,1,0:T(8,128)(2,1)}), bf16[32,320,128]{2,1,0:T(8,128)(2,1)S(1)}, u32[]{:S(2)}, u32[]{:S(2)}) async-start(bf16[32,320,128]{2,1,0:T(8,128)(2,1)} %attend_back.3), calls=%async_computation.8 | async-start | bytes 5242880 | tf_op jit(solution)/shard_map/all_to_all | solution.py:449
  476.7 33.6 %collective-permute-start.3 = (bf16[672,128]{1,0:T(8,128)(2,1)S(1)}, bf16[672,128]{1,0:T(8,128)(2,1)S(1)}, u32[]{:S(2)}, u32[]{:S(2)}) collective-permute-start(bf16[672,128]{1,0:T(8,128)(2,1)S(1)} %reduce_sum.25), channel_id=1, source_target_pairs={{0,2},{1,3},{2,0},{3,1},{4,6},{5,7},{6,4},{7,5},{8,10},{9,11},{10,... | collective-permute-start | bytes 516104 | tf_op jit(solution)/shard_map/ppermute | solution.py:445
  510.4 3.3 copy-start
  513.7 74.8 %all-to-all-start.10 = ((bf16[32,672,128]{2,1,0:T(8,128)(2,1)}), bf16[32,672,128]{2,1,0:T(8,128)(2,1)}, u32[]{:S(2)}, u32[]{:S(2)}) async-start(bf16[32,672,128]{2,1,0:T(8,128)(2,1)} %broadcast_in_dim.32), calls=%async_computation.10 | async-start | bytes 11010048 | tf_op jit(solution)/shard_map/all_to_all | solution.py:449
  544.4 46.7 %collective-permute-start.1 = (bf16[7680,128]{1,0:T(8,128)(2,1)}, bf16[7680,128]{1,0:T(8,128)(2,1)S(1)}, u32[]{:S(2)}, u32[]{:S(2)}) collective-permute-start(bf16[7680,128]{1,0:T(8,128)(2,1)} %get-tuple-element.109), channel_id=1, source_target_pairs={{0,1},{1,0},{2,3},{3,2},{4,5},{5,4},{6,7},{7,6},{8,9},{9,8},{10,11... | collective-permute-start | bytes 5898248 | tf_op jit(solution)/shard_map/ppermute | solution.py:445
  588.5 49.3 %collective-permute-start.4 = (bf16[21504,128]{1,0:T(8,128)(2,1)}, bf16[21504,128]{1,0:T(8,128)(2,1)}, u32[]{:S(2)}, u32[]{:S(2)}) collective-permute-start(bf16[21504,128]{1,0:T(8,128)(2,1)} %bitcast.16), channel_id=1, source_target_pairs={{0,1},{1,0},{2,3},{3,2},{4,5},{5,4},{6,7},{7,6},{8,9},{9,8},{10,11... | collective-permute-start | bytes 16515080 | tf_op jit(solution)/shard_map/ppermute | solution.py:445
  633.1 4.7 collective-permute-start.2
  684.7 8.1 %collective-permute-start.5 = (bf16[7680,128]{1,0:T(8,128)(2,1)S(1)}, bf16[7680,128]{1,0:T(8,128)(2,1)}, u32[]{:S(2)}, u32[]{:S(2)}) collective-permute-start(bf16[7680,128]{1,0:T(8,128)(2,1)S(1)} %bitcast.30), channel_id=1, source_target_pairs={{0,1},{1,0},{2,3},{3,2},{4,5},{5,4},{6,7},{7,6},{8,9},{9,8},{10,11... | collective-permute-start | bytes 5898248 | tf_op jit(solution)/shard_map/ppermute | solution.py:445

commit v2 on v1

--- a/solution.py
+++ b/solution.py
@@ -20,6 +20,7 @@
 EPS = 1e-5
 LOG2E = 1.4426950408889634
 LOW = -1e30
+SMALL = 60.0
 F32 = jnp.float32
 BF16 = jnp.bfloat16
 
@@ -308,55 +309,40 @@
     )(info, *small, *arrays)
 
 
-EARLY = 21504
 LATE = 7680
 CORE = 5
 
 
 def grads_kernel(info, small, ins, outs):
-    mid_one, dh_one, mid_two, dh_two, act_one, dz_one, act_two, dz_two, att_one, dy_one, att_two, dy_two = ins
-    core = info[CORE]
+    dh_one, mid_one, dh_two, mid_two, act_one, dz_one, act_two, dz_two, att_one, dy_one, att_two, dy_two = ins
+    up, down, out = outs
 
     def left(one, two):
         return jnp.concatenate([one, two], axis=0).T
 
-    def put(half, row, rows, value):
-        for to, out in enumerate(outs):
-
-            @pl.when((half ^ core) == to)
-            def _():
-                for i in range(value.shape[1] // 128):
-                    out[pl.ds(row + i * rows, value.shape[0]), :] = value[:, 128 * i : 128 * i + 128]
-
     mid = left(mid_one[...], mid_two[...])
     dh_one.ready(), dh_two.ready()
 
-    def up(c, _):
+    def step_up(c, _):
         here = pl.ds(pl.multiple_of(c * 512, 512), 512)
-        right = jnp.concatenate([dh_one[:, here], dh_two[:, here]], axis=0)
-        result = dot(mid, right).astype(BF16)
-        row = pl.multiple_of(c * 1536, 512)
-        put(0, row, 384, result[:384])
-        put(1, row, 384, result[384:])
+        up[:, here] = dot(mid, jnp.concatenate([dh_one[:, here], dh_two[:, here]], axis=0)).astype(BF16)
         return 0
 
-    lax.fori_loop(0, 6, up, 0)
+    lax.fori_loop(0, 6, step_up, 0)
+    up.flush()
     dz = jnp.concatenate([dz_one[...], dz_two[...]], axis=0)
     act_one.ready(), act_two.ready()
 
-    def down(c, _):
+    def step_down(c, _):
         here = pl.ds(pl.multiple_of(c * 512, 512), 512)
-        result = dot(left(act_one[:, here], act_two[:, here]), dz).astype(BF16)
-        put(c // 3, pl.multiple_of(9216 + (c % 3) * 512, 512), 1536, result)
+        down[here, :] = dot(left(act_one[:, here], act_two[:, here]), dz).astype(BF16)
         return 0
 
-    lax.fori_loop(0, 6, down, 0)
+    lax.fori_loop(0, 6, step_down, 0)
+    down.flush()
     dy = jnp.concatenate([dy_one[...], dy_two[...]], axis=0)
-    result = dot(left(att_one[...], att_two[...]), dy).astype(BF16)
-    put(0, 18432, 384, result[:384])
-    put(1, 18432, 384, result[384:])
-    for out in outs:
-        out[20736:20784, :] = small[...].astype(BF16)
+    out[0:WIDTH, :] = dot(left(att_one[...], att_two[...]), dy).astype(BF16)
+    out[WIDTH:, :] = small[...].astype(BF16)
 
 
 def grad_qkv_kernel(info, ins, outs):
@@ -454,18 +440,12 @@
     return (mine.astype(F32) + swap(other, 1).astype(F32)).astype(BF16)
 
 
-def deal(half):
-    return exchange(half.reshape(SEQ, half.shape[0] // SEQ, 128))
-
-
-def sum_chips(blocks):
-    block = jnp.sum(blocks.astype(F32), axis=0).astype(BF16)
-    return (block.astype(F32) + swap(block, 2).astype(F32)).astype(BF16)
-
-
-def spread(block):
-    whole = exchange(jnp.broadcast_to(block[None], (SEQ, *block.shape))).reshape(-1, 128)
-    return whole, swap(whole, 1)
+CHIPS = 64
+
+
+def across_chips(slots):
+    groups = [[s * 4 + z * 2 + c for s in range(SEQ) for z in range(2)] for c in range(2)]
+    return lax.all_to_all(slots, ("seq", "batch"), 0, 0, axis_index_groups=groups)
 
 
 def positions(half, first_row, count):
@@ -512,17 +492,38 @@
 
         third = third_keys(recv, tile_rows)
 
-        def one_tile(t, _):
+        def square_top(features):
+            wide = features.astype(F32)
+            return jnp.max(jnp.sum(wide * wide, axis=0, keepdims=True))
+
+        key_top = jnp.float32(0.0)
+        query_top = jnp.float32(0.0)
+        for c in range(8):
+            key_top = jnp.maximum(key_top, square_top(kv_t[0:64, 1024 * c : 1024 * c + 1024]))
+        for c in range(4):
+            query_top = jnp.maximum(query_top, square_top(q_t[0:64, 1024 * c : 1024 * c + 1024]))
+        small = key_top * query_top < (SMALL / LOG2E) ** 2
+
+        def one_tile(t, shifted):
             start = t * span
             columns = pl.ds(pl.multiple_of(t * tile_rows, tile_rows), tile_rows)
             at = positions(half, start, tile_rows)
             first = first_keys(at, second, third)
-            top[...] = jnp.full((1, tile_rows), LOW, F32)
+            top[...] = jnp.full((1, tile_rows), LOW if shifted else 0.0, F32)
             acc[...] = jnp.zeros((80, tile_rows), F32)
             queries = q_t[:, columns]
 
-            def update(scores, key_rows, left):
+            def update(kv, key_rows, left, mask):
                 here = slice(left, tile_rows)
+                scores = dot(kv, queries[:, here]) * LOG2E
+                if not shifted:
+                    weights = jnp.exp2(scores)
+                    if mask is not None:
+                        weights = jnp.where(mask, weights, 0.0)
+                    acc[:, here] = acc[:, here] + dot(kv_t[64:144, key_rows], weights.astype(BF16))
+                    return
+                if mask is not None:
+                    scores = jnp.where(mask, scores, LOW)
                 old_top = top[:, here]
                 new_top = jnp.maximum(old_top, jnp.max(scores, axis=0, keepdims=True))
                 weights = jnp.exp2(scores - new_top).astype(BF16)
@@ -533,11 +534,10 @@
             def whole(j, masked):
                 key_start = pl.multiple_of(j * 1024, 1024)
                 kv = recv[pl.ds(j * 4, 4), 0:ROWS, :].reshape(1024, 128)
-                scores = dot(kv, queries) * LOG2E
+                mask = None
                 if masked:
-                    key_at = lax.broadcasted_iota(jnp.int32, (1024, 1), 0)
-                    scores = jnp.where(key_at >= second, scores, LOW)
-                update(scores, pl.ds(key_start, 1024), 0)
+                    mask = lax.broadcasted_iota(jnp.int32, (1024, 1), 0) >= second
+                update(kv, pl.ds(key_start, 1024), 0, mask)
 
             @pl.when(t > 0)
             def _():
@@ -549,16 +549,15 @@
 
             lax.fori_loop(1, t * (span // 1024), step, 0)
             fresh = first >= start
-            top[...] = jnp.where(fresh, LOW, top[...])
+            top[...] = jnp.where(fresh, LOW if shifted else 0.0, top[...])
             acc[...] = jnp.where(fresh, 0.0, acc[...])
             for i in range(devs // 2):
                 left = 256 * i
                 key_start = pl.multiple_of(start + 512 * i, 512)
                 kv = recv[pl.ds(t * devs + 2 * i, 2), 0:ROWS, :].reshape(512, 128)
-                scores = dot(kv, queries[:, left:]) * LOG2E
                 key_at = key_start + lax.broadcasted_iota(jnp.int32, (512, 1), 0)
                 allowed = (key_at >= first[:, left:]) & (key_at <= at[:, left:])
-                update(jnp.where(allowed, scores, LOW), pl.ds(key_start, 512), left)
+                update(kv, pl.ds(key_start, 512), left, allowed)
             total = acc[64:65, :]
             result = acc[0:64, :] / total
             out_f[:, columns] = result
@@ -566,9 +565,17 @@
             low = result.astype(BF16)
             for i in range(devs):
                 out_low[t * devs + i] = low[:, i * HALF : (i + 1) * HALF]
-            return 0
-
-        lax.fori_loop(0, SEQ // devs, one_tile, 0)
+
+        for shifted in (False, True):
+
+            @pl.when(small != shifted)
+            def _():
+                def tile(t, _):
+                    one_tile(t, shifted)
+                    return 0
+
+                lax.fori_loop(0, SEQ // devs, tile, 0)
+
         for one in kept[2:]:
             one.flush()
         for one in kept:
@@ -814,24 +821,22 @@
     )
     back = exchange(slots)
     small = jnp.concatenate(
-        [grad_table[:PASSES], gain_a_two, gain_m_one + gain_m_two, jnp.zeros((1, WIDTH), F32)]
-    ).reshape(48, 128)
+        [grad_table[:PASSES], gain_a_two, gain_m_one + gain_m_two, jnp.zeros((9, WIDTH), F32)]
+    )
     early = in_vmem(
         grads_kernel,
         "grads",
         info,
         (small,),
-        (midn_one, dh_one, midn_two, dh_two, act_one, dz_one, act_two, cotangent[0], att_one, dy_one, att_two, dy_two),
-        (shape(EARLY, 128),) * 2,
+        (dh_one, midn_one, dh_two, midn_two, act_one, dz_one, act_two, cotangent[0], att_one, dy_one, att_two, dy_two),
+        (shape(WIDTH, FF), shape(FF, WIDTH), shape(WIDTH + 16, WIDTH)),
         [],
         5.4e10,
     )
-    early = sum_cores(early)
     back, early = lax.optimization_barrier((back, early))
+    early = lax.psum(early, ("seq", "batch"))
     sent_one = attend_back(info, *saved_one[1:], back)
-    sent_one, early = lax.optimization_barrier((sent_one, deal(early)))
     recv = exchange(sent_one)
-    early = sum_chips(early)
     grad_tokens, dproj_one, gain_a_one = in_vmem(
         leave_kernel,
         "leave",
@@ -862,21 +867,21 @@
         [],
         9e8,
     )
-    core = info[CORE : CORE + 1]
-    early = spread(early)
-    grad_down = widen(core, *early, 6, 1536, 6)
-    grad_up = widen(core, *early, 24, 384, 0)
-    grad_out = widen(core, *early, 6, 384, 48)
-    late = sum_chips(deal(sum_cores(late)))
-    late, grad_down, grad_up, grad_out = lax.optimization_barrier((late, grad_down, grad_up, grad_out))
-    late = spread(late)
-    tail = early[0][20736:20784].reshape(8, WIDTH).astype(F32)
+    late, early = lax.optimization_barrier((late, early))
+    late = across_chips(sum_cores(late).reshape(CHIPS, -1, 128))
+    early = tuple(x.astype(F32) for x in early)
+    late, early = lax.optimization_barrier((late, early))
+    late = jnp.sum(late.astype(F32), axis=0).astype(BF16)
+    whole = across_chips(jnp.broadcast_to(late[None], (CHIPS, *late.shape))).reshape(-1, 128)
+    late = (whole, swap(whole, 1))
+    grad_up, grad_down, grad_out = early
+    tail = grad_out[WIDTH : WIDTH + 8]
     gain_a_sum = late[0][6912:6918].reshape(WIDTH).astype(F32)
     return (
         mixed[None],
         grad_tokens[None],
-        widen(core, *late, 18, 384, 0),
-        grad_out,
+        widen(info[CORE : CORE + 1], *late, 18, 384, 0),
+        grad_out[:WIDTH],
         grad_up,
         grad_down,
         tail[PASSES] + gain_a_sum,

time: 708 us -> 649 us (0.917)
  blocking collectives: 174 us -> 139 us
  Pallas kernels: 298 us -> 265 us
  starting transfers between devices: 61.9 us -> 36.5 us
  waiting for transfers between devices: 131 us -> 150 us
  between operations: 2.73 us -> 16.1 us
    psum x0 -> x1, waiting for transfers between devices: none -> 74.3 us  [on_device(): early = lax.psum(early, ('seq', 'batch'))]
    all_to_all x6 -> x4, blocking collectives: 174 us -> 107 us  [exchange(): return lax.all_to_all(slots, 'seq', 0, 0)]
    ppermute x6 -> x2, waiting for transfers between devices: 38.8 us -> 4.04 us  [swap(): return lax.ppermute(value, 'batch', [(i, i ^ bit) for i in range(4)])]
    all_to_all x6 -> x4, waiting for transfers between devices: 91.8 us -> 58 us  [exchange(): return lax.all_to_all(slots, 'seq', 0, 0)]
    all_to_all x0 -> x1, blocking collectives: none -> 31.7 us  [across_chips(): lax.all_to_all(slots, ('seq', 'batch'), 0, 0, axis_index_groups=groups)]
    pallas_call x4 -> x1, Pallas kernels: 24.7 us -> 3.9 us  [widen(): pl.pallas_call(widen_kernel, out_shape=shape(2 * height, columns * 128, d...]
    all_to_all x6 -> x4, starting transfers between devices: 42.9 us -> 25.8 us  [exchange(): return lax.all_to_all(slots, 'seq', 0, 0)]
    ppermute x6 -> x2, starting transfers between devices: 19 us -> 3.05 us  [swap(): return lax.ppermute(value, 'batch', [(i, i ^ bit) for i in range(4)])]
  transfers between devices with their start and end apart: 12 -> 8, of which waited for: 8 -> 7; matrix products, arithmetic and copies ran while one was open for 3% -> 3% of each run, Pallas kernels for 11% -> 14%
where the time goes in v2:
time: 649 us; the launch traced here: 642 us
  Pallas kernels  265 us (41%)
  waiting for transfers between devices  150 us (23%)
  blocking collectives  139 us (21%)
  starting transfers between devices  36.5 us (6%)
  other arithmetic  22.8 us (4%)
  between operations  16.1 us (2%)
  local copies, waits for them, and re-layouts  12.7 us (2%)
    pallas_call x2, Pallas kernels, attend_back(): pl.pallas_call(functools.partial(attend_back_kernel, devs=devs), out_shap...  112 us
    all_to_all x4, blocking collectives, exchange(): return lax.all_to_all(slots, 'seq', 0, 0)  107 us
    pallas_call x8, Pallas kernels, in_vmem(): pl.pallas_call(body, out_shape=tuple(outs), in_specs=[pl.BlockSpec(memory...  89.7 us
    psum x1, waiting for transfers between devices, on_device(): early = lax.psum(early, ('seq', 'batch'))  74.3 us
    pallas_call x2, Pallas kernels, attend(): pl.pallas_call(functools.partial(attend_kernel, devs=devs), out_shape=(ja...  59.7 us
    all_to_all x4, waiting for transfers between devices, exchange(): return lax.all_to_all(slots, 'seq', 0, 0)  58 us
    all_to_all x1, blocking collectives, across_chips(): lax.all_to_all(slots, ('seq', 'batch'), 0, 0, axis_index_groups=groups)  31.7 us
    all_to_all x4, starting transfers between devices, exchange(): return lax.all_to_all(slots, 'seq', 0, 0)  25.8 us
  transfers between devices with their start and end apart: 8, of which 7 were waited for; matrix products, arithmetic and copies ran while one was open for 3% of the time, Pallas kernels for 14%

profile of v2, /device:TPU:1, one launch (start us, length us, event | category | flops | bytes accessed | tf_op | source)
XLA Modules:
  0.0 642.3 jit_solution(2209792105365667012)
XLA Ops:
  11.7 6.6 %enter.1 = (bf16[32,336,128]{2,1,0:T(8,128)(2,1)}, bf16[256,768]{1,0:T(8,128)(2,1)}) custom-call(s32[6]{0:T(128)} %stack.31.info, f32[1,768]{1,0:T(1,128)} %broadcast_in_dim.22.refs_0_.refs_2_.refs_1_, bf16[256,768]{1,0:T(8,128)(2,1)} %bitcast.30, bf16[768,2304]{1,0:T(8,128)(2,1)} %refs_2_.3), custom_call_target="tpu_custom_call" | custom-call | flops 1000000000 | bytes 16777216 | tf_op jit(solution)/shard_map/enter/pallas_call | solution.py:298
  18.3 43.0 %all_to_all.50.recv_far = bf16[32,336,128]{2,1,0:T(8,128)(2,1)} all-to-all(bf16[32,336,128]{2,1,0:T(8,128)(2,1)} %get-tuple-element.68), channel_id=1, replica_groups=mesh['seq'=32,'batch'=4] {'seq'}, dimensions={0} | all-to-all | bytes 5505024 | tf_op jit(solution)/shard_map/all_to_all | solution.py:435
  61.3 29.9 %attend.2 = (bf16[32,64,128]{2,1,0:T(8,128)(2,1)}, f32[64,4096]{1,0:T(8,128)}, f32[1,4096]{1,0:T(1,128)}, bf16[144,8192]{1,0:T(8,128)(2,1)}, bf16[128,4096]{1,0:T(8,128)(2,1)}) custom-call(s32[6]{0:T(128)} %stack.31.info, bf16[32,336,128]{2,1,0:T(8,128)(2,1)} %all_to_all.50.recv_far), custom_call_target="tpu_custom_call" | custom-call | flops 18227200000 | bytes 8388608 | tf_op jit(solution)/shard_map/attend/pallas_call | solution.py:588
  91.3 4.3 all-to-all-start.1
  97.6 7.5 %all-to-all-done.1.refs_4_ = bf16[32,64,128]{2,1,0:T(8,128)(2,1)S(1)} async-done(((bf16[32,64,128]{2,1,0:T(8,128)(2,1)}), bf16[32,64,128]{2,1,0:T(8,128)(2,1)S(1)}, u32[]{:S(2)}, u32[]{:S(2)}) %all-to-all-start.1) | async-done | bytes 524320 | tf_op jit(solution)/shard_map/all_to_all | solution.py:435
  105.9 14.2 %turn.1 = (bf16[32,336,128]{2,1,0:T(8,128)(2,1)}, bf16[256,768]{1,0:T(8,128)(2,1)}, f32[256,768]{1,0:T(8,128)}, bf16[256,768]{1,0:T(8,128)(2,1)}, f32[256,768]{1...) custom-call(s32[6]{0:T(128)} %stack.31.info, s32[256,1]{1,0:T(8,128)} %copy.21.refs_0_, ...), custom_call_target="tpu_custom_call" | custom-call | flops 3600000000 | bytes 16777216 | tf_op jit(solution)/shard_map/turn/pallas_call | solution.py:298
  120.1 36.6 %all_to_all.51.recv_far = bf16[32,336,128]{2,1,0:T(8,128)(2,1)} all-to-all(bf16[32,336,128]{2,1,0:T(8,128)(2,1)} %get-tuple-element.70), channel_id=1, replica_groups=mesh['seq'=32,'batch'=4] {'seq'}, dimensions={0} | all-to-all | bytes 5505024 | tf_op jit(solution)/shard_map/all_to_all | solution.py:435
  156.6 29.8 %attend.3 = (bf16[32,64,128]{2,1,0:T(8,128)(2,1)}, f32[64,4096]{1,0:T(8,128)}, f32[1,4096]{1,0:T(1,128)}, bf16[144,8192]{1,0:T(8,128)(2,1)}, bf16[128,4096]{1,0:T(8,128)(2,1)}) custom-call(s32[6]{0:T(128)} %stack.31.info, bf16[32,336,128]{2,1,0:T(8,128)(2,1)} %all_to_all.51.recv_far), custom_call_target="tpu_custom_call" | custom-call | flops 18227200000 | bytes 8388608 | tf_op jit(solution)/shard_map/attend/pallas_call | solution.py:588
  186.4 14.0 %all_to_all.52.refs_1_ = bf16[32,64,128]{2,1,0:T(8,128)(2,1)} all-to-all(bf16[32,64,128]{2,1,0:T(8,128)(2,1)} %get-tuple-element.71), channel_id=1, replica_groups=mesh['seq'=32,'batch'=4] {'seq'}, dimensions={0} | all-to-all | bytes 1048576 | tf_op jit(solution)/shard_map/all_to_all | solution.py:435
  200.4 17.0 %crest.1 = (bf16[32,64,128]{2,1,0:T(8,128)(2,1)}, bf16[256,768]{1,0:T(8,128)(2,1)}, bf16[256,768]{1,0:T(8,128)(2,1)}, bf16[256,768]{1,0:T(8,128)(2,1)}, bf16[256...) custom-call(s32[6]{0:T(128)} %stack.31.info, ...), custom_call_target="tpu_custom_call" | custom-call | flops 5000000000 | bytes 16777216 | tf_op jit(solution)/shard_map/crest/pallas_call | solution.py:298
  217.5 13.6 %all_to_all.53.grad_out_far = bf16[32,64,128]{2,1,0:T(8,128)(2,1)} all-to-all(bf16[32,64,128]{2,1,0:T(8,128)(2,1)} %get-tuple-element.82), channel_id=1, replica_groups=mesh['seq'=32,'batch'=4] {'seq'}, dimensions={0} | all-to-all | bytes 1048576 | tf_op jit(solution)/shard_map/all_to_all | solution.py:435
  231.1 55.8 %attend_back.2 = bf16[32,320,128]{2,1,0:T(8,128)(2,1)} custom-call(s32[6]{0:T(128)} %stack.31.info, bf16[32,336,128]{2,1,0:T(8,128)(2,1)} %all_to_all.51.recv_far, bf16[144,8192]{1,0:T(8,128)(2,1)} %get-tuple-element.78.kv_t_far, bf16[128,4096]{1,0:T(8,128)(2,1)} %get-tuple-element.79.q_t_far, f32[64,4096]{1,0:T(8,128)} %get-tuple-element.80.out_f_far, ...), custom_call_target="tpu_custom_call" | custom-call | flops 18227200000 | bytes 8388608 | tf_op jit(solution)/shard_map/attend_back/pallas_call | solution.py:711
  286.9 4.3 all-to-all-start.5
  291.3 27.8 %all-to-all-done.5.refs_3_ = bf16[32,320,128]{2,1,0:T(8,128)(2,1)S(1)} async-done(((bf16[32,320,128]{2,1,0:T(8,128)(2,1)}), bf16[32,320,128]{2,1,0:T(8,128)(2,1)S(1)}, u32[]{:S(2)}, u32[]{:S(2)}) %all-to-all-start.5) | async-done | bytes 2621472 | tf_op jit(solution)/shard_map/all_to_all | solution.py:435
  320.6 15.6 %return.1 = (bf16[32,64,128]{2,1,0:T(8,128)(2,1)}, bf16[256,2304]{1,0:T(8,128)(2,1)}, f32[1,768]{1,0:T(1,128)}, f32[8,768]{1,0:T(8,128)}, bf16[256,768]{1,0:T(8,...) custom-call(s32[6]{0:T(128)} %stack.31.info, ...), custom_call_target="tpu_custom_call" | custom-call | flops 5000000000 | bytes 16777216 | tf_op jit(solution)/shard_map/return/pallas_call | solution.py:298
  336.2 9.2 %all-to-all-start.6 = ((bf16[32,64,128]{2,1,0:T(8,128)(2,1)}), bf16[32,64,128]{2,1,0:T(8,128)(2,1)S(1)}, u32[]{:S(2)}, u32[]{:S(2)}) async-start(bf16[32,64,128]{2,1,0:T(8,128)(2,1)} %get-tuple-element.86), calls=%async_computation.6 | async-start | bytes 1048576 | tf_op jit(solution)/shard_map/all_to_all | solution.py:435
  347.6 13.4 %grads.1 = (bf16[768,3072]{1,0:T(8,128)(2,1)}, bf16[3072,768]{1,0:T(8,128)(2,1)}, bf16[784,768]{1,0:T(8,128)(2,1)}) custom-call(s32[6]{0:T(128)} %stack.31.info, f32[16,768]{1,0:T(8,128)} %maximum_maximum_fusion.refs_0_, bf16[256,3072]{1,0:T(8,128)(2,1)} %get-tuple-element.91.refs_1_, bf16[256,768]{1,0:T(8,128)(2,1)} %get-tuple-element.92.refs_2_, ...), custom_call_target="tpu_custom_call" | custom-call | flops 54000001024 | bytes 16777216 | tf_op jit(solution)/shard_map/grads/pallas_call | solution.py:298
  361.7 55.8 %attend_back.3 = bf16[32,320,128]{2,1,0:T(8,128)(2,1)} custom-call(s32[6]{0:T(128)} %stack.31.info, bf16[32,336,128]{2,1,0:T(8,128)(2,1)} %all_to_all.50.recv_far, bf16[144,8192]{1,0:T(8,128)(2,1)} %get-tuple-element.74.kv_t_far, bf16[128,4096]{1,0:T(8,128)(2,1)} %get-tuple-element.75.q_t_far, f32[64,4096]{1,0:T(8,128)} %get-tuple-element.76.out_f_far, ...), custom_call_target="tpu_custom_call" | custom-call | flops 18227200000 | bytes 8388608 | tf_op jit(solution)/shard_map/attend_back/pallas_call | solution.py:711
  417.5 8.0 %all-to-all-start.7 = ((bf16[32,320,128]{2,1,0:T(8,128)(2,1)}), bf16[32,320,128]{2,1,0:T(8,128)(2,1)S(1)}, u32[]{:S(2)}, u32[]{:S(2)}) async-start(bf16[32,320,128]{2,1,0:T(8,128)(2,1)} %attend_back.3), calls=%async_computation.7 | async-start | bytes 5242880 | tf_op jit(solution)/shard_map/all_to_all | solution.py:435
  425.5 7.3 %grad_qkv_two.1.refs_3_ = f32[18,768,128]{2,1,0:T(8,128)} custom-call(s32[6]{0:T(128)} %stack.31.info, bf16[256,768]{1,0:T(8,128)(2,1)} %get-tuple-element.111.refs_0_, bf16[256,2304]{1,0:T(8,128)(2,1)} %get-tuple-element.112.refs_1_), custom_call_target="tpu_custom_call" | custom-call | flops 900000000 | bytes 16777216 | tf_op jit(solution)/shard_map/grad_qkv_two/pallas_call | solution.py:298
  432.8 22.7 %all-to-all-done.7.refs_1_ = bf16[32,320,128]{2,1,0:T(8,128)(2,1)S(1)} async-done(((bf16[32,320,128]{2,1,0:T(8,128)(2,1)}), bf16[32,320,128]{2,1,0:T(8,128)(2,1)S(1)}, u32[]{:S(2)}, u32[]{:S(2)}) %all-to-all-start.7) | async-done | bytes 2621472 | tf_op jit(solution)/shard_map/all_to_all | solution.py:435
  456.9 6.6 %leave.1 = (f32[256,768]{1,0:T(8,128)}, bf16[256,2304]{1,0:T(8,128)(2,1)}, f32[1,768]{1,0:T(1,128)}) custom-call(s32[6]{0:T(128)} %stack.31.info, f32[1,768]{1,0:T(1,128)} %broadcast_in_dim.22.refs_0_.refs_2_.refs_1_, bf16[32,320,128]{2,1,0:T(8,128)(2,1)} %copy-done, bf16[768,2304]{1,0:T(8,128)(2,1)} %refs_2_.3, bf16[256,768]{1,0:T(8,128)(2,1)} %bitcast.32, ...), custom_call_target="tpu_custom_call" | custom-call | flops 1000000000 | bytes 16777216 | tf_op jit(solution)/shard_map/leave/pallas_call | solution.py:298
  464.8 9.1 %grad_qkv.1 = (bf16[7680,128]{1,0:T(8,128)(2,1)}, bf16[7680,128]{1,0:T(8,128)(2,1)}) custom-call(s32[6]{0:T(128)} %stack.31.info, f32[16,128]{1,0:T(8,128)} %pad.9.refs_0_, bf16[256,768]{1,0:T(8,128)(2,1)} %get-tuple-element.109.refs_1_, bf16[256,2304]{1,0:T(8,128)(2,1)} %get-tuple-element.110.refs_2_, f32[18,768,128]{2,1,0:T(8,128)} %grad_qkv_two.1.refs_3_), custom_call_target="tpu_custom_call" | custom-call | flops 900000000 | bytes 16777216 | tf_op jit(solution)/shard_map/grad_qkv/pallas_call | solution.py:298
  474.0 74.3 %all-reduce.5.cloned.1.call-done = (bf16[768,3072]{1,0:T(8,128)(2,1)}, bf16[3072,768]{1,0:T(8,128)(2,1)}, bf16[784,768]{1,0:T(8,128)(2,1)}) async-done(((bf16[768,3072]{1,0:T(8,128)(2,1)}, bf16[3072,768]{1,0:T(8,128)(2,1)}, bf16[784,768]{1,0:T(8,128)(2,1)}), (bf16[768,3072]{1,0:T(8,128)(2,1)}, bf16[3072,768]{1,0:T(8,128)(2,1)}, bf16[784,768]{1,0:T(8,128)(2,1)})) %all-reduce.5.cloned.1.call-update) | async-done | bytes 10641424 | tf_op jit(solution)/shard_map/psum | solution.py:837
  549.0 3.8 collective-permute-done
  552.8 3.3 add_convert_fusion
  556.1 7.6 %all-to-all-start.8 = ((bf16[64,120,128]{2,1,0:T(8,128)(2,1)}), bf16[64,120,128]{2,1,0:T(8,128)(2,1)}, u32[]{:S(2)}, u32[]{:S(2)}) async-start(bf16[64,120,128]{2,1,0:T(8,128)(2,1)} %bitcast.13), calls=%async_computation.8 | async-start | bytes 3932160 | tf_op jit(solution)/shard_map/all_to_all | solution.py:448
  565.4 7.4 %convert_element_type.34 = f32[768,3072]{1,0:T(8,128)} convert(bf16[768,3072]{1,0:T(8,128)(2,1)} %get-tuple-element.120) | non-fusion elementwise | flops 2359296 | bytes 14155776 | tf_op jit(solution)/shard_map/convert_element_type | solution.py:872
  572.8 4.5 convert_element_type.35
  577.3 14.1 %all-to-all-done.8 = bf16[64,120,128]{2,1,0:T(8,128)(2,1)} async-done(((bf16[64,120,128]{2,1,0:T(8,128)(2,1)}), bf16[64,120,128]{2,1,0:T(8,128)(2,1)}, u32[]{:S(2)}, u32[]{:S(2)}) %all-to-all-start.8) | async-done | bytes 1966112 | tf_op jit(solution)/shard_map/all_to_all | solution.py:448
  593.5 31.7 %all_to_all.54 = bf16[64,120,128]{2,1,0:T(8,128)(2,1)S(1)} all-to-all(bf16[64,120,128]{2,1,0:T(8,128)(2,1)S(1)} %broadcast_in_dim.26), channel_id=1, replica_groups={{0,2,4,6,8,10,12,14,16,18,20,22,24,26,28,30,32,34,36,38,40,42,44,46,48,..., dimensions={0} | all-to-all | bytes 3932160 | tf_op jit(solution)/shard_map/all_to_all | solution.py:448
  631.1 3.9 widen.1
  (47 shorter events, 23.6 us)
Async XLA Ops:
  61.3 34.3 %copy-start.6 = (f32[768]{0:T(1024)S(1)}, f32[768]{0:T(1024)}, u32[]{:S(2)}) copy-start(f32[768]{0:T(1024)} %param.21) | copy-start | bytes 9220
  61.3 34.9 %copy-start.5 = (s32[1,256]{1,0:T(1,128)S(1)}, s32[1,256]{1,0:T(1,128)}, u32[]{:S(2)}) copy-start(s32[1,256]{1,0:T(1,128)} %param.14) | copy-start | bytes 3076
  61.3 35.7 %copy-start.4 = (f32[5,768]{1,0:T(8,128)S(1)}, f32[5,768]{1,0:T(8,128)}, u32[]{:S(2)}) copy-start(f32[5,768]{1,0:T(8,128)} %param.22) | copy-start | bytes 46084
  91.3 13.8 %all-to-all-start.1 = ((bf16[32,64,128]{2,1,0:T(8,128)(2,1)}), bf16[32,64,128]{2,1,0:T(8,128)(2,1)S(1)}, u32[]{:S(2)}, u32[]{:S(2)}) async-start(bf16[32,64,128]{2,1,0:T(8,128)(2,1)} %get-tuple-element.69), calls=%async_computation.1 | async-start | bytes 1048576 | tf_op jit(solution)/shard_map/all_to_all | solution.py:435
  105.1 0.8 copy-start.2
  286.9 32.2 %all-to-all-start.5 = ((bf16[32,320,128]{2,1,0:T(8,128)(2,1)}), bf16[32,320,128]{2,1,0:T(8,128)(2,1)S(1)}, u32[]{:S(2)}, u32[]{:S(2)}) async-start(bf16[32,320,128]{2,1,0:T(8,128)(2,1)} %attend_back.2), calls=%async_computation.5 | async-start | bytes 5242880 | tf_op jit(solution)/shard_map/all_to_all | solution.py:435
  319.1 1.5 copy-start.1
  320.6 24.8 %copy-start.7 = (f32[1,768]{1,0:T(1,128)S(1)}, f32[1,768]{1,0:T(1,128)}, u32[]{:S(2)}) copy-start(f32[1,768]{1,0:T(1,128)} %get-tuple-element.90) | copy-start | bytes 9220
  336.2 24.8 %all-to-all-start.6 = ((bf16[32,64,128]{2,1,0:T(8,128)(2,1)}), bf16[32,64,128]{2,1,0:T(8,128)(2,1)S(1)}, u32[]{:S(2)}, u32[]{:S(2)}) async-start(bf16[32,64,128]{2,1,0:T(8,128)(2,1)} %get-tuple-element.86), calls=%async_computation.6 | async-start | bytes 1048576 | tf_op jit(solution)/shard_map/all_to_all | solution.py:435
  345.4 202.9 %all-reduce.5.cloned.1.call-start = ((), (), s32[]{:S(2)}) async-start(), calls=%async_computation.10 | async-start | bytes 21282816 | tf_op jit(solution)/shard_map/psum | solution.py:837
  360.9 0.8 copy-start.3
  417.5 38.0 %all-to-all-start.7 = ((bf16[32,320,128]{2,1,0:T(8,128)(2,1)}), bf16[32,320,128]{2,1,0:T(8,128)(2,1)S(1)}, u32[]{:S(2)}, u32[]{:S(2)}) async-start(bf16[32,320,128]{2,1,0:T(8,128)(2,1)} %attend_back.3), calls=%async_computation.7 | async-start | bytes 5242880 | tf_op jit(solution)/shard_map/all_to_all | solution.py:435
  455.5 1.5 copy-start
  548.3 4.5 collective-permute-start
  556.1 35.3 %all-to-all-start.8 = ((bf16[64,120,128]{2,1,0:T(8,128)(2,1)}), bf16[64,120,128]{2,1,0:T(8,128)(2,1)}, u32[]{:S(2)}, u32[]{:S(2)}) async-start(bf16[64,120,128]{2,1,0:T(8,128)(2,1)} %bitcast.13), calls=%async_computation.8 | async-start | bytes 3932160 | tf_op jit(solution)/shard_map/all_to_all | solution.py:448
  563.7 9.1 %slice-start = ((s8[4718592]{0:T(1024)(128)(4,1)}), s8[4194304]{0:T(1024)(128)(4,1)S(1)}, s32[]{:S(2)}) async-start(s8[4718592]{0:T(1024)(128)(4,1)} %bitcast.28), calls=%async_computation.11 | async-start | bytes 8388608
  565.3 7.4 %slice-start.1 = ((s8[4718592]{0:T(1024)(128)(4,1)}), s8[524288]{0:T(1024)(128)(4,1)S(1)}, s32[]{:S(2)}) async-start(s8[4718592]{0:T(1024)(128)(4,1)} %bitcast.28), calls=%async_computation.12 | async-start | bytes 1048576
  625.2 5.9 collective-permute-start.1
Sparse Core Ops, SparseCore 0:
  361.1 187.1 all-reduce.4

commit v3 on v2

--- a/solution.py
+++ b/solution.py
@@ -89,6 +89,28 @@
 
     def __getitem__(self, at):
         return self.ready()[at]
+
+
+class HeldBlocks:
+    def __init__(self, source, target, sems, axis):
+        self.source, self.target, self.sems, self.axis = source, target, sems, axis
+        self.waited = False
+
+    def copy(self, c):
+        here = pl.ds(c * FF_BLOCK if isinstance(c, int) else pl.multiple_of(c * FF_BLOCK, FF_BLOCK), FF_BLOCK)
+        at = (here, slice(None)) if self.axis == 0 else (slice(None), here)
+        return pltpu.make_async_copy(self.source.at[at], self.target.at[at], self.sems.at[c])
+
+    def wait(self, c):
+        if not self.waited:
+            self.copy(c).wait()
+
+    def ready(self):
+        assert self.waited
+        return self.target
+
+    def __getitem__(self, at):
+        return self.target[at]
 
 
 class Kept:
@@ -160,10 +182,12 @@
     mid_out[...] = mid
     normed_out[...] = (standardise(mid)[0] * gain).astype(BF16)
     acc[...] = mid
-    up, down = weights[1].ready(), weights[2].ready()
+    up, down = weights[1:]
 
     def step(c, _):
         here = pl.ds(pl.multiple_of(c * FF_BLOCK, FF_BLOCK), FF_BLOCK)
+        up.wait(c)
+        down.wait(c)
         hidden = dot(normed_out[...], up[:, here])
         hidden_out[:, here] = hidden
         active = gelu(hidden).astype(BF16)
@@ -172,16 +196,18 @@
         return 0
 
     lax.fori_loop(0, FF // FF_BLOCK, step, 0)
+    up.waited = down.waited = True
 
 
 def mix_back(grad, odd, gain, mid, hidden, weights, acc, dz_out, dh_out, dy_out, dmid_out, gain_out, slots):
     out, up, down = weights
-    up, down = up.ready(), down.ready()
     dz_out[...] = grad.astype(BF16)
     acc[...] = jnp.zeros(acc.shape, F32)
 
     def step(c, _):
         here = pl.ds(pl.multiple_of(c * FF_BLOCK, FF_BLOCK), FF_BLOCK)
+        up.wait(c)
+        down.wait(c)
         grad_act = times_transposed(dz_out[...], down[here, :])
         low = (gelu_slope(hidden[:, here]) * grad_act).astype(BF16)
         dh_out[:, here] = low
@@ -189,6 +215,7 @@
         return 0
 
     lax.fori_loop(0, FF // FF_BLOCK, step, 0)
+    up.waited = down.waited = True
     grad_mid, grad_gain = standardise_back(acc[...], gain, mid[...])
     gain_out[...] = grad_gain
     grad_mid = grad_mid + grad
@@ -221,10 +248,20 @@
     return grad_stream + grad_mid[...]
 
 
-def enter_kernel(info, gain_attn, ins, outs):
+def start_of(pos, passes, count, here, at):
+    return at - (pos[0, at] * count[0, at] + passes[0, at])
+
+
+def third_start(start):
+    return jnp.where((start < 0) | (start > ROWS), ROWS, start)
+
+
+def enter_kernel(pos, passes, count, gain_attn, ins, outs):
     tokens, w_qkv = ins
     slots, normed = outs
-    project(tokens[...].astype(F32), gain_attn[...], w_qkv, info[3], info[4].astype(F32), slots, normed)
+    here = lax.axis_index("seq")
+    third = third_start(start_of(pos, passes, count, here, ROWS - 1))
+    project(tokens[...].astype(F32), gain_attn[...], w_qkv, here % 2, third.astype(F32), slots, normed)
 
 
 def turn_kernel(info, passes, table, gain_attn, gain_mlp, ins, outs, features, acc):
@@ -254,16 +291,26 @@
     mix_back(cotangent[...].astype(F32), odd, gain, mid, hidden, (w_out, w_up, w_down), acc, dz, dh, dy, dmid, gain_out, slots)
 
 
-def return_kernel(info, passes, gain_attn, gain_mlp, ins, outs, features, acc):
-    recv, w_qkv, stream, grad_mid, w_down, hidden, w_up, mid, w_out = ins
-    slots, dproj, gain_attn_out, table_out, dz, dh, dy, dmid, gain_mlp_out = outs
+def return_kernel(info, passes, gain_attn, gain_mlp, gain_m_two, ins, outs, features, acc, dz, dh, dy, gain_m):
+    (recv, w_qkv, stream, grad_mid, hidden, w_down, w_up, mid, w_out,
+     mid_one, mid_two, dh_two, act_one, act_two, dz_two, att_one, att_two, dy_two) = ins
+    slots, dproj, dmid, up_out, down_out, out_out = outs
     odd = info[3]
-    grad = project_back(recv, odd, gain_attn[...], stream, grad_mid, w_qkv, features, dproj, gain_attn_out)
+    small = jnp.zeros((16, WIDTH), F32)
+    at = lax.broadcasted_iota(jnp.int32, (16, 1), 0)
+    grad = project_back(recv, odd, gain_attn[...], stream, grad_mid, w_qkv, features, dproj, gain_m)
     dproj.flush()
+    small = jnp.where(at == PASSES, gain_m[...], small)
     for row in range(PASSES):
-        table_out[row : row + 1, :] = jnp.sum(jnp.where(passes[...] == row, grad, 0.0), axis=0, keepdims=True)
-    table_out[PASSES:8, :] = jnp.zeros((8 - PASSES, WIDTH), F32)
-    mix_back(grad, odd, gain_mlp[...], mid, hidden.ready(), (w_out, w_up, w_down), acc, dz, dh, dy, dmid, gain_mlp_out, slots)
+        part = jnp.sum(jnp.where(passes[...] == row, grad, 0.0), axis=0, keepdims=True)
+        small = jnp.where(at == row, part, small)
+    mix_back(grad, odd, gain_mlp[...], mid, hidden.ready(), (w_out, w_up, w_down), acc, dz, dh, dy, dmid, gain_m, slots)
+    slots.flush()
+    small = jnp.where(at == PASSES + 1, gain_m[...] + gain_m_two[...], small)
+    weight_gradients(
+        (mid_one, dh, mid_two, dh_two, act_one, dz, act_two, dz_two, att_one, dy, att_two, dy_two),
+        small, up_out, down_out, out_out,
+    )
 
 
 def leave_kernel(info, gain_attn, ins, outs, features):
@@ -276,17 +323,31 @@
     return jax.ShapeDtypeStruct(dims, dtype)
 
 
-def in_vmem(kernel, name, info, small, arrays, outs, scratch, flops):
+def in_vmem(kernel, name, info, small, arrays, outs, scratch, flops, split={}):
     vmem = pl.BlockSpec(memory_space=pltpu.VMEM)
     hbm = pl.BlockSpec(memory_space=pl.ANY)
     ins, count = len(arrays), len(arrays) + len(outs)
 
-    def body(info, *refs):
+    info = info if isinstance(info, tuple) else (info,)
+
+    def body(*refs):
+        known, refs = refs[: len(info)], refs[len(info) :]
         few, refs = refs[: len(small)], refs[len(small) :]
         far, near, sems, rest = refs[:count], refs[count : 2 * count], refs[2 * count], refs[2 * count + 1 :]
-        held = [Held(far[i], near[i], sems.at[i]) for i in range(ins)]
+        held, blocks = [], []
+        for i in range(ins):
+            if i in split:
+                own = sems.at[pl.ds(count + 6 * len(blocks), 6)]
+                held.append(HeldBlocks(far[i], near[i], own, split[i]))
+                blocks.append(held[-1])
+                if len(blocks) == 2:
+                    for c in range(6):
+                        for one in blocks:
+                            one.copy(c).start()
+            else:
+                held.append(Held(far[i], near[i], sems.at[i]))
         kept = [Kept(near[i], far[i], sems.at[i]) for i in range(ins, count)]
-        kernel(info, *few, held, kept, *rest)
+        kernel(*known, *few, held, kept, *rest)
         for one in kept:
             if not one.started:
                 one.flush()
@@ -298,30 +359,30 @@
     return pl.pallas_call(
         body,
         out_shape=tuple(outs),
-        in_specs=[pl.BlockSpec(memory_space=pltpu.SMEM)] + [vmem] * len(small) + [hbm] * ins,
+        in_specs=[pl.BlockSpec(memory_space=pltpu.SMEM)] * len(info) + [vmem] * len(small) + [hbm] * ins,
         out_specs=(hbm,) * len(outs),
         scratch_shapes=[pltpu.VMEM(x.shape, x.dtype) for x in (*arrays, *outs)]
-        + [pltpu.SemaphoreType.DMA((count,))]
+        + [pltpu.SemaphoreType.DMA((count + 12,))]
         + scratch,
-        compiler_params=pltpu.CompilerParams(vmem_limit_bytes=56 << 20),
+        compiler_params=pltpu.CompilerParams(vmem_limit_bytes=62 << 20),
         cost_estimate=pl.CostEstimate(flops=int(flops), bytes_accessed=16 << 20, transcendentals=1 << 20),
         name=name,
-    )(info, *small, *arrays)
-
-
-LATE = 7680
+    )(*info, *small, *arrays)
+
+
+LATE = 7168
 CORE = 5
 
 
-def grads_kernel(info, small, ins, outs):
-    dh_one, mid_one, dh_two, mid_two, act_one, dz_one, act_two, dz_two, att_one, dy_one, att_two, dy_two = ins
-    up, down, out = outs
+def weight_gradients(factors, small, up, down, out):
+    mid_one, dh_one, mid_two, dh_two, act_one, dz_one, act_two, dz_two, att_one, dy_one, att_two, dy_two = factors
+    for one in (dh_two, act_one, act_two):
+        one.ready()
 
     def left(one, two):
         return jnp.concatenate([one, two], axis=0).T
 
     mid = left(mid_one[...], mid_two[...])
-    dh_one.ready(), dh_two.ready()
 
     def step_up(c, _):
         here = pl.ds(pl.multiple_of(c * 512, 512), 512)
@@ -331,7 +392,6 @@
     lax.fori_loop(0, 6, step_up, 0)
     up.flush()
     dz = jnp.concatenate([dz_one[...], dz_two[...]], axis=0)
-    act_one.ready(), act_two.ready()
 
     def step_down(c, _):
         here = pl.ds(pl.multiple_of(c * 512, 512), 512)
@@ -342,7 +402,7 @@
     down.flush()
     dy = jnp.concatenate([dy_one[...], dy_two[...]], axis=0)
     out[0:WIDTH, :] = dot(left(att_one[...], att_two[...]), dy).astype(BF16)
-    out[WIDTH:, :] = small[...].astype(BF16)
+    out[WIDTH:, :] = small.astype(BF16)
 
 
 def grad_qkv_kernel(info, ins, outs):
@@ -368,18 +428,16 @@
     def step(c, _):
         result = dot(left, dproj[:, pl.ds(pl.multiple_of(c * 384, 384), 384)])
         for to, out in enumerate(outs):
-
-            @pl.when(core == to)
-            def _():
-                for i in range(3):
-                    part = (result[:384, 128 * i : 128 * i + 128] + before[3 * c + i, :384, :]).astype(BF16)
-                    out[pl.ds(pl.multiple_of((3 * c + i) * 384, 384), 384), :] = part
-
-            @pl.when(core != to)
-            def _():
-                for i in range(3):
-                    part = (result[384:, 128 * i : 128 * i + 128] + before[3 * c + i, 384:, :]).astype(BF16)
-                    out[pl.ds(pl.multiple_of((3 * c + i) * 384, 384), 384), :] = part
+            for half in range(2):
+
+                @pl.when((half ^ core) == to)
+                def _():
+                    for i in range(3):
+                        for part in range(3):
+                            rows = slice(384 * half + 128 * part, 384 * half + 128 * part + 128)
+                            value = result[rows, 128 * i : 128 * i + 128] + before[3 * c + i, rows, :]
+                            at = pl.multiple_of(part * 2304 + (3 * c + i) * 128, 128)
+                            out[pl.ds(at, 128), :] = value.astype(BF16)
 
         return 0
 
@@ -392,8 +450,8 @@
     half = pl.program_id(0) // 3
 
     def put(ref):
-        for i in range(ref.shape[0]):
-            out[:, 128 * i : 128 * i + 128] = ref[i].astype(F32)
+        for i in range(18):
+            out[:, 128 * i : 128 * i + 128] = ref[128 * i : 128 * i + 128, :].astype(F32)
 
     @pl.when(half == core[0])
     def _():
@@ -404,27 +462,26 @@
         put(other)
 
 
-def widen(core, mine, other, columns, height, first):
+def widen(core, mine, other):
     def place(own):
         def index(i, core):
             low = core[0] == (0 if own else 1)
-            part = jnp.where(low, jnp.minimum(i, 2), jnp.maximum(i - 3, 0))
-            return (first // columns, part, 0)
-
-        return pl.BlockSpec((columns, height // 3, 128), index)
+            return (jnp.where(low, jnp.minimum(i, 2), jnp.maximum(i - 3, 0)), 0)
+
+        return pl.BlockSpec((2304, 128), index)
 
     return pl.pallas_call(
         widen_kernel,
-        out_shape=shape(2 * height, columns * 128, dtype=F32),
+        out_shape=shape(WIDTH, 3 * WIDTH, dtype=F32),
         grid_spec=pltpu.PrefetchScalarGridSpec(
             num_scalar_prefetch=1,
             grid=(6,),
             in_specs=[place(True), place(False)],
-            out_specs=pl.BlockSpec((height // 3, columns * 128), lambda i, core: (i, 0)),
+            out_specs=pl.BlockSpec((128, 3 * WIDTH), lambda i, core: (i, 0)),
         ),
         compiler_params=pltpu.CompilerParams(vmem_limit_bytes=20 << 20),
         name="widen",
-    )(core, mine.reshape(-1, height, 128), other.reshape(-1, height, 128))
+    )(core, mine, other)
 
 
 def swap(value, bit):
@@ -464,7 +521,7 @@
     return jnp.where(at < second, 0, jnp.where(at < third, second, third))
 
 
-def attend_kernel(info, recv_far, out_low_far, out_f_far, lse_far, kv_t_far, q_t_far, recv, out_low, out_f, lse, kv_t, q_t, sems, top, acc, *, devs):
+def attend_kernel(info, recv_far, out_low_far, out_f_far, lse_far, k_t_far, q_t_far, recv, out_low, out_f, lse, kv_t, q_t, sems, acc, *, devs):
     tile_rows = devs * HALF
     span = devs * ROWS
     active, half, second = info[0], info[1], info[2]
@@ -474,10 +531,10 @@
         parts = [
             Held(recv_far.at[8 * i : 8 * i + 8], recv.at[8 * i : 8 * i + 8], sems.at[i]) for i in range(4)
         ]
-        fars = (kv_t_far, q_t_far, out_low_far, out_f_far, lse_far)
+        fars = (k_t_far, q_t_far, out_low_far, out_f_far, lse_far)
         kept = [
             Kept(near, far, sems.at[4 + i])
-            for i, (near, far) in enumerate(zip((kv_t, q_t, out_low, out_f, lse), fars))
+            for i, (near, far) in enumerate(zip((kv_t.at[0:64], q_t, out_low, out_f, lse), fars))
         ]
         ones = (lax.broadcasted_iota(jnp.int32, (16, ROWS), 0) == 0).astype(BF16)
         for d in range(SEQ):
@@ -504,53 +561,28 @@
             query_top = jnp.maximum(query_top, square_top(q_t[0:64, 1024 * c : 1024 * c + 1024]))
         small = key_top * query_top < (SMALL / LOG2E) ** 2
 
-        def one_tile(t, shifted):
+        def one_tile(t, _):
             start = t * span
             columns = pl.ds(pl.multiple_of(t * tile_rows, tile_rows), tile_rows)
             at = positions(half, start, tile_rows)
             first = first_keys(at, second, third)
-            top[...] = jnp.full((1, tile_rows), LOW if shifted else 0.0, F32)
             acc[...] = jnp.zeros((80, tile_rows), F32)
             queries = q_t[:, columns]
 
             def update(kv, key_rows, left, mask):
                 here = slice(left, tile_rows)
-                scores = dot(kv, queries[:, here]) * LOG2E
-                if not shifted:
-                    weights = jnp.exp2(scores)
-                    if mask is not None:
-                        weights = jnp.where(mask, weights, 0.0)
-                    acc[:, here] = acc[:, here] + dot(kv_t[64:144, key_rows], weights.astype(BF16))
-                    return
+                weights = jnp.exp2(dot(kv, queries[:, here]) * LOG2E)
                 if mask is not None:
-                    scores = jnp.where(mask, scores, LOW)
-                old_top = top[:, here]
-                new_top = jnp.maximum(old_top, jnp.max(scores, axis=0, keepdims=True))
-                weights = jnp.exp2(scores - new_top).astype(BF16)
-                shrink = jnp.exp2(old_top - new_top)
-                acc[:, here] = acc[:, here] * shrink + dot(kv_t[64:144, key_rows], weights)
-                top[:, here] = new_top
-
-            def whole(j, masked):
-                key_start = pl.multiple_of(j * 1024, 1024)
+                    weights = jnp.where(mask, weights, 0.0)
+                acc[:, here] = acc[:, here] + dot(kv_t[64:144, key_rows], weights.astype(BF16))
+
+            def step(j, _):
                 kv = recv[pl.ds(j * 4, 4), 0:ROWS, :].reshape(1024, 128)
-                mask = None
-                if masked:
-                    mask = lax.broadcasted_iota(jnp.int32, (1024, 1), 0) >= second
-                update(kv, pl.ds(key_start, 1024), 0, mask)
-
-            @pl.when(t > 0)
-            def _():
-                whole(0, True)
-
-            def step(j, _):
-                whole(j, False)
+                update(kv, pl.ds(pl.multiple_of(j * 1024, 1024), 1024), 0, None)
                 return 0
 
-            lax.fori_loop(1, t * (span // 1024), step, 0)
-            fresh = first >= start
-            top[...] = jnp.where(fresh, LOW if shifted else 0.0, top[...])
-            acc[...] = jnp.where(fresh, 0.0, acc[...])
+            lax.fori_loop(0, t * (span // 1024), step, 0)
+            acc[...] = jnp.where(first >= start, 0.0, acc[...])
             for i in range(devs // 2):
                 left = 256 * i
                 key_start = pl.multiple_of(start + 512 * i, 512)
@@ -561,20 +593,51 @@
             total = acc[64:65, :]
             result = acc[0:64, :] / total
             out_f[:, columns] = result
-            lse[:, columns] = top[...] + jnp.log2(total)
+            lse[:, columns] = jnp.log2(total)
             low = result.astype(BF16)
             for i in range(devs):
                 out_low[t * devs + i] = low[:, i * HALF : (i + 1) * HALF]
 
-        for shifted in (False, True):
-
-            @pl.when(small != shifted)
+            @pl.when(t == 0)
             def _():
-                def tile(t, _):
-                    one_tile(t, shifted)
-                    return 0
-
-                lax.fori_loop(0, SEQ // devs, tile, 0)
+                key_at = lax.broadcasted_iota(jnp.int32, (1, ROWS), 1)
+                kv_t[64:144, 0:ROWS] = jnp.where(key_at >= second, kv_t[64:144, 0:ROWS], 0.0).astype(BF16)
+
+            return 0
+
+        def one_device(d, _):
+            columns = pl.ds(pl.multiple_of(d * HALF, HALF), HALF)
+            at = d * ROWS + (half + d) % 2 * HALF + lax.broadcasted_iota(jnp.int32, (1, HALF), 1)
+            first = first_keys(at, second, third_keys(recv, HALF))
+            queries = q_t[:, columns]
+
+            def step(j, state):
+                old_top, old_acc = state
+                kv = recv[pl.ds(j * 2, 2), 0:ROWS, :].reshape(512, 128)
+                key_at = j * 512 + lax.broadcasted_iota(jnp.int32, (512, 1), 0)
+                allowed = (key_at >= first) & (key_at <= at)
+                scores = jnp.where(allowed, dot(kv, queries) * LOG2E, LOW)
+                new_top = jnp.maximum(old_top, jnp.max(scores, axis=0, keepdims=True))
+                weights = jnp.exp2(scores - new_top).astype(BF16)
+                keys = pl.ds(pl.multiple_of(j * 512, 512), 512)
+                return new_top, old_acc * jnp.exp2(old_top - new_top) + dot(kv_t[64:144, keys], weights)
+
+            state = (jnp.full((1, HALF), LOW, F32), jnp.zeros((80, HALF), F32))
+            top, state = lax.fori_loop(0, d // 2 + 1, step, state)
+            total = state[64:65, :]
+            result = state[0:64, :] / total
+            out_f[:, columns] = result
+            lse[:, columns] = top + jnp.log2(total)
+            out_low[d] = result.astype(BF16)
+            return 0
+
+        @pl.when(small)
+        def _():
+            lax.fori_loop(0, SEQ // devs, one_tile, 0)
+
+        @pl.when(jnp.logical_not(small))
+        def _():
+            lax.fori_loop(0, SEQ, one_device, 0)
 
         for one in kept[2:]:
             one.flush()
@@ -591,7 +654,7 @@
             jax.ShapeDtypeStruct((SEQ, 64, HALF), BF16),
             jax.ShapeDtypeStruct((64, SEQ * HALF), F32),
             jax.ShapeDtypeStruct((1, SEQ * HALF), F32),
-            jax.ShapeDtypeStruct((144, SEQ * ROWS), BF16),
+            jax.ShapeDtypeStruct((64, SEQ * ROWS), BF16),
             jax.ShapeDtypeStruct((128, SEQ * HALF), BF16),
         ),
         in_specs=[
@@ -607,10 +670,9 @@
             pltpu.VMEM((144, SEQ * ROWS), BF16),
             pltpu.VMEM((128, SEQ * HALF), BF16),
             pltpu.SemaphoreType.DMA((9,)),
-            pltpu.VMEM((1, devs * HALF), F32),
             pltpu.VMEM((80, devs * HALF), F32),
         ],
-        compiler_params=pltpu.CompilerParams(vmem_limit_bytes=56 << 20),
+        compiler_params=pltpu.CompilerParams(vmem_limit_bytes=62 << 20),
         cost_estimate=pl.CostEstimate(
             flops=int(pairs * 1024), bytes_accessed=8 << 20, transcendentals=int(pairs)
         ),
@@ -659,9 +721,7 @@
             def update(kv, key_rows, left, row_lse, mask):
                 here = slice(left, tile_rows)
                 scores = dot(kv, queries[:, here]) * LOG2E
-                probs = jnp.exp2(scores - row_lse[:, here])
-                if mask is not None:
-                    probs = jnp.where(mask, probs, 0.0)
+                probs = jnp.where(mask, jnp.exp2(scores - row_lse[:, here]), 0.0)
                 grad_probs = dot(kv, grads[:, here])
                 grad_scores = (probs * (grad_probs - delta[:, here])).astype(BF16)
                 grad_kv[key_rows, :] += dot(grad_scores, query_rows[here, :]) + dot(
@@ -669,23 +729,13 @@
                 )
                 grad_q[:, here] += dot(kv_t[0:64, key_rows], grad_scores)
 
-            def whole(j, masked):
-                key_start = pl.multiple_of(j * 1024, 1024)
+            def step(j, _):
                 kv = recv[pl.ds(j * 4, 4), 0:ROWS, :].reshape(1024, 128)
-                mask = None
-                if masked:
-                    mask = lax.broadcasted_iota(jnp.int32, (1024, 1), 0) >= second
-                update(kv, pl.ds(key_start, 1024), 0, far_lse, mask)
-
-            @pl.when(t > 0)
-            def _():
-                whole(0, True)
-
-            def step(j, _):
-                whole(j, False)
+                key_at = j * 1024 + lax.broadcasted_iota(jnp.int32, (1024, 1), 0)
+                update(kv, pl.ds(pl.multiple_of(j * 1024, 1024), 1024), 0, far_lse, key_at >= second)
                 return 0
 
-            lax.fori_loop(1, t * (span // 1024), step, 0)
+            lax.fori_loop(0, t * (span // 1024), step, 0)
             for i in range(devs // 2):
                 left = 256 * i
                 key_start = pl.multiple_of(start + 512 * i, 512)
@@ -695,18 +745,26 @@
                 update(kv, pl.ds(key_start, 512), left, own_lse, allowed)
             low = (grad_q[...] * HEAD_DIM**-0.5).astype(BF16)
             for i in range(devs):
-                send[t * devs + i, ROWS:, :] = low[:, i * HALF : (i + 1) * HALF]
+                d = t * devs + i
+                send[d, ROWS:, :] = low[:, i * HALF : (i + 1) * HALF]
+                send[d, 0:ROWS, :] = grad_kv[pl.ds(pl.multiple_of(d * ROWS, ROWS), ROWS), :].astype(BF16)
+            sending(t).start()
             return 0
 
-        lax.fori_loop(0, SEQ // devs, one_tile, 0)
-        for d in range(SEQ):
-            send[d, 0:ROWS, :] = grad_kv[d * ROWS : (d + 1) * ROWS, :].astype(BF16)
-        out = Kept(send, send_far, sems.at[6])
-        out.finish()
+        def sending(t):
+            here = pl.ds(t * devs, devs)
+            return pltpu.make_async_copy(send.at[here], send_far.at[here], sems.at[6 + t])
+
+        def from_last(i, _):
+            return one_tile(SEQ // devs - 1 - i, 0)
+
+        lax.fori_loop(0, SEQ // devs, from_last, 0)
+        for t in range(SEQ // devs):
+            sending(t).wait()
 
 
 def attend_back(info, recv, kv_t, q_t, out_f, lse, grad_out):
-    devs = 4
+    devs = 8
     pairs = 17.8e6
     return pl.pallas_call(
         functools.partial(attend_back_kernel, devs=devs),
@@ -716,18 +774,18 @@
         out_specs=pl.BlockSpec(memory_space=pl.ANY),
         scratch_shapes=[
             pltpu.VMEM((SEQ, SLOT, 128), BF16),
-            pltpu.VMEM((144, SEQ * ROWS), BF16),
+            pltpu.VMEM((64, SEQ * ROWS), BF16),
             pltpu.VMEM((128, SEQ * HALF), BF16),
             pltpu.VMEM((64, SEQ * HALF), F32),
             pltpu.VMEM((1, SEQ * HALF), F32),
             pltpu.VMEM((SEQ, 64, HALF), BF16),
             pltpu.VMEM((SEQ, ROWS + 64, HALF), BF16),
-            pltpu.SemaphoreType.DMA((7,)),
+            pltpu.SemaphoreType.DMA((14,)),
             pltpu.VMEM((SEQ * ROWS, 128), F32),
             pltpu.VMEM((128, SEQ * HALF), BF16),
             pltpu.VMEM((64, devs * HALF), F32),
         ],
-        compiler_params=pltpu.CompilerParams(vmem_limit_bytes=56 << 20),
+        compiler_params=pltpu.CompilerParams(vmem_limit_bytes=62 << 20),
         cost_estimate=pl.CostEstimate(
             flops=int(pairs * 1024), bytes_accessed=8 << 20, transcendentals=int(pairs)
         ),
@@ -750,12 +808,10 @@
     cotangent,
 ):
     here = lax.axis_index("seq")
-    offset = token_pos[0] * token_count[0] + token_pass[0]
-    first_token = here * ROWS - offset[0]
-    last_token = here * ROWS + ROWS - 1 - offset[ROWS - 1]
-    second = jnp.where(here == 0, last_token, first_token)
-    third = last_token - (SEQ - 1) * ROWS
-    third = jnp.where((third < 0) | (third > ROWS), ROWS, third)
+    documents = (token_pos, token_pass, token_count)
+    edge = jnp.where(here == 0, ROWS - 1, 0)
+    second = here * ROWS + start_of(*documents, here, edge)
+    third = third_start(start_of(*documents, here, ROWS - 1))
     group, place = here // 4, here % 4
     active = (place < 3).astype(jnp.int32)
     core = lax.axis_index("batch") % 2
@@ -773,7 +829,7 @@
     sent_back = shape(SEQ, 64, 128)
 
     slots, normed_one = in_vmem(
-        enter_kernel, "enter", info, (gain_a,), (stream_one, w_qkv), (sent, square), [], 1e9
+        enter_kernel, "enter", documents, (gain_a,), (stream_one, w_qkv), (sent, square), [], 1e9
     )
     saved_one = attend(info, exchange(slots))
     slots, normed_two, stream_two, att_one, mid_one, midn_one, hidden_one, act_one = in_vmem(
@@ -785,6 +841,7 @@
         (sent, square, wide, square, wide, square, shape(ROWS, FF, dtype=F32), shape(ROWS, FF)),
         [features, acc],
         3.6e9,
+        {3: 1, 4: 0},
     )
     saved_two = attend(info, exchange(slots))
     slots, mixed, att_two, midn_two, act_two, dh_two, dy_two, dmid_two, gain_m_two = in_vmem(
@@ -796,45 +853,25 @@
         (sent_back, square, square, square, shape(ROWS, FF), shape(ROWS, FF), square, wide, row),
         [features, acc, acc, pltpu.VMEM((ROWS, FF), F32), pltpu.VMEM((ROWS, WIDTH), BF16)],
         5e9,
+        {3: 1, 4: 0},
     )
     back = exchange(slots)
     recv = exchange(attend_back(info, *saved_two[1:], back))
-    slots, dproj_two, gain_a_two, grad_table, dz_one, dh_one, dy_one, dmid_one, gain_m_one = in_vmem(
+    slots, dproj_two, dmid_one, *early = in_vmem(
         return_kernel,
         "return",
         info,
-        (passes, gain_a, gain_m),
-        (recv, w_qkv, stream_two, dmid_two, w_down, hidden_one, w_up, mid_one, w_out),
-        (
-            sent_back,
-            shape(ROWS, 3 * WIDTH),
-            row,
-            shape(8, WIDTH, dtype=F32),
-            square,
-            shape(ROWS, FF),
-            square,
-            wide,
-            row,
-        ),
-        [features, acc],
-        5e9,
+        (passes, gain_a, gain_m, gain_m_two),
+        (recv, w_qkv, stream_two, dmid_two, hidden_one, w_down, w_up, mid_one, w_out,
+         midn_one, midn_two, dh_two, act_one, act_two, cotangent[0], att_one, att_two, dy_two),
+        (sent_back, shape(ROWS, 3 * WIDTH), wide, shape(WIDTH, FF), shape(FF, WIDTH), shape(WIDTH + 16, WIDTH)),
+        [features, acc, pltpu.VMEM((ROWS, WIDTH), BF16), pltpu.VMEM((ROWS, FF), BF16),
+         pltpu.VMEM((ROWS, WIDTH), BF16), pltpu.VMEM((1, WIDTH), F32)],
+        1e10,
+        {5: 0, 6: 1},
     )
     back = exchange(slots)
-    small = jnp.concatenate(
-        [grad_table[:PASSES], gain_a_two, gain_m_one + gain_m_two, jnp.zeros((9, WIDTH), F32)]
-    )
-    early = in_vmem(
-        grads_kernel,
-        "grads",
-        info,
-        (small,),
-        (dh_one, midn_one, dh_two, midn_two, act_one, dz_one, act_two, cotangent[0], att_one, dy_one, att_two, dy_two),
-        (shape(WIDTH, FF), shape(FF, WIDTH), shape(WIDTH + 16, WIDTH)),
-        [],
-        5.4e10,
-    )
-    back, early = lax.optimization_barrier((back, early))
-    early = lax.psum(early, ("seq", "batch"))
+    early = lax.psum(tuple(early), ("seq", "batch"))
     sent_one = attend_back(info, *saved_one[1:], back)
     recv = exchange(sent_one)
     grad_tokens, dproj_one, gain_a_one = in_vmem(
@@ -869,19 +906,19 @@
     )
     late, early = lax.optimization_barrier((late, early))
     late = across_chips(sum_cores(late).reshape(CHIPS, -1, 128))
-    early = tuple(x.astype(F32) for x in early)
+    tail = early[2][WIDTH:].astype(F32)
+    early = (early[0].astype(F32), early[1].astype(F32), early[2][:WIDTH].astype(F32))
     late, early = lax.optimization_barrier((late, early))
     late = jnp.sum(late.astype(F32), axis=0).astype(BF16)
     whole = across_chips(jnp.broadcast_to(late[None], (CHIPS, *late.shape))).reshape(-1, 128)
     late = (whole, swap(whole, 1))
     grad_up, grad_down, grad_out = early
-    tail = grad_out[WIDTH : WIDTH + 8]
     gain_a_sum = late[0][6912:6918].reshape(WIDTH).astype(F32)
     return (
         mixed[None],
         grad_tokens[None],
-        widen(info[CORE : CORE + 1], *late, 18, 384, 0),
-        grad_out[:WIDTH],
+        widen(info[CORE : CORE + 1], *late),
+        grad_out,
         grad_up,
         grad_down,
         tail[PASSES] + gain_a_sum,

time: 649 us -> 618 us (0.952)
  Pallas kernels: 265 us -> 236 us
    pallas_call x2, Pallas kernels: 59.7 us -> 47.6 us  [attend(): pl.pallas_call(functools.partial(attend_kernel, devs=devs), out_shape=(ja...]
    pallas_call x8 -> x7, Pallas kernels: 89.7 us -> 79.7 us  [in_vmem(): pl.pallas_call(body, out_shape=tuple(outs), in_specs=[pl.BlockSpec(memory...]
    pallas_call x2, Pallas kernels: 112 us -> 105 us  [attend_back(): pl.pallas_call(functools.partial(attend_back_kernel, devs=devs), out_shap...]
    all_to_all x4 -> x5, blocking collectives: 107 us -> 113 us  [exchange(): return lax.all_to_all(slots, 'seq', 0, 0)]
    all_to_all x4 -> x3, starting transfers between devices: 25.8 us -> 22.3 us  [exchange(): return lax.all_to_all(slots, 'seq', 0, 0)]
    convert_element_type x3 -> x4, other arithmetic: 13.5 us -> 15.9 us  [the longest x1 7.37 us: on_device(): early[0].astype(F32)]
    all_to_all x4 -> x3, waiting for transfers between devices: 58 us -> 56.9 us  [exchange(): return lax.all_to_all(slots, 'seq', 0, 0)]
  transfers between devices with their start and end apart: 8 -> 7, of which waited for: 7 -> 7; matrix products, arithmetic and copies ran while one was open for 3% -> 4% of each run, Pallas kernels for 14% -> 12%
where the time goes in v3:
time: 618 us; the launch traced here: 609 us
  Pallas kernels  236 us (38%)
  waiting for transfers between devices  149 us (24%)
  blocking collectives  143 us (23%)
  starting transfers between devices  33 us (5%)
  other arithmetic  20.6 us (3%)
  between operations  18.4 us (3%)
  local copies, waits for them, and re-layouts  8.94 us (1%)
    all_to_all x5, blocking collectives, exchange(): return lax.all_to_all(slots, 'seq', 0, 0)  113 us
    pallas_call x2, Pallas kernels, attend_back(): pl.pallas_call(functools.partial(attend_back_kernel, devs=devs), out_shap...  105 us
    pallas_call x7, Pallas kernels, in_vmem(): pl.pallas_call(body, out_shape=tuple(outs), in_specs=[pl.BlockSpec(memory...  79.7 us
    psum x1, waiting for transfers between devices, on_device(): early = lax.psum(tuple(early), ('seq', 'batch'))  76.1 us
    all_to_all x3, waiting for transfers between devices, exchange(): return lax.all_to_all(slots, 'seq', 0, 0)  56.9 us
    pallas_call x2, Pallas kernels, attend(): pl.pallas_call(functools.partial(attend_kernel, devs=devs), out_shape=(ja...  47.6 us
    all_to_all x1, blocking collectives, across_chips(): lax.all_to_all(slots, ('seq', 'batch'), 0, 0, axis_index_groups=groups)  30.1 us
    all_to_all x3, starting transfers between devices, exchange(): return lax.all_to_all(slots, 'seq', 0, 0)  22.3 us
  transfers between devices with their start and end apart: 7, of which 7 were waited for; matrix products, arithmetic and copies ran while one was open for 4% of the time, Pallas kernels for 12%

profile of v3, /device:TPU:1, one launch (start us, length us, event | category | flops | bytes accessed | tf_op | source)
XLA Modules:
  0.0 608.8 jit_solution(12774172478548927599)
XLA Ops:
  8.4 6.7 %enter.1 = (bf16[32,336,128]{2,1,0:T(8,128)(2,1)}, bf16[256,768]{1,0:T(8,128)(2,1)}) custom-call(s32[1,256]{1,0:T(1,128)} %refs_0_.1, s32[1,256]{1,0:T(1,128)} %refs_1_.1, s32[1,256]{1,0:T(1,128)} %refs_2_.1, f32[1,768]{1,0:T(1,128)} %broadcast_in_dim.19.refs_3_.refs_2_.refs_1_, bf16[256,768]{1,0:T(8,128)(2,1)} %bitcast.25, bf16[768,2304]{1,0:T(8,128)(2,1)} %refs_3_.1), custom_call_target="tpu_custom_call" | custom-call | flops 1000000000 | bytes 16777216 | tf_op jit(solution)/shard_map/enter/pallas_call | solution.py:359
  15.2 9.5 %all-to-all-start = ((bf16[32,336,128]{2,1,0:T(8,128)(2,1)}), bf16[32,336,128]{2,1,0:T(8,128)(2,1)}, u32[]{:S(2)}, u32[]{:S(2)}) async-start(bf16[32,336,128]{2,1,0:T(8,128)(2,1)} %get-tuple-element.58), calls=%async_computation | async-start | bytes 5505024 | tf_op jit(solution)/shard_map/all_to_all | solution.py:492
  30.5 28.1 %all-to-all-done.recv_far = bf16[32,336,128]{2,1,0:T(8,128)(2,1)} async-done(((bf16[32,336,128]{2,1,0:T(8,128)(2,1)}), bf16[32,336,128]{2,1,0:T(8,128)(2,1)}, u32[]{:S(2)}, u32[]{:S(2)}) %all-to-all-start) | async-done | bytes 2752544 | tf_op jit(solution)/shard_map/all_to_all | solution.py:492
  58.6 23.8 %attend.2 = (bf16[32,64,128]{2,1,0:T(8,128)(2,1)}, f32[64,4096]{1,0:T(8,128)}, f32[1,4096]{1,0:T(1,128)}, bf16[64,8192]{1,0:T(8,128)(2,1)}, bf16[128,4096]{1,0:T(8,128)(2,1)}) custom-call(s32[6]{0:T(128)} %stack.31.info.refs_0_, bf16[32,336,128]{2,1,0:T(8,128)(2,1)} %all-to-all-done.recv_far), custom_call_target="tpu_custom_call" | custom-call | flops 18227200000 | bytes 8388608 | tf_op jit(solution)/shard_map/attend/pallas_call | solution.py:651
  82.4 8.0 %all-to-all-start.1 = ((bf16[32,64,128]{2,1,0:T(8,128)(2,1)}), bf16[32,64,128]{2,1,0:T(8,128)(2,1)S(1)}, u32[]{:S(2)}, u32[]{:S(2)}) async-start(bf16[32,64,128]{2,1,0:T(8,128)(2,1)} %get-tuple-element.59), calls=%async_computation.1 | async-start | bytes 1048576 | tf_op jit(solution)/shard_map/all_to_all | solution.py:492
  92.4 7.3 %all-to-all-done.1.refs_5_ = bf16[32,64,128]{2,1,0:T(8,128)(2,1)S(1)} async-done(((bf16[32,64,128]{2,1,0:T(8,128)(2,1)}), bf16[32,64,128]{2,1,0:T(8,128)(2,1)S(1)}, u32[]{:S(2)}, u32[]{:S(2)}) %all-to-all-start.1) | async-done | bytes 524320 | tf_op jit(solution)/shard_map/all_to_all | solution.py:492
  100.5 12.1 %turn.1 = (bf16[32,336,128]{2,1,0:T(8,128)(2,1)}, bf16[256,768]{1,0:T(8,128)(2,1)}, f32[256,768]{1,0:T(8,128)}, bf16[256,768]{1,0:T(8,128)(2,1)}, f32[256,768]{1...) custom-call(s32[6]{0:T(128)} %stack.31.info.refs_0_, ...), custom_call_target="tpu_custom_call" | custom-call | flops 3600000000 | bytes 16777216 | tf_op jit(solution)/shard_map/turn/pallas_call | solution.py:359
  112.7 36.8 %all_to_all.50.recv_far = bf16[32,336,128]{2,1,0:T(8,128)(2,1)} all-to-all(bf16[32,336,128]{2,1,0:T(8,128)(2,1)} %get-tuple-element.60), channel_id=1, replica_groups=mesh['seq'=32,'batch'=4] {'seq'}, dimensions={0} | all-to-all | bytes 5505024 | tf_op jit(solution)/shard_map/all_to_all | solution.py:492
  149.4 23.8 %attend.3 = (bf16[32,64,128]{2,1,0:T(8,128)(2,1)}, f32[64,4096]{1,0:T(8,128)}, f32[1,4096]{1,0:T(1,128)}, bf16[64,8192]{1,0:T(8,128)(2,1)}, bf16[128,4096]{1,0:T(8,128)(2,1)}) custom-call(s32[6]{0:T(128)} %stack.31.info.refs_0_, bf16[32,336,128]{2,1,0:T(8,128)(2,1)} %all_to_all.50.recv_far), custom_call_target="tpu_custom_call" | custom-call | flops 18227200000 | bytes 8388608 | tf_op jit(solution)/shard_map/attend/pallas_call | solution.py:651
  173.2 14.1 %all_to_all.51.refs_2_ = bf16[32,64,128]{2,1,0:T(8,128)(2,1)} all-to-all(bf16[32,64,128]{2,1,0:T(8,128)(2,1)} %get-tuple-element.61), channel_id=1, replica_groups=mesh['seq'=32,'batch'=4] {'seq'}, dimensions={0} | all-to-all | bytes 1048576 | tf_op jit(solution)/shard_map/all_to_all | solution.py:492
  187.3 14.9 %crest.1 = (bf16[32,64,128]{2,1,0:T(8,128)(2,1)}, bf16[256,768]{1,0:T(8,128)(2,1)}, bf16[256,768]{1,0:T(8,128)(2,1)}, bf16[256,768]{1,0:T(8,128)(2,1)}, bf16[256...) custom-call(s32[6]{0:T(128)} %stack.31.info.refs_0_, ...), custom_call_target="tpu_custom_call" | custom-call | flops 5000000000 | bytes 16777216 | tf_op jit(solution)/shard_map/crest/pallas_call | solution.py:359
  202.2 13.6 %all_to_all.52.grad_out_far = bf16[32,64,128]{2,1,0:T(8,128)(2,1)} all-to-all(bf16[32,64,128]{2,1,0:T(8,128)(2,1)} %get-tuple-element.73), channel_id=1, replica_groups=mesh['seq'=32,'batch'=4] {'seq'}, dimensions={0} | all-to-all | bytes 1048576 | tf_op jit(solution)/shard_map/all_to_all | solution.py:492
  215.9 52.4 %attend_back.2 = bf16[32,320,128]{2,1,0:T(8,128)(2,1)} custom-call(s32[6]{0:T(128)} %stack.31.info.refs_0_, bf16[32,336,128]{2,1,0:T(8,128)(2,1)} %all_to_all.50.recv_far, bf16[64,8192]{1,0:T(8,128)(2,1)} %get-tuple-element.69.kv_t_far, bf16[128,4096]{1,0:T(8,128)(2,1)} %get-tuple-element.70.q_t_far, f32[64,4096]{1,0:T(8,128)} %get-tuple-element.71.out_f_far, ...), custom_call_target="tpu_custom_call" | custom-call | flops 18227200000 | bytes 8388608 | tf_op jit(solution)/shard_map/attend_back/pallas_call | solution.py:769
  268.3 31.9 %all_to_all.53.refs_5_ = bf16[32,320,128]{2,1,0:T(8,128)(2,1)} all-to-all(bf16[32,320,128]{2,1,0:T(8,128)(2,1)} %attend_back.2), channel_id=1, replica_groups=mesh['seq'=32,'batch'=4] {'seq'}, dimensions={0} | all-to-all | bytes 5242880 | tf_op jit(solution)/shard_map/all_to_all | solution.py:492
  300.2 22.7 %return.1 = (bf16[32,64,128]{2,1,0:T(8,128)(2,1)}, bf16[256,2304]{1,0:T(8,128)(2,1)}, f32[256,768]{1,0:T(8,128)}, bf16[768,3072]{1,0:T(8,128)(2,1)}, bf16[3072,7...) custom-call(s32[6]{0:T(128)} %stack.31.info.refs_0_, s32[256,1]{1,0:T(8,128)} %copy.21.refs_1_, ...), custom_call_target="tpu_custom_call" | custom-call | flops 10000000000 | bytes 16777216 | tf_op jit(solution)/shard_map/return/pallas_call | solution.py:359
  324.0 16.7 %all_to_all.54.grad_out_far = bf16[32,64,128]{2,1,0:T(8,128)(2,1)} all-to-all(bf16[32,64,128]{2,1,0:T(8,128)(2,1)S(1)} %copy-done.2), channel_id=1, replica_groups=mesh['seq'=32,'batch'=4] {'seq'}, dimensions={0} | all-to-all | bytes 1048576 | tf_op jit(solution)/shard_map/all_to_all | solution.py:492
  340.7 52.5 %attend_back.3 = bf16[32,320,128]{2,1,0:T(8,128)(2,1)} custom-call(s32[6]{0:T(128)} %stack.31.info.refs_0_, bf16[32,336,128]{2,1,0:T(8,128)(2,1)} %all-to-all-done.recv_far, bf16[64,8192]{1,0:T(8,128)(2,1)} %get-tuple-element.64.kv_t_far, bf16[128,4096]{1,0:T(8,128)(2,1)} %get-tuple-element.65.q_t_far, f32[64,4096]{1,0:T(8,128)} %get-tuple-element.66.out_f_far, ...), custom_call_target="tpu_custom_call" | custom-call | flops 18227200000 | bytes 8388608 | tf_op jit(solution)/shard_map/attend_back/pallas_call | solution.py:769
  393.2 4.8 all-to-all-start.7
  398.1 7.4 %grad_qkv_two.1.refs_4_ = f32[18,768,128]{2,1,0:T(8,128)} custom-call(s32[6]{0:T(128)} %stack.31.info.refs_0_, bf16[256,768]{1,0:T(8,128)(2,1)} %get-tuple-element.91.refs_1_, bf16[256,2304]{1,0:T(8,128)(2,1)} %get-tuple-element.92.refs_2_), custom_call_target="tpu_custom_call" | custom-call | flops 900000000 | bytes 16777216 | tf_op jit(solution)/shard_map/grad_qkv_two/pallas_call | solution.py:359
  405.4 21.5 %all-to-all-done.7.refs_2_ = bf16[32,320,128]{2,1,0:T(8,128)(2,1)} async-done(((bf16[32,320,128]{2,1,0:T(8,128)(2,1)}), bf16[32,320,128]{2,1,0:T(8,128)(2,1)}, u32[]{:S(2)}, u32[]{:S(2)}) %all-to-all-start.7) | async-done | bytes 2621472 | tf_op jit(solution)/shard_map/all_to_all | solution.py:492
  427.0 6.7 %leave.1 = (f32[256,768]{1,0:T(8,128)}, bf16[256,2304]{1,0:T(8,128)(2,1)}, f32[1,768]{1,0:T(1,128)}) custom-call(s32[6]{0:T(128)} %stack.31.info.refs_0_, f32[1,768]{1,0:T(1,128)} %broadcast_in_dim.19.refs_3_.refs_2_.refs_1_, bf16[32,320,128]{2,1,0:T(8,128)(2,1)} %all-to-all-done.7.refs_2_, bf16[768,2304]{1,0:T(8,128)(2,1)} %refs_3_.1, ...), custom_call_target="tpu_custom_call" | custom-call | flops 1000000000 | bytes 16777216 | tf_op jit(solution)/shard_map/leave/pallas_call | solution.py:359
  435.0 9.1 %grad_qkv.1 = (bf16[7168,128]{1,0:T(8,128)(2,1)}, bf16[7168,128]{1,0:T(8,128)(2,1)}) custom-call(s32[6]{0:T(128)} %stack.31.info.refs_0_, f32[16,128]{1,0:T(8,128)} %pad.9.refs_1_, bf16[256,768]{1,0:T(8,128)(2,1)} %get-tuple-element.89.refs_2_, bf16[256,2304]{1,0:T(8,128)(2,1)} %get-tuple-element.90.refs_3_, f32[18,768,128]{2,1,0:T(8,128)} %grad_qkv_two.1.refs_4_), custom_call_target="tpu_custom_call" | custom-call | flops 900000000 | bytes 16777216 | tf_op jit(solution)/shard_map/grad_qkv/pallas_call | solution.py:359
  444.1 76.1 %all-reduce.5.cloned.1.call-done = (bf16[768,3072]{1,0:T(8,128)(2,1)}, bf16[3072,768]{1,0:T(8,128)(2,1)}, bf16[784,768]{1,0:T(8,128)(2,1)}) async-done(((bf16[768,3072]{1,0:T(8,128)(2,1)}, bf16[3072,768]{1,0:T(8,128)(2,1)}, bf16[784,768]{1,0:T(8,128)(2,1)}), (bf16[768,3072]{1,0:T(8,128)(2,1)}, bf16[3072,768]{1,0:T(8,128)(2,1)}, bf16[784,768]{1,0:T(8,128)(2,1)})) %all-reduce.5.cloned.1.call-update) | async-done | bytes 10641424 | tf_op jit(solution)/shard_map/psum | solution.py:874
  520.9 3.6 collective-permute-done
  524.5 3.2 add_convert_fusion
  527.7 7.6 %all-to-all-start.8 = ((bf16[64,112,128]{2,1,0:T(8,128)(2,1)}), bf16[64,112,128]{2,1,0:T(8,128)(2,1)S(1)}, u32[]{:S(2)}, u32[]{:S(2)}) async-start(bf16[64,112,128]{2,1,0:T(8,128)(2,1)} %bitcast.24), calls=%async_computation.8 | async-start | bytes 3670016 | tf_op jit(solution)/shard_map/all_to_all | solution.py:505
  535.3 7.4 %convert_element_type.37 = f32[768,3072]{1,0:T(8,128)} convert(bf16[768,3072]{1,0:T(8,128)(2,1)} %get-tuple-element.100) | non-fusion elementwise | flops 2359296 | bytes 14155776 | tf_op jit(solution)/shard_map/convert_element_type | solution.py:910
  542.7 6.9 %convert_element_type.38 = f32[3072,768]{1,0:T(8,128)} convert(bf16[3072,768]{1,0:T(8,128)(2,1)} %get-tuple-element.101) | non-fusion elementwise | flops 2359296 | bytes 14155776 | tf_op jit(solution)/shard_map/convert_element_type | solution.py:910
  551.2 10.5 %all-to-all-done.8 = bf16[64,112,128]{2,1,0:T(8,128)(2,1)S(1)} async-done(((bf16[64,112,128]{2,1,0:T(8,128)(2,1)}), bf16[64,112,128]{2,1,0:T(8,128)(2,1)S(1)}, u32[]{:S(2)}, u32[]{:S(2)}) %all-to-all-start.8) | async-done | bytes 1835040 | tf_op jit(solution)/shard_map/all_to_all | solution.py:505
  562.2 30.1 %all_to_all.55 = bf16[64,112,128]{2,1,0:T(8,128)(2,1)S(1)} all-to-all(bf16[64,112,128]{2,1,0:T(8,128)(2,1)S(1)} %broadcast_in_dim.22), channel_id=1, replica_groups={{0,2,4,6,8,10,12,14,16,18,20,22,24,26,28,30,32,34,36,38,40,42,44,46,48,..., dimensions={0} | all-to-all | bytes 3670016 | tf_op jit(solution)/shard_map/all_to_all | solution.py:505
  592.3 2.4 collective-permute-start.1
  598.1 3.7 widen.1
  (36 shorter events, 14.4 us)
Async XLA Ops:
  15.2 9.6 %copy-start.6 = (s32[1,256]{1,0:T(1,128)S(1)}, s32[1,256]{1,0:T(1,128)}, u32[]{:S(2)}) copy-start(s32[1,256]{1,0:T(1,128)} %refs_0_.1) | copy-start | bytes 3076
  15.2 10.2 %copy-start.4 = (s32[1,256]{1,0:T(1,128)S(1)}, s32[1,256]{1,0:T(1,128)}, u32[]{:S(2)}) copy-start(s32[1,256]{1,0:T(1,128)} %refs_1_.1) | copy-start | bytes 3076
  15.2 10.2 %copy-start.7 = (s32[1,256]{1,0:T(1,128)S(1)}, s32[1,256]{1,0:T(1,128)}, u32[]{:S(2)}) copy-start(s32[1,256]{1,0:T(1,128)} %refs_2_.1) | copy-start | bytes 3076
  15.2 43.4 %all-to-all-start = ((bf16[32,336,128]{2,1,0:T(8,128)(2,1)}), bf16[32,336,128]{2,1,0:T(8,128)(2,1)}, u32[]{:S(2)}, u32[]{:S(2)}) async-start(bf16[32,336,128]{2,1,0:T(8,128)(2,1)} %get-tuple-element.58), calls=%async_computation | async-start | bytes 5505024 | tf_op jit(solution)/shard_map/all_to_all | solution.py:492
  30.5 60.0 %copy-start.5 = (f32[768]{0:T(1024)S(1)}, f32[768]{0:T(1024)}, u32[]{:S(2)}) copy-start(f32[768]{0:T(1024)} %param.21) | copy-start | bytes 9220
  30.5 61.3 %copy-start.3 = (f32[5,768]{1,0:T(8,128)S(1)}, f32[5,768]{1,0:T(8,128)}, u32[]{:S(2)}) copy-start(f32[5,768]{1,0:T(8,128)} %param.22) | copy-start | bytes 46084
  82.4 17.3 %all-to-all-start.1 = ((bf16[32,64,128]{2,1,0:T(8,128)(2,1)}), bf16[32,64,128]{2,1,0:T(8,128)(2,1)S(1)}, u32[]{:S(2)}, u32[]{:S(2)}) async-start(bf16[32,64,128]{2,1,0:T(8,128)(2,1)} %get-tuple-element.59), calls=%async_computation.1 | async-start | bytes 1048576 | tf_op jit(solution)/shard_map/all_to_all | solution.py:492
  90.4 429.7 %all-reduce.5.cloned.1.call-start = ((), (), s32[]{:S(2)}) async-start(), calls=%async_computation.10 | async-start | bytes 21282816 | tf_op jit(solution)/shard_map/psum | solution.py:874
  99.7 0.8 copy-start
  323.0 1.0 copy-start.2
  393.2 33.7 %all-to-all-start.7 = ((bf16[32,320,128]{2,1,0:T(8,128)(2,1)}), bf16[32,320,128]{2,1,0:T(8,128)(2,1)}, u32[]{:S(2)}, u32[]{:S(2)}) async-start(bf16[32,320,128]{2,1,0:T(8,128)(2,1)} %attend_back.3), calls=%async_computation.7 | async-start | bytes 5242880 | tf_op jit(solution)/shard_map/all_to_all | solution.py:492
  520.2 4.3 collective-permute-start
  527.7 34.0 %all-to-all-start.8 = ((bf16[64,112,128]{2,1,0:T(8,128)(2,1)}), bf16[64,112,128]{2,1,0:T(8,128)(2,1)S(1)}, u32[]{:S(2)}, u32[]{:S(2)}) async-start(bf16[64,112,128]{2,1,0:T(8,128)(2,1)} %bitcast.24), calls=%async_computation.8 | async-start | bytes 3670016 | tf_op jit(solution)/shard_map/all_to_all | solution.py:505
  542.7 6.9 %copy-start.1 = (bf16[784,768]{1,0:T(8,128)(2,1)S(1)}, bf16[784,768]{1,0:T(8,128)(2,1)}, u32[]{:S(2)}) copy-start(bf16[784,768]{1,0:T(8,128)(2,1)} %get-tuple-element.102) | copy-start | bytes 3612676
  592.3 5.8 collective-permute-start.1
Sparse Core Ops, SparseCore 0:
  323.1 196.9 all-reduce.4

commit v4 on v3

--- a/solution.py
+++ b/solution.py
@@ -16,7 +16,7 @@
 SLOT = ROWS + 64 + 16
 WIDTH = 768
 FF = 3072
-FF_BLOCK = 512
+FF_BLOCK = 1024
 EPS = 1e-5
 LOG2E = 1.4426950408889634
 LOW = -1e30
@@ -133,6 +133,21 @@
         if not self.started:
             self.flush()
         self.copy.wait()
+
+
+class KeptSlots(Kept):
+    def __init__(self, source, target, sems):
+        self.source = source
+        self.copies = [pltpu.make_async_copy(source.at[e], target.at[e], sems.at[w]) for w, e in SLOT_OF.items()]
+        self.started = True
+
+    def flush_head(self, head):
+        for half in range(2):
+            self.copies[2 * head + half].start()
+
+    def finish(self):
+        for copy in self.copies:
+            copy.wait()
 
 
 def project(stream, gain, w_qkv, odd, third, slots, normed_out):
@@ -156,6 +171,7 @@
                     64 * j : 64 * j + 64, block * HALF : (block + 1) * HALF
                 ]
                 slots[to, ROWS + 64 : SLOT, :] = jnp.broadcast_to(third, (16, 128)).astype(BF16)
+            slots.flush_head(head)
 
 
 def gather_heads(recv, odd, row, target):
@@ -261,29 +277,34 @@
     slots, normed = outs
     here = lax.axis_index("seq")
     third = third_start(start_of(pos, passes, count, here, ROWS - 1))
-    project(tokens[...].astype(F32), gain_attn[...], w_qkv, here % 2, third.astype(F32), slots, normed)
+    project(tokens[...].astype(F32), gain_attn[...].reshape(1, WIDTH), w_qkv, here % 2, third.astype(F32), slots, normed)
+
+
+def as_column(row):
+    return jnp.broadcast_to(row.astype(F32), (8, ROWS)).T[:, 0:1]
 
 
 def turn_kernel(info, passes, table, gain_attn, gain_mlp, ins, outs, features, acc):
     recv, tokens, w_out, w_up, w_down, w_qkv = ins
     slots, normed, second, att, mid, mid_normed, hidden, act = outs
     odd = info[3]
-    mix(recv, tokens[...].astype(F32), odd, gain_mlp[...], (w_out, w_up, w_down), features, acc, att, mid, mid_normed, hidden, act)
+    mix(recv, tokens[...].astype(F32), odd, gain_mlp[...].reshape(1, WIDTH), (w_out, w_up, w_down), features, acc, att, mid, mid_normed, hidden, act)
     for out in (att, mid, mid_normed, hidden, act):
         out.flush()
     stream = acc[...]
+    column = as_column(passes[...])
     for row in range(PASSES):
-        stream = stream + jnp.where(passes[...] == row, table[row : row + 1, :], 0.0)
+        stream = stream + jnp.where(column == row, table[row : row + 1, :], 0.0)
     second[...] = stream
     second.flush()
-    project(stream, gain_attn[...], w_qkv, odd, info[4].astype(F32), slots, normed)
+    project(stream, gain_attn[...].reshape(1, WIDTH), w_qkv, odd, info[4].astype(F32), slots, normed)
 
 
 def crest_kernel(info, gain_mlp, ins, outs, features, acc, mid, hidden, dz):
     recv, stream, w_out, w_up, w_down, cotangent = ins
     slots, mixed, att, mid_normed, act, dh, dy, dmid, gain_out = outs
     odd = info[3]
-    gain = gain_mlp[...]
+    gain = gain_mlp[...].reshape(1, WIDTH)
     mix(recv, stream[...], odd, gain, (w_out, w_up, w_down), features, acc, att, mid, mid_normed, hidden, act)
     mixed[...] = acc[...].astype(BF16)
     for out in (att, mid_normed, act, mixed):
@@ -298,13 +319,14 @@
     odd = info[3]
     small = jnp.zeros((16, WIDTH), F32)
     at = lax.broadcasted_iota(jnp.int32, (16, 1), 0)
-    grad = project_back(recv, odd, gain_attn[...], stream, grad_mid, w_qkv, features, dproj, gain_m)
+    grad = project_back(recv, odd, gain_attn[...].reshape(1, WIDTH), stream, grad_mid, w_qkv, features, dproj, gain_m)
     dproj.flush()
     small = jnp.where(at == PASSES, gain_m[...], small)
+    column = as_column(passes[...])
     for row in range(PASSES):
-        part = jnp.sum(jnp.where(passes[...] == row, grad, 0.0), axis=0, keepdims=True)
+        part = jnp.sum(jnp.where(column == row, grad, 0.0), axis=0, keepdims=True)
         small = jnp.where(at == row, part, small)
-    mix_back(grad, odd, gain_mlp[...], mid, hidden.ready(), (w_out, w_up, w_down), acc, dz, dh, dy, dmid, gain_m, slots)
+    mix_back(grad, odd, gain_mlp[...].reshape(1, WIDTH), mid, hidden.ready(), (w_out, w_up, w_down), acc, dz, dh, dy, dmid, gain_m, slots)
     slots.flush()
     small = jnp.where(at == PASSES + 1, gain_m[...] + gain_m_two[...], small)
     weight_gradients(
@@ -316,7 +338,7 @@
 def leave_kernel(info, gain_attn, ins, outs, features):
     recv, w_qkv, tokens, grad_mid = ins
     grad_tokens, dproj, gain_out = outs
-    grad_tokens[...] = project_back(recv, info[3], gain_attn[...], tokens, grad_mid, w_qkv, features, dproj, gain_out)
+    grad_tokens[...] = project_back(recv, info[3], gain_attn[...].reshape(1, WIDTH), tokens, grad_mid, w_qkv, features, dproj, gain_out)
 
 
 def shape(*dims, dtype=BF16):
@@ -341,12 +363,14 @@
                 held.append(HeldBlocks(far[i], near[i], own, split[i]))
                 blocks.append(held[-1])
                 if len(blocks) == 2:
-                    for c in range(6):
+                    for c in range(FF // FF_BLOCK):
                         for one in blocks:
                             one.copy(c).start()
             else:
                 held.append(Held(far[i], near[i], sems.at[i]))
         kept = [Kept(near[i], far[i], sems.at[i]) for i in range(ins, count)]
+        if outs[0].shape == (SEQ, SLOT, 128):
+            kept[0] = KeptSlots(near[ins], far[ins], sems.at[pl.ds(count + 12, 24)])
         kernel(*known, *few, held, kept, *rest)
         for one in kept:
             if not one.started:
@@ -362,7 +386,7 @@
         in_specs=[pl.BlockSpec(memory_space=pltpu.SMEM)] * len(info) + [vmem] * len(small) + [hbm] * ins,
         out_specs=(hbm,) * len(outs),
         scratch_shapes=[pltpu.VMEM(x.shape, x.dtype) for x in (*arrays, *outs)]
-        + [pltpu.SemaphoreType.DMA((count + 12,))]
+        + [pltpu.SemaphoreType.DMA((count + 36,))]
         + scratch,
         compiler_params=pltpu.CompilerParams(vmem_limit_bytes=62 << 20),
         cost_estimate=pl.CostEstimate(flops=int(flops), bytes_accessed=16 << 20, transcendentals=1 << 20),
@@ -816,9 +840,9 @@
     active = (place < 3).astype(jnp.int32)
     core = lax.axis_index("batch") % 2
     info = jnp.stack([active, (3 * group + place) % 2, second, here % 2, third, core])
-    passes = token_pass[0][:, None]
+    passes = token_pass
     table = jnp.pad(pass_table, ((0, 8 - PASSES), (0, 0)))
-    gain_a, gain_m = gain_attn[None], gain_mlp[None]
+    gain_a, gain_m = gain_attn, gain_mlp
     stream_one = tokens[0]
     features = pltpu.VMEM((WIDTH, ROWS), BF16)
     acc = pltpu.VMEM((ROWS, WIDTH), F32)
@@ -831,7 +855,9 @@
     slots, normed_one = in_vmem(
         enter_kernel, "enter", documents, (gain_a,), (stream_one, w_qkv), (sent, square), [], 1e9
     )
-    saved_one = attend(info, exchange(slots))
+    recv = exchange(slots)
+    recv, passes, table, gain_m = lax.optimization_barrier((recv, passes, table, gain_m))
+    saved_one = attend(info, recv)
     slots, normed_two, stream_two, att_one, mid_one, midn_one, hidden_one, act_one = in_vmem(
         turn_kernel,
         "turn",

time: 618 us -> 610 us (0.987)
  blocking collectives: 143 us -> 161 us
  waiting for transfers between devices: 149 us -> 140 us
  starting transfers between devices: 33 us -> 25 us
    all_to_all x5 -> x6, blocking collectives: 113 us -> 131 us  [exchange(): return lax.all_to_all(slots, 'seq', 0, 0)]
    all_to_all x3 -> x2, waiting for transfers between devices: 56.9 us -> 48.6 us  [exchange(): return lax.all_to_all(slots, 'seq', 0, 0)]
    all_to_all x3 -> x2, starting transfers between devices: 22.3 us -> 14.3 us  [exchange(): return lax.all_to_all(slots, 'seq', 0, 0)]
  transfers between devices with their start and end apart: 7 -> 6, of which waited for: 7 -> 6; matrix products, arithmetic and copies ran while one was open for 4% -> 4% of each run, Pallas kernels for 12% -> 13%
where the time goes in v4:
time: 610 us; the launch traced here: 602 us
  Pallas kernels  232 us (38%)
  blocking collectives  161 us (26%)
  waiting for transfers between devices  140 us (23%)
  starting transfers between devices  25 us (4%)
  other arithmetic  20.6 us (3%)
  between operations  18.4 us (3%)
    all_to_all x6, blocking collectives, exchange(): return lax.all_to_all(slots, 'seq', 0, 0)  131 us
    pallas_call x2, Pallas kernels, attend_back(): pl.pallas_call(functools.partial(attend_back_kernel, devs=devs), out_shap...  105 us
    pallas_call x7, Pallas kernels, in_vmem(): pl.pallas_call(body, out_shape=tuple(outs), in_specs=[pl.BlockSpec(memory...  76.5 us
    psum x1, waiting for transfers between devices, on_device(): early = lax.psum(tuple(early), ('seq', 'batch'))  75.2 us
    all_to_all x2, waiting for transfers between devices, exchange(): return lax.all_to_all(slots, 'seq', 0, 0)  48.6 us
    pallas_call x2, Pallas kernels, attend(): pl.pallas_call(functools.partial(attend_kernel, devs=devs), out_shape=(ja...  47.6 us
    all_to_all x1, blocking collectives, across_chips(): lax.all_to_all(slots, ('seq', 'batch'), 0, 0, axis_index_groups=groups)  30.1 us
    all_to_all x2, starting transfers between devices, exchange(): return lax.all_to_all(slots, 'seq', 0, 0)  14.3 us
  transfers between devices with their start and end apart: 6, of which 6 were waited for; matrix products, arithmetic and copies ran while one was open for 4% of the time, Pallas kernels for 13%

profile of v4, /device:TPU:1, one launch (start us, length us, event | category | flops | bytes accessed | tf_op | source)
XLA Modules:
  0.0 602.5 jit_solution(610068547416743133)
XLA Ops:
  7.2 6.2 %enter.1 = (bf16[32,336,128]{2,1,0:T(8,128)(2,1)}, bf16[256,768]{1,0:T(8,128)(2,1)}) custom-call(s32[1,256]{1,0:T(1,128)} %refs_0_.1, s32[1,256]{1,0:T(1,128)} %refs_1_.5, s32[1,256]{1,0:T(1,128)} %refs_2_.2, f32[768]{0:T(1024)} %refs_1_.6, bf16[256,768]{1,0:T(8,128)(2,1)} %bitcast.24, bf16[768,2304]{1,0:T(8,128)(2,1)} %refs_3_.6), custom_call_target="tpu_custom_call" | custom-call | flops 1000000000 | bytes 16777216 | tf_op jit(solution)/shard_map/enter/pallas_call | solution.py:383
  13.4 9.5 %all-to-all-start = ((bf16[32,336,128]{2,1,0:T(8,128)(2,1)}), bf16[32,336,128]{2,1,0:T(8,128)(2,1)}, u32[]{:S(2)}, u32[]{:S(2)}) async-start(bf16[32,336,128]{2,1,0:T(8,128)(2,1)} %get-tuple-element.62), calls=%async_computation | async-start | bytes 5505024 | tf_op jit(solution)/shard_map/all_to_all | solution.py:516
  29.4 27.4 %all-to-all-done.recv_far = bf16[32,336,128]{2,1,0:T(8,128)(2,1)} async-done(((bf16[32,336,128]{2,1,0:T(8,128)(2,1)}), bf16[32,336,128]{2,1,0:T(8,128)(2,1)}, u32[]{:S(2)}, u32[]{:S(2)}) %all-to-all-start) | async-done | bytes 2752544 | tf_op jit(solution)/shard_map/all_to_all | solution.py:516
  56.8 23.8 %attend.2 = (bf16[32,64,128]{2,1,0:T(8,128)(2,1)}, f32[64,4096]{1,0:T(8,128)}, f32[1,4096]{1,0:T(1,128)}, bf16[64,8192]{1,0:T(8,128)(2,1)}, bf16[128,4096]{1,0:T(8,128)(2,1)}) custom-call(s32[6]{0:T(128)} %stack.31.info.refs_0_, bf16[32,336,128]{2,1,0:T(8,128)(2,1)} %all-to-all-done.recv_far), custom_call_target="tpu_custom_call" | custom-call | flops 18227200000 | bytes 8388608 | tf_op jit(solution)/shard_map/attend/pallas_call | solution.py:675
  80.6 17.6 %all_to_all.50.refs_5_ = bf16[32,64,128]{2,1,0:T(8,128)(2,1)} all-to-all(bf16[32,64,128]{2,1,0:T(8,128)(2,1)} %get-tuple-element.67), channel_id=1, replica_groups=mesh['seq'=32,'batch'=4] {'seq'}, dimensions={0} | all-to-all | bytes 1048576 | tf_op jit(solution)/shard_map/all_to_all | solution.py:516
  98.2 10.9 %turn.1 = (bf16[32,336,128]{2,1,0:T(8,128)(2,1)}, bf16[256,768]{1,0:T(8,128)(2,1)}, f32[256,768]{1,0:T(8,128)}, bf16[256,768]{1,0:T(8,128)(2,1)}, f32[256,768]{1...) custom-call(s32[6]{0:T(128)} %stack.31.info.refs_0_, s32[1,256]{1,0:T(1,128)} %refs_1_.5, ...), custom_call_target="tpu_custom_call" | custom-call | flops 3600000000 | bytes 16777216 | tf_op jit(solution)/shard_map/turn/pallas_call | solution.py:383
  109.1 36.6 %all_to_all.51.recv_far = bf16[32,336,128]{2,1,0:T(8,128)(2,1)} all-to-all(bf16[32,336,128]{2,1,0:T(8,128)(2,1)} %get-tuple-element.68), channel_id=1, replica_groups=mesh['seq'=32,'batch'=4] {'seq'}, dimensions={0} | all-to-all | bytes 5505024 | tf_op jit(solution)/shard_map/all_to_all | solution.py:516
  145.7 23.8 %attend.3 = (bf16[32,64,128]{2,1,0:T(8,128)(2,1)}, f32[64,4096]{1,0:T(8,128)}, f32[1,4096]{1,0:T(1,128)}, bf16[64,8192]{1,0:T(8,128)(2,1)}, bf16[128,4096]{1,0:T(8,128)(2,1)}) custom-call(s32[6]{0:T(128)} %stack.31.info.refs_0_, bf16[32,336,128]{2,1,0:T(8,128)(2,1)} %all_to_all.51.recv_far), custom_call_target="tpu_custom_call" | custom-call | flops 18227200000 | bytes 8388608 | tf_op jit(solution)/shard_map/attend/pallas_call | solution.py:675
  169.5 14.2 %all_to_all.52.refs_2_ = bf16[32,64,128]{2,1,0:T(8,128)(2,1)} all-to-all(bf16[32,64,128]{2,1,0:T(8,128)(2,1)} %get-tuple-element.69), channel_id=1, replica_groups=mesh['seq'=32,'batch'=4] {'seq'}, dimensions={0} | all-to-all | bytes 1048576 | tf_op jit(solution)/shard_map/all_to_all | solution.py:516
  183.7 13.6 %crest.1 = (bf16[32,64,128]{2,1,0:T(8,128)(2,1)}, bf16[256,768]{1,0:T(8,128)(2,1)}, bf16[256,768]{1,0:T(8,128)(2,1)}, bf16[256,768]{1,0:T(8,128)(2,1)}, bf16[256...) custom-call(s32[6]{0:T(128)} %stack.31.info.refs_0_, ...), custom_call_target="tpu_custom_call" | custom-call | flops 5000000000 | bytes 16777216 | tf_op jit(solution)/shard_map/crest/pallas_call | solution.py:383
  197.3 13.6 %all_to_all.53.grad_out_far = bf16[32,64,128]{2,1,0:T(8,128)(2,1)} all-to-all(bf16[32,64,128]{2,1,0:T(8,128)(2,1)} %get-tuple-element.81), channel_id=1, replica_groups=mesh['seq'=32,'batch'=4] {'seq'}, dimensions={0} | all-to-all | bytes 1048576 | tf_op jit(solution)/shard_map/all_to_all | solution.py:516
  210.9 52.2 %attend_back.2 = bf16[32,320,128]{2,1,0:T(8,128)(2,1)} custom-call(s32[6]{0:T(128)} %stack.31.info.refs_0_, bf16[32,336,128]{2,1,0:T(8,128)(2,1)} %all_to_all.51.recv_far, bf16[64,8192]{1,0:T(8,128)(2,1)} %get-tuple-element.77.kv_t_far, bf16[128,4096]{1,0:T(8,128)(2,1)} %get-tuple-element.78.q_t_far, f32[64,4096]{1,0:T(8,128)} %get-tuple-element.79.out_f_far, ...), custom_call_target="tpu_custom_call" | custom-call | flops 18227200000 | bytes 8388608 | tf_op jit(solution)/shard_map/attend_back/pallas_call | solution.py:793
  263.1 31.9 %all_to_all.54.refs_5_ = bf16[32,320,128]{2,1,0:T(8,128)(2,1)} all-to-all(bf16[32,320,128]{2,1,0:T(8,128)(2,1)} %attend_back.2), channel_id=1, replica_groups=mesh['seq'=32,'batch'=4] {'seq'}, dimensions={0} | all-to-all | bytes 5242880 | tf_op jit(solution)/shard_map/all_to_all | solution.py:516
  295.0 22.1 %return.1 = (bf16[32,64,128]{2,1,0:T(8,128)(2,1)}, bf16[256,2304]{1,0:T(8,128)(2,1)}, f32[256,768]{1,0:T(8,128)}, bf16[768,3072]{1,0:T(8,128)(2,1)}, bf16[3072,7...) custom-call(s32[6]{0:T(128)} %stack.31.info.refs_0_, s32[1,256]{1,0:T(1,128)} %refs_1_.5, f32[768]{0:T(1024)} %refs_1_.6, ...), custom_call_target="tpu_custom_call" | custom-call | flops 10000000000 | bytes 16777216 | tf_op jit(solution)/shard_map/return/pallas_call | solution.py:383
  318.1 16.8 %all_to_all.55.grad_out_far = bf16[32,64,128]{2,1,0:T(8,128)(2,1)} all-to-all(bf16[32,64,128]{2,1,0:T(8,128)(2,1)S(1)} %copy-done.1), channel_id=1, replica_groups=mesh['seq'=32,'batch'=4] {'seq'}, dimensions={0} | all-to-all | bytes 1048576 | tf_op jit(solution)/shard_map/all_to_all | solution.py:516
  334.9 52.5 %attend_back.3 = bf16[32,320,128]{2,1,0:T(8,128)(2,1)} custom-call(s32[6]{0:T(128)} %stack.31.info.refs_0_, bf16[32,336,128]{2,1,0:T(8,128)(2,1)} %all-to-all-done.recv_far, bf16[64,8192]{1,0:T(8,128)(2,1)} %get-tuple-element.72.kv_t_far, bf16[128,4096]{1,0:T(8,128)(2,1)} %get-tuple-element.73.q_t_far, f32[64,4096]{1,0:T(8,128)} %get-tuple-element.74.out_f_far, ...), custom_call_target="tpu_custom_call" | custom-call | flops 18227200000 | bytes 8388608 | tf_op jit(solution)/shard_map/attend_back/pallas_call | solution.py:793
  387.4 4.8 all-to-all-start.7
  392.3 7.6 %grad_qkv_two.1.refs_4_ = f32[18,768,128]{2,1,0:T(8,128)} custom-call(s32[6]{0:T(128)} %stack.31.info.refs_0_, bf16[256,768]{1,0:T(8,128)(2,1)} %get-tuple-element.99.refs_1_, bf16[256,2304]{1,0:T(8,128)(2,1)} %get-tuple-element.100.refs_2_), custom_call_target="tpu_custom_call" | custom-call | flops 900000000 | bytes 16777216 | tf_op jit(solution)/shard_map/grad_qkv_two/pallas_call | solution.py:383
  399.8 21.2 %all-to-all-done.7.refs_2_ = bf16[32,320,128]{2,1,0:T(8,128)(2,1)} async-done(((bf16[32,320,128]{2,1,0:T(8,128)(2,1)}), bf16[32,320,128]{2,1,0:T(8,128)(2,1)}, u32[]{:S(2)}, u32[]{:S(2)}) %all-to-all-start.7) | async-done | bytes 2621472 | tf_op jit(solution)/shard_map/all_to_all | solution.py:516
  421.1 6.9 %leave.1 = (f32[256,768]{1,0:T(8,128)}, bf16[256,2304]{1,0:T(8,128)(2,1)}, f32[1,768]{1,0:T(1,128)}) custom-call(s32[6]{0:T(128)} %stack.31.info.refs_0_, f32[768]{0:T(1024)} %refs_1_.6, bf16[32,320,128]{2,1,0:T(8,128)(2,1)} %all-to-all-done.7.refs_2_, bf16[768,2304]{1,0:T(8,128)(2,1)} %refs_3_.6, bf16[256,768]{1,0:T(8,128)(2,1)} %bitcast.26, ...), custom_call_target="tpu_custom_call" | custom-call | flops 1000000000 | bytes 16777216 | tf_op jit(solution)/shard_map/leave/pallas_call | solution.py:383
  429.3 9.3 %grad_qkv.1 = (bf16[7168,128]{1,0:T(8,128)(2,1)}, bf16[7168,128]{1,0:T(8,128)(2,1)}) custom-call(s32[6]{0:T(128)} %stack.31.info.refs_0_, f32[16,128]{1,0:T(8,128)} %pad.9.refs_1_, bf16[256,768]{1,0:T(8,128)(2,1)} %get-tuple-element.97.refs_2_, bf16[256,2304]{1,0:T(8,128)(2,1)} %get-tuple-element.98.refs_3_, f32[18,768,128]{2,1,0:T(8,128)} %grad_qkv_two.1.refs_4_), custom_call_target="tpu_custom_call" | custom-call | flops 900000000 | bytes 16777216 | tf_op jit(solution)/shard_map/grad_qkv/pallas_call | solution.py:383
  438.6 75.2 %all-reduce.5.cloned.1.call-done = (bf16[768,3072]{1,0:T(8,128)(2,1)}, bf16[3072,768]{1,0:T(8,128)(2,1)}, bf16[784,768]{1,0:T(8,128)(2,1)}) async-done(((bf16[768,3072]{1,0:T(8,128)(2,1)}, bf16[3072,768]{1,0:T(8,128)(2,1)}, bf16[784,768]{1,0:T(8,128)(2,1)}), (bf16[768,3072]{1,0:T(8,128)(2,1)}, bf16[3072,768]{1,0:T(8,128)(2,1)}, bf16[784,768]{1,0:T(8,128)(2,1)})) %all-reduce.5.cloned.1.call-update) | async-done | bytes 10641424 | tf_op jit(solution)/shard_map/psum | solution.py:900
  514.6 3.6 collective-permute-done
  518.2 3.2 add_convert_fusion
  521.4 7.6 %all-to-all-start.8 = ((bf16[64,112,128]{2,1,0:T(8,128)(2,1)}), bf16[64,112,128]{2,1,0:T(8,128)(2,1)S(1)}, u32[]{:S(2)}, u32[]{:S(2)}) async-start(bf16[64,112,128]{2,1,0:T(8,128)(2,1)} %bitcast.23), calls=%async_computation.8 | async-start | bytes 3670016 | tf_op jit(solution)/shard_map/all_to_all | solution.py:529
  529.0 7.4 %convert_element_type.37 = f32[768,3072]{1,0:T(8,128)} convert(bf16[768,3072]{1,0:T(8,128)(2,1)} %get-tuple-element.108) | non-fusion elementwise | flops 2359296 | bytes 14155776 | tf_op jit(solution)/shard_map/convert_element_type | solution.py:936
  536.4 6.9 %convert_element_type.38 = f32[3072,768]{1,0:T(8,128)} convert(bf16[3072,768]{1,0:T(8,128)(2,1)} %get-tuple-element.109) | non-fusion elementwise | flops 2359296 | bytes 14155776 | tf_op jit(solution)/shard_map/convert_element_type | solution.py:936
  544.9 10.5 %all-to-all-done.8 = bf16[64,112,128]{2,1,0:T(8,128)(2,1)S(1)} async-done(((bf16[64,112,128]{2,1,0:T(8,128)(2,1)}), bf16[64,112,128]{2,1,0:T(8,128)(2,1)S(1)}, u32[]{:S(2)}, u32[]{:S(2)}) %all-to-all-start.8) | async-done | bytes 1835040 | tf_op jit(solution)/shard_map/all_to_all | solution.py:529
  555.9 30.1 %all_to_all.56 = bf16[64,112,128]{2,1,0:T(8,128)(2,1)S(1)} all-to-all(bf16[64,112,128]{2,1,0:T(8,128)(2,1)S(1)} %broadcast_in_dim.14), channel_id=1, replica_groups={{0,2,4,6,8,10,12,14,16,18,20,22,24,26,28,30,32,34,36,38,40,42,44,46,48,..., dimensions={0} | all-to-all | bytes 3670016 | tf_op jit(solution)/shard_map/all_to_all | solution.py:529
  586.0 2.4 collective-permute-start.1
  590.2 1.6 collective-permute-done.1.other
  591.8 3.7 widen.1
  (28 shorter events, 9.5 us)
Async XLA Ops:
  13.3 9.6 %copy-start.4 = (s32[1,256]{1,0:T(1,128)S(1)}, s32[1,256]{1,0:T(1,128)}, u32[]{:S(2)}) copy-start(s32[1,256]{1,0:T(1,128)} %refs_0_.1) | copy-start | bytes 3076
  13.4 10.2 %copy-start.3 = (s32[1,256]{1,0:T(1,128)S(1)}, s32[1,256]{1,0:T(1,128)}, u32[]{:S(2)}) copy-start(s32[1,256]{1,0:T(1,128)} %refs_1_.5) | copy-start | bytes 3076
  13.4 10.2 %copy-start.5 = (s32[1,256]{1,0:T(1,128)S(1)}, s32[1,256]{1,0:T(1,128)}, u32[]{:S(2)}) copy-start(s32[1,256]{1,0:T(1,128)} %refs_2_.2) | copy-start | bytes 3076
  13.4 14.7 %copy-start.2 = (f32[5,768]{1,0:T(8,128)S(1)}, f32[5,768]{1,0:T(8,128)}, u32[]{:S(2)}) copy-start(f32[5,768]{1,0:T(8,128)} %param.22) | copy-start | bytes 46084
  13.4 43.4 %all-to-all-start = ((bf16[32,336,128]{2,1,0:T(8,128)(2,1)}), bf16[32,336,128]{2,1,0:T(8,128)(2,1)}, u32[]{:S(2)}, u32[]{:S(2)}) async-start(bf16[32,336,128]{2,1,0:T(8,128)(2,1)} %get-tuple-element.62), calls=%async_computation | async-start | bytes 5505024 | tf_op jit(solution)/shard_map/all_to_all | solution.py:516
  22.9 491.0 %all-reduce.5.cloned.1.call-start = ((), (), s32[]{:S(2)}) async-start(), calls=%async_computation.10 | async-start | bytes 21282816 | tf_op jit(solution)/shard_map/psum | solution.py:900
  317.1 1.0 copy-start.1
  387.4 33.6 %all-to-all-start.7 = ((bf16[32,320,128]{2,1,0:T(8,128)(2,1)}), bf16[32,320,128]{2,1,0:T(8,128)(2,1)}, u32[]{:S(2)}, u32[]{:S(2)}) async-start(bf16[32,320,128]{2,1,0:T(8,128)(2,1)} %attend_back.3), calls=%async_computation.7 | async-start | bytes 5242880 | tf_op jit(solution)/shard_map/all_to_all | solution.py:516
  513.8 4.3 collective-permute-start
  521.4 34.0 %all-to-all-start.8 = ((bf16[64,112,128]{2,1,0:T(8,128)(2,1)}), bf16[64,112,128]{2,1,0:T(8,128)(2,1)S(1)}, u32[]{:S(2)}, u32[]{:S(2)}) async-start(bf16[64,112,128]{2,1,0:T(8,128)(2,1)} %bitcast.23), calls=%async_computation.8 | async-start | bytes 3670016 | tf_op jit(solution)/shard_map/all_to_all | solution.py:529
  536.4 6.9 %copy-start = (bf16[784,768]{1,0:T(8,128)(2,1)S(1)}, bf16[784,768]{1,0:T(8,128)(2,1)}, u32[]{:S(2)}) copy-start(bf16[784,768]{1,0:T(8,128)(2,1)} %get-tuple-element.110) | copy-start | bytes 3612676
  586.0 5.8 collective-permute-start.1
Sparse Core Ops, SparseCore 0:
  317.2 196.5 all-reduce.4

commit v5 on v4

--- a/solution.py
+++ b/solution.py
@@ -133,6 +133,20 @@
         if not self.started:
             self.flush()
         self.copy.wait()
+
+
+class KeptBlocks(Kept):
+    def __init__(self, source, target, sems):
+        self.source, self.target, self.sems = source, target, sems
+        self.started = True
+
+    def copy_of(self, c):
+        here = pl.ds(c * 512 if isinstance(c, int) else pl.multiple_of(c * 512, 512), 512)
+        return pltpu.make_async_copy(self.source.at[here], self.target.at[here], self.sems.at[c])
+
+    def finish(self):
+        for c in range(FF // 512):
+            self.copy_of(c).wait()
 
 
 class KeptSlots(Kept):
@@ -371,6 +385,9 @@
         kept = [Kept(near[i], far[i], sems.at[i]) for i in range(ins, count)]
         if outs[0].shape == (SEQ, SLOT, 128):
             kept[0] = KeptSlots(near[ins], far[ins], sems.at[pl.ds(count + 12, 24)])
+        for i, out in enumerate(outs):
+            if out.shape == (FF, WIDTH):
+                kept[i] = KeptBlocks(near[ins + i], far[ins + i], sems.at[pl.ds(count + 12, 6)])
         kernel(*known, *few, held, kept, *rest)
         for one in kept:
             if not one.started:
@@ -415,18 +432,19 @@
 
     lax.fori_loop(0, 6, step_up, 0)
     up.flush()
+    dy = jnp.concatenate([dy_one[...], dy_two[...]], axis=0)
+    out[0:WIDTH, :] = dot(left(att_one[...], att_two[...]), dy).astype(BF16)
+    out[WIDTH:, :] = small.astype(BF16)
+    out.flush()
     dz = jnp.concatenate([dz_one[...], dz_two[...]], axis=0)
 
     def step_down(c, _):
         here = pl.ds(pl.multiple_of(c * 512, 512), 512)
         down[here, :] = dot(left(act_one[:, here], act_two[:, here]), dz).astype(BF16)
+        down.copy_of(c).start()
         return 0
 
     lax.fori_loop(0, 6, step_down, 0)
-    down.flush()
-    dy = jnp.concatenate([dy_one[...], dy_two[...]], axis=0)
-    out[0:WIDTH, :] = dot(left(att_one[...], att_two[...]), dy).astype(BF16)
-    out[WIDTH:, :] = small.astype(BF16)
 
 
 def grad_qkv_kernel(info, ins, outs):
@@ -601,11 +619,22 @@
                 acc[:, here] = acc[:, here] + dot(kv_t[64:144, key_rows], weights.astype(BF16))
 
             def step(j, _):
-                kv = recv[pl.ds(j * 4, 4), 0:ROWS, :].reshape(1024, 128)
-                update(kv, pl.ds(pl.multiple_of(j * 1024, 1024), 1024), 0, None)
+                def scores(c, k):
+                    kv = recv[pl.ds(j * 8 + k * 2, 2), 0:ROWS, :].reshape(512, 128)
+                    return dot(kv, queries[:, c : c + 1024])
+
+                pieces = [(c, k) for c in range(0, tile_rows, 1024) for k in range(4)]
+                ahead = scores(*pieces[0])
+                for n, (c, k) in enumerate(pieces):
+                    now, ahead = ahead, scores(*pieces[n + 1]) if n + 1 < len(pieces) else None
+                    keys = pl.ds(pl.multiple_of(j * 2048 + k * 512, 512), 512)
+                    part = dot(kv_t[64:144, keys], jnp.exp2(now * LOG2E).astype(BF16))
+                    total = part if k == 0 else total + part
+                    if k == 3:
+                        acc[:, c : c + 1024] += total
                 return 0
 
-            lax.fori_loop(0, t * (span // 1024), step, 0)
+            lax.fori_loop(0, t, step, 0)
             acc[...] = jnp.where(first >= start, 0.0, acc[...])
             for i in range(devs // 2):
                 left = 256 * i

time: 610 us -> 608 us (level)
  no operation moved by 1% of the time
where the time goes in v5:
time: 608 us; the launch traced here: 600 us
  Pallas kernels  230 us (38%)
  blocking collectives  161 us (26%)
  waiting for transfers between devices  140 us (23%)
  starting transfers between devices  25.1 us (4%)
  other arithmetic  20.6 us (3%)
  between operations  18.7 us (3%)
    all_to_all x6, blocking collectives, exchange(): return lax.all_to_all(slots, 'seq', 0, 0)  131 us
    pallas_call x2, Pallas kernels, attend_back(): pl.pallas_call(functools.partial(attend_back_kernel, devs=devs), out_shap...  105 us
    pallas_call x7, Pallas kernels, in_vmem(): pl.pallas_call(body, out_shape=tuple(outs), in_specs=[pl.BlockSpec(memory...  75.8 us
    psum x1, waiting for transfers between devices, on_device(): early = lax.psum(tuple(early), ('seq', 'batch'))  75.5 us
    all_to_all x2, waiting for transfers between devices, exchange(): return lax.all_to_all(slots, 'seq', 0, 0)  48.4 us
    pallas_call x2, Pallas kernels, attend(): pl.pallas_call(functools.partial(attend_kernel, devs=devs), out_shape=(ja...  45.8 us
    all_to_all x1, blocking collectives, across_chips(): lax.all_to_all(slots, ('seq', 'batch'), 0, 0, axis_index_groups=groups)  30.1 us
    all_to_all x2, starting transfers between devices, exchange(): return lax.all_to_all(slots, 'seq', 0, 0)  14.3 us
  transfers between devices with their start and end apart: 6, of which 6 were waited for; matrix products, arithmetic and copies ran while one was open for 4% of the time, Pallas kernels for 13%

profile of v5, /device:TPU:1, one launch (start us, length us, event | category | flops | bytes accessed | tf_op | source)
XLA Modules:
  0.0 600.3 jit_solution(7620920530305905783)
XLA Ops:
  7.2 6.2 %enter.1 = (bf16[32,336,128]{2,1,0:T(8,128)(2,1)}, bf16[256,768]{1,0:T(8,128)(2,1)}) custom-call(s32[1,256]{1,0:T(1,128)} %refs_0_.1, s32[1,256]{1,0:T(1,128)} %refs_1_.5, s32[1,256]{1,0:T(1,128)} %refs_2_.2, f32[768]{0:T(1024)} %refs_1_.6, bf16[256,768]{1,0:T(8,128)(2,1)} %bitcast.24, bf16[768,2304]{1,0:T(8,128)(2,1)} %refs_3_.6), custom_call_target="tpu_custom_call" | custom-call | flops 1000000000 | bytes 16777216 | tf_op jit(solution)/shard_map/enter/pallas_call | solution.py:400
  13.4 9.5 %all-to-all-start = ((bf16[32,336,128]{2,1,0:T(8,128)(2,1)}), bf16[32,336,128]{2,1,0:T(8,128)(2,1)}, u32[]{:S(2)}, u32[]{:S(2)}) async-start(bf16[32,336,128]{2,1,0:T(8,128)(2,1)} %get-tuple-element.62), calls=%async_computation | async-start | bytes 5505024 | tf_op jit(solution)/shard_map/all_to_all | solution.py:534
  29.4 27.4 %all-to-all-done.recv_far = bf16[32,336,128]{2,1,0:T(8,128)(2,1)} async-done(((bf16[32,336,128]{2,1,0:T(8,128)(2,1)}), bf16[32,336,128]{2,1,0:T(8,128)(2,1)}, u32[]{:S(2)}, u32[]{:S(2)}) %all-to-all-start) | async-done | bytes 2752544 | tf_op jit(solution)/shard_map/all_to_all | solution.py:534
  56.8 22.9 %attend.2 = (bf16[32,64,128]{2,1,0:T(8,128)(2,1)}, f32[64,4096]{1,0:T(8,128)}, f32[1,4096]{1,0:T(1,128)}, bf16[64,8192]{1,0:T(8,128)(2,1)}, bf16[128,4096]{1,0:T(8,128)(2,1)}) custom-call(s32[6]{0:T(128)} %stack.31.info.refs_0_, bf16[32,336,128]{2,1,0:T(8,128)(2,1)} %all-to-all-done.recv_far), custom_call_target="tpu_custom_call" | custom-call | flops 18227200000 | bytes 8388608 | tf_op jit(solution)/shard_map/attend/pallas_call | solution.py:704
  79.7 17.9 %all_to_all.50.refs_5_ = bf16[32,64,128]{2,1,0:T(8,128)(2,1)} all-to-all(bf16[32,64,128]{2,1,0:T(8,128)(2,1)} %get-tuple-element.67), channel_id=1, replica_groups=mesh['seq'=32,'batch'=4] {'seq'}, dimensions={0} | all-to-all | bytes 1048576 | tf_op jit(solution)/shard_map/all_to_all | solution.py:534
  97.6 10.9 %turn.1 = (bf16[32,336,128]{2,1,0:T(8,128)(2,1)}, bf16[256,768]{1,0:T(8,128)(2,1)}, f32[256,768]{1,0:T(8,128)}, bf16[256,768]{1,0:T(8,128)(2,1)}, f32[256,768]{1...) custom-call(s32[6]{0:T(128)} %stack.31.info.refs_0_, s32[1,256]{1,0:T(1,128)} %refs_1_.5, ...), custom_call_target="tpu_custom_call" | custom-call | flops 3600000000 | bytes 16777216 | tf_op jit(solution)/shard_map/turn/pallas_call | solution.py:400
  108.5 36.6 %all_to_all.51.recv_far = bf16[32,336,128]{2,1,0:T(8,128)(2,1)} all-to-all(bf16[32,336,128]{2,1,0:T(8,128)(2,1)} %get-tuple-element.68), channel_id=1, replica_groups=mesh['seq'=32,'batch'=4] {'seq'}, dimensions={0} | all-to-all | bytes 5505024 | tf_op jit(solution)/shard_map/all_to_all | solution.py:534
  145.1 22.9 %attend.3 = (bf16[32,64,128]{2,1,0:T(8,128)(2,1)}, f32[64,4096]{1,0:T(8,128)}, f32[1,4096]{1,0:T(1,128)}, bf16[64,8192]{1,0:T(8,128)(2,1)}, bf16[128,4096]{1,0:T(8,128)(2,1)}) custom-call(s32[6]{0:T(128)} %stack.31.info.refs_0_, bf16[32,336,128]{2,1,0:T(8,128)(2,1)} %all_to_all.51.recv_far), custom_call_target="tpu_custom_call" | custom-call | flops 18227200000 | bytes 8388608 | tf_op jit(solution)/shard_map/attend/pallas_call | solution.py:704
  168.0 14.1 %all_to_all.52.refs_2_ = bf16[32,64,128]{2,1,0:T(8,128)(2,1)} all-to-all(bf16[32,64,128]{2,1,0:T(8,128)(2,1)} %get-tuple-element.69), channel_id=1, replica_groups=mesh['seq'=32,'batch'=4] {'seq'}, dimensions={0} | all-to-all | bytes 1048576 | tf_op jit(solution)/shard_map/all_to_all | solution.py:534
  182.1 13.6 %crest.1 = (bf16[32,64,128]{2,1,0:T(8,128)(2,1)}, bf16[256,768]{1,0:T(8,128)(2,1)}, bf16[256,768]{1,0:T(8,128)(2,1)}, bf16[256,768]{1,0:T(8,128)(2,1)}, bf16[256...) custom-call(s32[6]{0:T(128)} %stack.31.info.refs_0_, ...), custom_call_target="tpu_custom_call" | custom-call | flops 5000000000 | bytes 16777216 | tf_op jit(solution)/shard_map/crest/pallas_call | solution.py:400
  195.7 13.6 %all_to_all.53.grad_out_far = bf16[32,64,128]{2,1,0:T(8,128)(2,1)} all-to-all(bf16[32,64,128]{2,1,0:T(8,128)(2,1)} %get-tuple-element.81), channel_id=1, replica_groups=mesh['seq'=32,'batch'=4] {'seq'}, dimensions={0} | all-to-all | bytes 1048576 | tf_op jit(solution)/shard_map/all_to_all | solution.py:534
  209.3 52.2 %attend_back.2 = bf16[32,320,128]{2,1,0:T(8,128)(2,1)} custom-call(s32[6]{0:T(128)} %stack.31.info.refs_0_, bf16[32,336,128]{2,1,0:T(8,128)(2,1)} %all_to_all.51.recv_far, bf16[64,8192]{1,0:T(8,128)(2,1)} %get-tuple-element.77.kv_t_far, bf16[128,4096]{1,0:T(8,128)(2,1)} %get-tuple-element.78.q_t_far, f32[64,4096]{1,0:T(8,128)} %get-tuple-element.79.out_f_far, ...), custom_call_target="tpu_custom_call" | custom-call | flops 18227200000 | bytes 8388608 | tf_op jit(solution)/shard_map/attend_back/pallas_call | solution.py:822
  261.5 31.5 %all_to_all.54.refs_5_ = bf16[32,320,128]{2,1,0:T(8,128)(2,1)} all-to-all(bf16[32,320,128]{2,1,0:T(8,128)(2,1)} %attend_back.2), channel_id=1, replica_groups=mesh['seq'=32,'batch'=4] {'seq'}, dimensions={0} | all-to-all | bytes 5242880 | tf_op jit(solution)/shard_map/all_to_all | solution.py:534
  293.0 21.3 %return.1 = (bf16[32,64,128]{2,1,0:T(8,128)(2,1)}, bf16[256,2304]{1,0:T(8,128)(2,1)}, f32[256,768]{1,0:T(8,128)}, bf16[768,3072]{1,0:T(8,128)(2,1)}, bf16[3072,7...) custom-call(s32[6]{0:T(128)} %stack.31.info.refs_0_, s32[1,256]{1,0:T(1,128)} %refs_1_.5, f32[768]{0:T(1024)} %refs_1_.6, ...), custom_call_target="tpu_custom_call" | custom-call | flops 10000000000 | bytes 16777216 | tf_op jit(solution)/shard_map/return/pallas_call | solution.py:400
  315.4 16.8 %all_to_all.55.grad_out_far = bf16[32,64,128]{2,1,0:T(8,128)(2,1)} all-to-all(bf16[32,64,128]{2,1,0:T(8,128)(2,1)S(1)} %copy-done.1), channel_id=1, replica_groups=mesh['seq'=32,'batch'=4] {'seq'}, dimensions={0} | all-to-all | bytes 1048576 | tf_op jit(solution)/shard_map/all_to_all | solution.py:534
  332.2 52.6 %attend_back.3 = bf16[32,320,128]{2,1,0:T(8,128)(2,1)} custom-call(s32[6]{0:T(128)} %stack.31.info.refs_0_, bf16[32,336,128]{2,1,0:T(8,128)(2,1)} %all-to-all-done.recv_far, bf16[64,8192]{1,0:T(8,128)(2,1)} %get-tuple-element.72.kv_t_far, bf16[128,4096]{1,0:T(8,128)(2,1)} %get-tuple-element.73.q_t_far, f32[64,4096]{1,0:T(8,128)} %get-tuple-element.74.out_f_far, ...), custom_call_target="tpu_custom_call" | custom-call | flops 18227200000 | bytes 8388608 | tf_op jit(solution)/shard_map/attend_back/pallas_call | solution.py:822
  384.8 4.8 all-to-all-start.7
  389.7 7.6 %grad_qkv_two.1.refs_4_ = f32[18,768,128]{2,1,0:T(8,128)} custom-call(s32[6]{0:T(128)} %stack.31.info.refs_0_, bf16[256,768]{1,0:T(8,128)(2,1)} %get-tuple-element.99.refs_1_, bf16[256,2304]{1,0:T(8,128)(2,1)} %get-tuple-element.100.refs_2_), custom_call_target="tpu_custom_call" | custom-call | flops 900000000 | bytes 16777216 | tf_op jit(solution)/shard_map/grad_qkv_two/pallas_call | solution.py:400
  397.2 21.0 %all-to-all-done.7.refs_2_ = bf16[32,320,128]{2,1,0:T(8,128)(2,1)} async-done(((bf16[32,320,128]{2,1,0:T(8,128)(2,1)}), bf16[32,320,128]{2,1,0:T(8,128)(2,1)}, u32[]{:S(2)}, u32[]{:S(2)}) %all-to-all-start.7) | async-done | bytes 2621472 | tf_op jit(solution)/shard_map/all_to_all | solution.py:534
  418.2 6.9 %leave.1 = (f32[256,768]{1,0:T(8,128)}, bf16[256,2304]{1,0:T(8,128)(2,1)}, f32[1,768]{1,0:T(1,128)}) custom-call(s32[6]{0:T(128)} %stack.31.info.refs_0_, f32[768]{0:T(1024)} %refs_1_.6, bf16[32,320,128]{2,1,0:T(8,128)(2,1)} %all-to-all-done.7.refs_2_, bf16[768,2304]{1,0:T(8,128)(2,1)} %refs_3_.6, bf16[256,768]{1,0:T(8,128)(2,1)} %bitcast.26, ...), custom_call_target="tpu_custom_call" | custom-call | flops 1000000000 | bytes 16777216 | tf_op jit(solution)/shard_map/leave/pallas_call | solution.py:400
  426.5 9.3 %grad_qkv.1 = (bf16[7168,128]{1,0:T(8,128)(2,1)}, bf16[7168,128]{1,0:T(8,128)(2,1)}) custom-call(s32[6]{0:T(128)} %stack.31.info.refs_0_, f32[16,128]{1,0:T(8,128)} %pad.9.refs_1_, bf16[256,768]{1,0:T(8,128)(2,1)} %get-tuple-element.97.refs_2_, bf16[256,2304]{1,0:T(8,128)(2,1)} %get-tuple-element.98.refs_3_, f32[18,768,128]{2,1,0:T(8,128)} %grad_qkv_two.1.refs_4_), custom_call_target="tpu_custom_call" | custom-call | flops 900000000 | bytes 16777216 | tf_op jit(solution)/shard_map/grad_qkv/pallas_call | solution.py:400
  435.8 75.5 %all-reduce.5.cloned.1.call-done = (bf16[768,3072]{1,0:T(8,128)(2,1)}, bf16[3072,768]{1,0:T(8,128)(2,1)}, bf16[784,768]{1,0:T(8,128)(2,1)}) async-done(((bf16[768,3072]{1,0:T(8,128)(2,1)}, bf16[3072,768]{1,0:T(8,128)(2,1)}, bf16[784,768]{1,0:T(8,128)(2,1)}), (bf16[768,3072]{1,0:T(8,128)(2,1)}, bf16[3072,768]{1,0:T(8,128)(2,1)}, bf16[784,768]{1,0:T(8,128)(2,1)})) %all-reduce.5.cloned.1.call-update) | async-done | bytes 10641424 | tf_op jit(solution)/shard_map/psum | solution.py:929
  512.0 3.6 collective-permute-done
  515.7 3.2 add_convert_fusion
  518.9 7.7 %all-to-all-start.8 = ((bf16[64,112,128]{2,1,0:T(8,128)(2,1)}), bf16[64,112,128]{2,1,0:T(8,128)(2,1)S(1)}, u32[]{:S(2)}, u32[]{:S(2)}) async-start(bf16[64,112,128]{2,1,0:T(8,128)(2,1)} %bitcast.23), calls=%async_computation.8 | async-start | bytes 3670016 | tf_op jit(solution)/shard_map/all_to_all | solution.py:547
  526.5 7.4 %convert_element_type.37 = f32[768,3072]{1,0:T(8,128)} convert(bf16[768,3072]{1,0:T(8,128)(2,1)} %get-tuple-element.108) | non-fusion elementwise | flops 2359296 | bytes 14155776 | tf_op jit(solution)/shard_map/convert_element_type | solution.py:965
  533.9 6.9 %convert_element_type.38 = f32[3072,768]{1,0:T(8,128)} convert(bf16[3072,768]{1,0:T(8,128)(2,1)} %get-tuple-element.109) | non-fusion elementwise | flops 2359296 | bytes 14155776 | tf_op jit(solution)/shard_map/convert_element_type | solution.py:965
  542.4 10.5 %all-to-all-done.8 = bf16[64,112,128]{2,1,0:T(8,128)(2,1)S(1)} async-done(((bf16[64,112,128]{2,1,0:T(8,128)(2,1)}), bf16[64,112,128]{2,1,0:T(8,128)(2,1)S(1)}, u32[]{:S(2)}, u32[]{:S(2)}) %all-to-all-start.8) | async-done | bytes 1835040 | tf_op jit(solution)/shard_map/all_to_all | solution.py:547
  553.4 30.1 %all_to_all.56 = bf16[64,112,128]{2,1,0:T(8,128)(2,1)S(1)} all-to-all(bf16[64,112,128]{2,1,0:T(8,128)(2,1)S(1)} %broadcast_in_dim.14), channel_id=1, replica_groups={{0,2,4,6,8,10,12,14,16,18,20,22,24,26,28,30,32,34,36,38,40,42,44,46,48,..., dimensions={0} | all-to-all | bytes 3670016 | tf_op jit(solution)/shard_map/all_to_all | solution.py:547
  583.5 2.4 collective-permute-start.1
  587.7 1.6 collective-permute-done.1.other
  589.3 3.7 widen.1
  (28 shorter events, 9.5 us)
Async XLA Ops:
  13.3 9.6 %copy-start.4 = (s32[1,256]{1,0:T(1,128)S(1)}, s32[1,256]{1,0:T(1,128)}, u32[]{:S(2)}) copy-start(s32[1,256]{1,0:T(1,128)} %refs_0_.1) | copy-start | bytes 3076
  13.4 10.2 %copy-start.3 = (s32[1,256]{1,0:T(1,128)S(1)}, s32[1,256]{1,0:T(1,128)}, u32[]{:S(2)}) copy-start(s32[1,256]{1,0:T(1,128)} %refs_1_.5) | copy-start | bytes 3076
  13.4 10.2 %copy-start.5 = (s32[1,256]{1,0:T(1,128)S(1)}, s32[1,256]{1,0:T(1,128)}, u32[]{:S(2)}) copy-start(s32[1,256]{1,0:T(1,128)} %refs_2_.2) | copy-start | bytes 3076
  13.4 14.7 %copy-start.2 = (f32[5,768]{1,0:T(8,128)S(1)}, f32[5,768]{1,0:T(8,128)}, u32[]{:S(2)}) copy-start(f32[5,768]{1,0:T(8,128)} %param.22) | copy-start | bytes 46084
  13.4 43.4 %all-to-all-start = ((bf16[32,336,128]{2,1,0:T(8,128)(2,1)}), bf16[32,336,128]{2,1,0:T(8,128)(2,1)}, u32[]{:S(2)}, u32[]{:S(2)}) async-start(bf16[32,336,128]{2,1,0:T(8,128)(2,1)} %get-tuple-element.62), calls=%async_computation | async-start | bytes 5505024 | tf_op jit(solution)/shard_map/all_to_all | solution.py:534
  22.9 488.4 %all-reduce.5.cloned.1.call-start = ((), (), s32[]{:S(2)}) async-start(), calls=%async_computation.10 | async-start | bytes 21282816 | tf_op jit(solution)/shard_map/psum | solution.py:929
  314.4 1.0 copy-start.1
  384.8 33.4 %all-to-all-start.7 = ((bf16[32,320,128]{2,1,0:T(8,128)(2,1)}), bf16[32,320,128]{2,1,0:T(8,128)(2,1)}, u32[]{:S(2)}, u32[]{:S(2)}) async-start(bf16[32,320,128]{2,1,0:T(8,128)(2,1)} %attend_back.3), calls=%async_computation.7 | async-start | bytes 5242880 | tf_op jit(solution)/shard_map/all_to_all | solution.py:534
  511.3 4.3 collective-permute-start
  518.9 34.0 %all-to-all-start.8 = ((bf16[64,112,128]{2,1,0:T(8,128)(2,1)}), bf16[64,112,128]{2,1,0:T(8,128)(2,1)S(1)}, u32[]{:S(2)}, u32[]{:S(2)}) async-start(bf16[64,112,128]{2,1,0:T(8,128)(2,1)} %bitcast.23), calls=%async_computation.8 | async-start | bytes 3670016 | tf_op jit(solution)/shard_map/all_to_all | solution.py:547
  533.9 6.9 %copy-start = (bf16[784,768]{1,0:T(8,128)(2,1)S(1)}, bf16[784,768]{1,0:T(8,128)(2,1)}, u32[]{:S(2)}) copy-start(bf16[784,768]{1,0:T(8,128)(2,1)} %get-tuple-element.110) | copy-start | bytes 3612676
  583.5 5.8 collective-permute-start.1
Sparse Core Ops, SparseCore 0:
  314.5 196.7 all-reduce.4

commit v6 on v5

--- a/solution.py
+++ b/solution.py
@@ -167,6 +167,7 @@
 def project(stream, gain, w_qkv, odd, third, slots, normed_out):
     normed = (standardise(stream)[0] * gain).astype(BF16)
     normed_out[...] = normed
+    normed_out.flush()
     low_lanes = lax.broadcasted_iota(jnp.int32, (ROWS, 128), 1) < 64
     for pair in range(HEADS // 2):
         at = 128 * pair
@@ -255,6 +256,8 @@
             done.flush()
     low = grad_mid.astype(BF16)
     dy_out[...] = low
+    if isinstance(dy_out, Kept):
+        dy_out.flush()
     scatter_heads(times_transposed(low, out[...]).T.astype(BF16), odd, slots)
 
 

time: 608 us -> 607 us (level)
  no operation moved by 1% of the time
where the time goes in v6:
time: 607 us; the launch traced here: 600 us
  Pallas kernels  230 us (38%)
  blocking collectives  161 us (27%)
  waiting for transfers between devices  139 us (23%)
  starting transfers between devices  25.1 us (4%)
  other arithmetic  20.6 us (3%)
  between operations  18.7 us (3%)
    all_to_all x6, blocking collectives, exchange(): return lax.all_to_all(slots, 'seq', 0, 0)  131 us
    pallas_call x2, Pallas kernels, attend_back(): pl.pallas_call(functools.partial(attend_back_kernel, devs=devs), out_shap...  105 us
    pallas_call x7, Pallas kernels, in_vmem(): pl.pallas_call(body, out_shape=tuple(outs), in_specs=[pl.BlockSpec(memory...  75.4 us
    psum x1, waiting for transfers between devices, on_device(): early = lax.psum(tuple(early), ('seq', 'batch'))  75.3 us
    all_to_all x2, waiting for transfers between devices, exchange(): return lax.all_to_all(slots, 'seq', 0, 0)  48.4 us
    pallas_call x2, Pallas kernels, attend(): pl.pallas_call(functools.partial(attend_kernel, devs=devs), out_shape=(ja...  45.8 us
    all_to_all x1, blocking collectives, across_chips(): lax.all_to_all(slots, ('seq', 'batch'), 0, 0, axis_index_groups=groups)  30.1 us
    all_to_all x2, starting transfers between devices, exchange(): return lax.all_to_all(slots, 'seq', 0, 0)  14.3 us
  transfers between devices with their start and end apart: 6, of which 6 were waited for; matrix products, arithmetic and copies ran while one was open for 4% of the time, Pallas kernels for 13%

profile of v6, /device:TPU:1, one launch (start us, length us, event | category | flops | bytes accessed | tf_op | source)
XLA Modules:
  0.0 599.9 jit_solution(3484107002909960697)
XLA Ops:
  7.2 6.0 %enter.1 = (bf16[32,336,128]{2,1,0:T(8,128)(2,1)}, bf16[256,768]{1,0:T(8,128)(2,1)}) custom-call(s32[1,256]{1,0:T(1,128)} %refs_0_.1, s32[1,256]{1,0:T(1,128)} %refs_1_.5, s32[1,256]{1,0:T(1,128)} %refs_2_.2, f32[768]{0:T(1024)} %refs_1_.6, bf16[256,768]{1,0:T(8,128)(2,1)} %bitcast.24, bf16[768,2304]{1,0:T(8,128)(2,1)} %refs_3_.6), custom_call_target="tpu_custom_call" | custom-call | flops 1000000000 | bytes 16777216 | tf_op jit(solution)/shard_map/enter/pallas_call | solution.py:403
  13.3 9.5 %all-to-all-start = ((bf16[32,336,128]{2,1,0:T(8,128)(2,1)}), bf16[32,336,128]{2,1,0:T(8,128)(2,1)}, u32[]{:S(2)}, u32[]{:S(2)}) async-start(bf16[32,336,128]{2,1,0:T(8,128)(2,1)} %get-tuple-element.62), calls=%async_computation | async-start | bytes 5505024 | tf_op jit(solution)/shard_map/all_to_all | solution.py:537
  29.3 27.4 %all-to-all-done.recv_far = bf16[32,336,128]{2,1,0:T(8,128)(2,1)} async-done(((bf16[32,336,128]{2,1,0:T(8,128)(2,1)}), bf16[32,336,128]{2,1,0:T(8,128)(2,1)}, u32[]{:S(2)}, u32[]{:S(2)}) %all-to-all-start) | async-done | bytes 2752544 | tf_op jit(solution)/shard_map/all_to_all | solution.py:537
  56.7 22.9 %attend.2 = (bf16[32,64,128]{2,1,0:T(8,128)(2,1)}, f32[64,4096]{1,0:T(8,128)}, f32[1,4096]{1,0:T(1,128)}, bf16[64,8192]{1,0:T(8,128)(2,1)}, bf16[128,4096]{1,0:T(8,128)(2,1)}) custom-call(s32[6]{0:T(128)} %stack.31.info.refs_0_, bf16[32,336,128]{2,1,0:T(8,128)(2,1)} %all-to-all-done.recv_far), custom_call_target="tpu_custom_call" | custom-call | flops 18227200000 | bytes 8388608 | tf_op jit(solution)/shard_map/attend/pallas_call | solution.py:707
  79.6 17.9 %all_to_all.50.refs_5_ = bf16[32,64,128]{2,1,0:T(8,128)(2,1)} all-to-all(bf16[32,64,128]{2,1,0:T(8,128)(2,1)} %get-tuple-element.67), channel_id=1, replica_groups=mesh['seq'=32,'batch'=4] {'seq'}, dimensions={0} | all-to-all | bytes 1048576 | tf_op jit(solution)/shard_map/all_to_all | solution.py:537
  97.5 10.7 %turn.1 = (bf16[32,336,128]{2,1,0:T(8,128)(2,1)}, bf16[256,768]{1,0:T(8,128)(2,1)}, f32[256,768]{1,0:T(8,128)}, bf16[256,768]{1,0:T(8,128)(2,1)}, f32[256,768]{1...) custom-call(s32[6]{0:T(128)} %stack.31.info.refs_0_, s32[1,256]{1,0:T(1,128)} %refs_1_.5, ...), custom_call_target="tpu_custom_call" | custom-call | flops 3600000000 | bytes 16777216 | tf_op jit(solution)/shard_map/turn/pallas_call | solution.py:403
  108.3 36.6 %all_to_all.51.recv_far = bf16[32,336,128]{2,1,0:T(8,128)(2,1)} all-to-all(bf16[32,336,128]{2,1,0:T(8,128)(2,1)} %get-tuple-element.68), channel_id=1, replica_groups=mesh['seq'=32,'batch'=4] {'seq'}, dimensions={0} | all-to-all | bytes 5505024 | tf_op jit(solution)/shard_map/all_to_all | solution.py:537
  144.8 22.9 %attend.3 = (bf16[32,64,128]{2,1,0:T(8,128)(2,1)}, f32[64,4096]{1,0:T(8,128)}, f32[1,4096]{1,0:T(1,128)}, bf16[64,8192]{1,0:T(8,128)(2,1)}, bf16[128,4096]{1,0:T(8,128)(2,1)}) custom-call(s32[6]{0:T(128)} %stack.31.info.refs_0_, bf16[32,336,128]{2,1,0:T(8,128)(2,1)} %all_to_all.51.recv_far), custom_call_target="tpu_custom_call" | custom-call | flops 18227200000 | bytes 8388608 | tf_op jit(solution)/shard_map/attend/pallas_call | solution.py:707
  167.7 14.1 %all_to_all.52.refs_2_ = bf16[32,64,128]{2,1,0:T(8,128)(2,1)} all-to-all(bf16[32,64,128]{2,1,0:T(8,128)(2,1)} %get-tuple-element.69), channel_id=1, replica_groups=mesh['seq'=32,'batch'=4] {'seq'}, dimensions={0} | all-to-all | bytes 1048576 | tf_op jit(solution)/shard_map/all_to_all | solution.py:537
  181.9 13.5 %crest.1 = (bf16[32,64,128]{2,1,0:T(8,128)(2,1)}, bf16[256,768]{1,0:T(8,128)(2,1)}, bf16[256,768]{1,0:T(8,128)(2,1)}, bf16[256,768]{1,0:T(8,128)(2,1)}, bf16[256...) custom-call(s32[6]{0:T(128)} %stack.31.info.refs_0_, ...), custom_call_target="tpu_custom_call" | custom-call | flops 5000000000 | bytes 16777216 | tf_op jit(solution)/shard_map/crest/pallas_call | solution.py:403
  195.3 13.6 %all_to_all.53.grad_out_far = bf16[32,64,128]{2,1,0:T(8,128)(2,1)} all-to-all(bf16[32,64,128]{2,1,0:T(8,128)(2,1)} %get-tuple-element.81), channel_id=1, replica_groups=mesh['seq'=32,'batch'=4] {'seq'}, dimensions={0} | all-to-all | bytes 1048576 | tf_op jit(solution)/shard_map/all_to_all | solution.py:537
  209.0 52.2 %attend_back.2 = bf16[32,320,128]{2,1,0:T(8,128)(2,1)} custom-call(s32[6]{0:T(128)} %stack.31.info.refs_0_, bf16[32,336,128]{2,1,0:T(8,128)(2,1)} %all_to_all.51.recv_far, bf16[64,8192]{1,0:T(8,128)(2,1)} %get-tuple-element.77.kv_t_far, bf16[128,4096]{1,0:T(8,128)(2,1)} %get-tuple-element.78.q_t_far, f32[64,4096]{1,0:T(8,128)} %get-tuple-element.79.out_f_far, ...), custom_call_target="tpu_custom_call" | custom-call | flops 18227200000 | bytes 8388608 | tf_op jit(solution)/shard_map/attend_back/pallas_call | solution.py:825
  261.1 31.6 %all_to_all.54.refs_5_ = bf16[32,320,128]{2,1,0:T(8,128)(2,1)} all-to-all(bf16[32,320,128]{2,1,0:T(8,128)(2,1)} %attend_back.2), channel_id=1, replica_groups=mesh['seq'=32,'batch'=4] {'seq'}, dimensions={0} | all-to-all | bytes 5242880 | tf_op jit(solution)/shard_map/all_to_all | solution.py:537
  292.7 21.3 %return.1 = (bf16[32,64,128]{2,1,0:T(8,128)(2,1)}, bf16[256,2304]{1,0:T(8,128)(2,1)}, f32[256,768]{1,0:T(8,128)}, bf16[768,3072]{1,0:T(8,128)(2,1)}, bf16[3072,7...) custom-call(s32[6]{0:T(128)} %stack.31.info.refs_0_, s32[1,256]{1,0:T(1,128)} %refs_1_.5, f32[768]{0:T(1024)} %refs_1_.6, ...), custom_call_target="tpu_custom_call" | custom-call | flops 10000000000 | bytes 16777216 | tf_op jit(solution)/shard_map/return/pallas_call | solution.py:403
  315.1 16.8 %all_to_all.55.grad_out_far = bf16[32,64,128]{2,1,0:T(8,128)(2,1)} all-to-all(bf16[32,64,128]{2,1,0:T(8,128)(2,1)S(1)} %copy-done.1), channel_id=1, replica_groups=mesh['seq'=32,'batch'=4] {'seq'}, dimensions={0} | all-to-all | bytes 1048576 | tf_op jit(solution)/shard_map/all_to_all | solution.py:537
  331.9 52.6 %attend_back.3 = bf16[32,320,128]{2,1,0:T(8,128)(2,1)} custom-call(s32[6]{0:T(128)} %stack.31.info.refs_0_, bf16[32,336,128]{2,1,0:T(8,128)(2,1)} %all-to-all-done.recv_far, bf16[64,8192]{1,0:T(8,128)(2,1)} %get-tuple-element.72.kv_t_far, bf16[128,4096]{1,0:T(8,128)(2,1)} %get-tuple-element.73.q_t_far, f32[64,4096]{1,0:T(8,128)} %get-tuple-element.74.out_f_far, ...), custom_call_target="tpu_custom_call" | custom-call | flops 18227200000 | bytes 8388608 | tf_op jit(solution)/shard_map/attend_back/pallas_call | solution.py:825
  384.5 4.8 all-to-all-start.7
  389.3 7.6 %grad_qkv_two.1.refs_4_ = f32[18,768,128]{2,1,0:T(8,128)} custom-call(s32[6]{0:T(128)} %stack.31.info.refs_0_, bf16[256,768]{1,0:T(8,128)(2,1)} %get-tuple-element.99.refs_1_, bf16[256,2304]{1,0:T(8,128)(2,1)} %get-tuple-element.100.refs_2_), custom_call_target="tpu_custom_call" | custom-call | flops 900000000 | bytes 16777216 | tf_op jit(solution)/shard_map/grad_qkv_two/pallas_call | solution.py:403
  396.9 21.1 %all-to-all-done.7.refs_2_ = bf16[32,320,128]{2,1,0:T(8,128)(2,1)} async-done(((bf16[32,320,128]{2,1,0:T(8,128)(2,1)}), bf16[32,320,128]{2,1,0:T(8,128)(2,1)}, u32[]{:S(2)}, u32[]{:S(2)}) %all-to-all-start.7) | async-done | bytes 2621472 | tf_op jit(solution)/shard_map/all_to_all | solution.py:537
  418.0 6.9 %leave.1 = (f32[256,768]{1,0:T(8,128)}, bf16[256,2304]{1,0:T(8,128)(2,1)}, f32[1,768]{1,0:T(1,128)}) custom-call(s32[6]{0:T(128)} %stack.31.info.refs_0_, f32[768]{0:T(1024)} %refs_1_.6, bf16[32,320,128]{2,1,0:T(8,128)(2,1)} %all-to-all-done.7.refs_2_, bf16[768,2304]{1,0:T(8,128)(2,1)} %refs_3_.6, bf16[256,768]{1,0:T(8,128)(2,1)} %bitcast.26, ...), custom_call_target="tpu_custom_call" | custom-call | flops 1000000000 | bytes 16777216 | tf_op jit(solution)/shard_map/leave/pallas_call | solution.py:403
  426.2 9.3 %grad_qkv.1 = (bf16[7168,128]{1,0:T(8,128)(2,1)}, bf16[7168,128]{1,0:T(8,128)(2,1)}) custom-call(s32[6]{0:T(128)} %stack.31.info.refs_0_, f32[16,128]{1,0:T(8,128)} %pad.9.refs_1_, bf16[256,768]{1,0:T(8,128)(2,1)} %get-tuple-element.97.refs_2_, bf16[256,2304]{1,0:T(8,128)(2,1)} %get-tuple-element.98.refs_3_, f32[18,768,128]{2,1,0:T(8,128)} %grad_qkv_two.1.refs_4_), custom_call_target="tpu_custom_call" | custom-call | flops 900000000 | bytes 16777216 | tf_op jit(solution)/shard_map/grad_qkv/pallas_call | solution.py:403
  435.6 75.3 %all-reduce.5.cloned.1.call-done = (bf16[768,3072]{1,0:T(8,128)(2,1)}, bf16[3072,768]{1,0:T(8,128)(2,1)}, bf16[784,768]{1,0:T(8,128)(2,1)}) async-done(((bf16[768,3072]{1,0:T(8,128)(2,1)}, bf16[3072,768]{1,0:T(8,128)(2,1)}, bf16[784,768]{1,0:T(8,128)(2,1)}), (bf16[768,3072]{1,0:T(8,128)(2,1)}, bf16[3072,768]{1,0:T(8,128)(2,1)}, bf16[784,768]{1,0:T(8,128)(2,1)})) %all-reduce.5.cloned.1.call-update) | async-done | bytes 10641424 | tf_op jit(solution)/shard_map/psum | solution.py:932
  511.6 3.6 collective-permute-done
  515.2 3.2 add_convert_fusion
  518.4 7.7 %all-to-all-start.8 = ((bf16[64,112,128]{2,1,0:T(8,128)(2,1)}), bf16[64,112,128]{2,1,0:T(8,128)(2,1)S(1)}, u32[]{:S(2)}, u32[]{:S(2)}) async-start(bf16[64,112,128]{2,1,0:T(8,128)(2,1)} %bitcast.23), calls=%async_computation.8 | async-start | bytes 3670016 | tf_op jit(solution)/shard_map/all_to_all | solution.py:550
  526.1 7.4 %convert_element_type.37 = f32[768,3072]{1,0:T(8,128)} convert(bf16[768,3072]{1,0:T(8,128)(2,1)} %get-tuple-element.108) | non-fusion elementwise | flops 2359296 | bytes 14155776 | tf_op jit(solution)/shard_map/convert_element_type | solution.py:968
  533.5 6.9 %convert_element_type.38 = f32[3072,768]{1,0:T(8,128)} convert(bf16[3072,768]{1,0:T(8,128)(2,1)} %get-tuple-element.109) | non-fusion elementwise | flops 2359296 | bytes 14155776 | tf_op jit(solution)/shard_map/convert_element_type | solution.py:968
  542.0 10.5 %all-to-all-done.8 = bf16[64,112,128]{2,1,0:T(8,128)(2,1)S(1)} async-done(((bf16[64,112,128]{2,1,0:T(8,128)(2,1)}), bf16[64,112,128]{2,1,0:T(8,128)(2,1)S(1)}, u32[]{:S(2)}, u32[]{:S(2)}) %all-to-all-start.8) | async-done | bytes 1835040 | tf_op jit(solution)/shard_map/all_to_all | solution.py:550
  553.0 30.1 %all_to_all.56 = bf16[64,112,128]{2,1,0:T(8,128)(2,1)S(1)} all-to-all(bf16[64,112,128]{2,1,0:T(8,128)(2,1)S(1)} %broadcast_in_dim.14), channel_id=1, replica_groups={{0,2,4,6,8,10,12,14,16,18,20,22,24,26,28,30,32,34,36,38,40,42,44,46,48,..., dimensions={0} | all-to-all | bytes 3670016 | tf_op jit(solution)/shard_map/all_to_all | solution.py:550
  583.1 2.4 collective-permute-start.1
  587.3 1.6 collective-permute-done.1.other
  588.9 3.7 widen.1
  (28 shorter events, 9.5 us)
Async XLA Ops:
  13.2 9.6 %copy-start.4 = (s32[1,256]{1,0:T(1,128)S(1)}, s32[1,256]{1,0:T(1,128)}, u32[]{:S(2)}) copy-start(s32[1,256]{1,0:T(1,128)} %refs_0_.1) | copy-start | bytes 3076
  13.2 10.2 %copy-start.3 = (s32[1,256]{1,0:T(1,128)S(1)}, s32[1,256]{1,0:T(1,128)}, u32[]{:S(2)}) copy-start(s32[1,256]{1,0:T(1,128)} %refs_1_.5) | copy-start | bytes 3076
  13.2 10.2 %copy-start.5 = (s32[1,256]{1,0:T(1,128)S(1)}, s32[1,256]{1,0:T(1,128)}, u32[]{:S(2)}) copy-start(s32[1,256]{1,0:T(1,128)} %refs_2_.2) | copy-start | bytes 3076
  13.2 14.7 %copy-start.2 = (f32[5,768]{1,0:T(8,128)S(1)}, f32[5,768]{1,0:T(8,128)}, u32[]{:S(2)}) copy-start(f32[5,768]{1,0:T(8,128)} %param.22) | copy-start | bytes 46084
  13.3 43.4 %all-to-all-start = ((bf16[32,336,128]{2,1,0:T(8,128)(2,1)}), bf16[32,336,128]{2,1,0:T(8,128)(2,1)}, u32[]{:S(2)}, u32[]{:S(2)}) async-start(bf16[32,336,128]{2,1,0:T(8,128)(2,1)} %get-tuple-element.62), calls=%async_computation | async-start | bytes 5505024 | tf_op jit(solution)/shard_map/all_to_all | solution.py:537
  22.7 488.1 %all-reduce.5.cloned.1.call-start = ((), (), s32[]{:S(2)}) async-start(), calls=%async_computation.10 | async-start | bytes 21282816 | tf_op jit(solution)/shard_map/psum | solution.py:932
  314.0 1.0 copy-start.1
  384.5 33.5 %all-to-all-start.7 = ((bf16[32,320,128]{2,1,0:T(8,128)(2,1)}), bf16[32,320,128]{2,1,0:T(8,128)(2,1)}, u32[]{:S(2)}, u32[]{:S(2)}) async-start(bf16[32,320,128]{2,1,0:T(8,128)(2,1)} %attend_back.3), calls=%async_computation.7 | async-start | bytes 5242880 | tf_op jit(solution)/shard_map/all_to_all | solution.py:537
  510.9 4.3 collective-permute-start
  518.4 34.0 %all-to-all-start.8 = ((bf16[64,112,128]{2,1,0:T(8,128)(2,1)}), bf16[64,112,128]{2,1,0:T(8,128)(2,1)S(1)}, u32[]{:S(2)}, u32[]{:S(2)}) async-start(bf16[64,112,128]{2,1,0:T(8,128)(2,1)} %bitcast.23), calls=%async_computation.8 | async-start | bytes 3670016 | tf_op jit(solution)/shard_map/all_to_all | solution.py:550
  533.5 6.9 %copy-start = (bf16[784,768]{1,0:T(8,128)(2,1)S(1)}, bf16[784,768]{1,0:T(8,128)(2,1)}, u32[]{:S(2)}) copy-start(bf16[784,768]{1,0:T(8,128)(2,1)} %get-tuple-element.110) | copy-start | bytes 3612676
  583.1 5.8 collective-permute-start.1
Sparse Core Ops, SparseCore 0:
  314.2 196.6 all-reduce.4
